TPU v7x, 512 devices: a whole 4x8x8 slice. The times are simulated.
512 devices in a mesh: basis: 32 (over y, z_hi, core), ex: 16 (over z_lo, x).
Axes of the slice: x: 4, y: 8, z: 8 (z_hi: 2, z_lo: 4; z = z_hi * 4 + z_lo), core: 2. Of those that a mesh axis runs over, the one named last changes fastest.
Arguments:
- grad_out: bfloat16 [768, 13824], P('ex', 'basis'), may hold values from -6 to 6
- acts: bfloat16 [768, 5120], P('basis', 'ex'), may hold values from -6 to 6
- basis_out: bfloat16 [13824, 13824], P('basis', 'ex'), may hold values from -0.0546875 to 0.0546875
- basis_in: bfloat16 [5120, 5120], P('ex', 'basis'), may hold values from -0.078125 to 0.078125
- eigvals: float32 [13824, 5120], P('ex', 'basis'), may hold values from 0.1 to 10
- counts: int32 [48], replicated, may hold values from 1 to 16, as said below
Outputs:
- scores: float32 [16, 32], replicated
Inputs may be any that keep to these rules, and one draw needn't show every extreme that they name: `counts`: every draw holds some example with exactly 16 tokens in use.
All inputs are finite; a program needn't handle non-finite values.
Results may differ from a plain program's by a relative error of at most 0.0055.
Values may be sent and summed in bfloat16 or wider, within the bound.
No kernel may reach another device: no remote copies, remote signals or barrier semaphores. Data moves between devices by JAX's collectives and lax.ppermute only.
A program may use at most 64 MiB of HBM per device.

v0:
```python
import jax
import jax.numpy as jnp
from jax import lax
from jax.sharding import PartitionSpec as P

D = 5120
FF = 13824
NQ = 16
NT = 32
TOKX = 16
NTOK = 768


def body(grad_out, acts, basis_out, basis_in, eigvals, counts):
    total = NTOK
    partial_grad = jnp.dot(
        lax.all_gather(grad_out, "ex", axis=0, tiled=True),
        basis_out,
        preferred_element_type=jnp.float32,
    )
    partial_act = jnp.dot(
        lax.all_gather(acts, "basis", axis=0, tiled=True),
        basis_in,
        preferred_element_type=jnp.float32,
    )
    slots = jnp.arange(total, dtype=jnp.int32)
    mask = (slots % TOKX < jnp.repeat(counts, TOKX)).astype(jnp.float32)
    summed_grad = lax.psum(partial_grad, "basis")
    rot_grad = (summed_grad * mask[:, None]).astype(jnp.bfloat16)
    rot_act = lax.psum(partial_act, "ex").astype(jnp.bfloat16)
    cols_grad = rot_grad.shape[1]
    cols_act = rot_act.shape[1]
    query_grad = rot_grad[: NQ * TOKX].reshape(NQ, TOKX, cols_grad)
    query_act = rot_act[: NQ * TOKX].reshape(NQ, TOKX, cols_act)
    train_grad = rot_grad[NQ * TOKX :]
    train_act = rot_act[NQ * TOKX :]

    def one_query(pair):
        grad_q, act_q = pair
        outer = lax.dot_general(
            grad_q, act_q, (((0,), (0,)), ((), ())), preferred_element_type=jnp.float32
        )
        precond = (outer / eigvals).astype(jnp.bfloat16)
        projected = lax.dot_general(
            train_act, precond, (((1,), (1,)), ((), ())), preferred_element_type=jnp.float32
        )
        return jnp.sum((projected * train_grad).reshape(NT, TOKX * cols_grad), axis=1)

    raw = lax.map(one_query, (query_grad, query_act))
    scaled = raw / (TOKX * jnp.sqrt(jnp.float32(FF) * jnp.float32(D)))
    return lax.psum(scaled, ("basis", "ex"))


def solution(mesh):
    return jax.shard_map(
        body,
        mesh=mesh,
        in_specs=(
            P("ex", "basis"),
            P("basis", "ex"),
            P("basis", "ex"),
            P("ex", "basis"),
            P("ex", "basis"),
            P(),
        ),
        out_specs=P(),
        check_vma=False,
    )
```

profile of v0, /device:TPU:1, one launch (start us, length us, event | category | flops | bytes accessed | tf_op | source)
XLA Modules:
  0.0 538.2 jit_solution(5184239312704179613)
XLA Ops:
  6.5 43.3 %all_gather.6 = bf16[768,432]{1,0:T(8,128)(2,1)S(1)} all-gather(bf16[48,432]{1,0:T(8,128)(2,1)} %param.8), channel_id=1, replica_groups=mesh['basis'=32,'ex'=16] {'ex'}, dimensions={0}, use_global_device_ids=true | all-gather | bytes 705024 | tf_op jit(solution)/shard_map/all_gather | solution.py:17
  49.8 2.4 fusion.17
  52.3 65.9 %all_gather.7 = bf16[768,320]{1,0:T(8,128)(2,1)S(1)} all-gather(bf16[24,320]{1,0:T(8,128)(2,1)S(1)} %copy-done.2), channel_id=1, replica_groups=mesh['basis'=32,'ex'=16] {'basis'}, dimensions={0}, use_global_device_ids=true | all-gather | bytes 506880 | tf_op jit(solution)/shard_map/all_gather | solution.py:22
  118.6 75.2 %all-reduce.4 = bf16[768,160]{0,1:T(8,128)(2,1)S(1)} all-reduce(f32[768,160]{0,1:T(8,128)S(1)} %fusion.18), channel_id=1, replica_groups=mesh['basis'=32,'ex'=16] {'ex'}, use_global_device_ids=true, to_apply=%region_1.2 | all-reduce | flops 122880 | bytes 737280 | tf_op jit(solution)/shard_map/psum | solution.py:30
  194.3 218.3 %all-reduce.3.cloned.1.call-done = f32[768,864]{0,1:T(8,128)} async-done(((f32[768,864]{0,1:T(8,128)}), f32[768,864]{0,1:T(8,128)}) %all-reduce.3.cloned.1.call-update) | async-done | bytes 2654224 | tf_op jit(solution)/shard_map/psum | solution.py:28
  412.6 1.9 multiply_convert_fusion
  414.9 0.7 copy-done.4
  415.6 15.2 %while.10 = (s32[]{:T(128)}, f32[16,32]{1,0:T(8,128)S(1)}, bf16[16,16,864]{2,1,0:T(8,128)(2,1)S(1)}, bf16[16,16,160]{2,1,0:T(8,128)(2,1)S(1)}, f32[864,160]{0,1:...) while((s32[]{:T(128)}, f32[16,32]{1,0:T(8,128)S(1)}, ...), condition=%wide.region_5.6_spmd, body=%wide.region_2.5_spmd.sunk | while | flops 147584992 | bytes 1766893 | solution.py:49
  416.6 0.7 fusion.31
  417.5 0.7 fusion.31
  418.5 0.7 fusion.31
  419.4 0.7 fusion.31
  420.4 0.7 fusion.31
  421.4 0.7 fusion.31
  422.3 0.7 fusion.31
  423.2 0.7 fusion.31
  424.2 0.7 fusion.31
  425.2 0.7 fusion.31
  426.1 0.7 fusion.31
  427.1 0.7 fusion.31
  428.0 0.7 fusion.31
  429.0 0.7 fusion.31
  429.9 0.7 fusion.31
  430.9 100.5 %psum.23 = f32[16,32]{1,0:T(8,128)} all-reduce(f32[16,32]{1,0:T(8,128)S(1)} %broadcast_multiply_fusion), channel_id=1, replica_groups=mesh['basis'=32,'ex'=16] {'basis','ex'}, use_global_device_ids=true, to_apply=%region_6.7 | all-reduce | flops 512 | bytes 4096 | tf_op jit(solution)/shard_map/psum | solution.py:51
  (73 shorter events, 5.5 us)
Async XLA Ops:
  6.5 43.3 %copy-start = (bf16[432,864]{1,0:T(8,128)(2,1)S(1)}, bf16[432,864]{1,0:T(8,128)(2,1)}, u32[]{:S(2)}) copy-start(bf16[432,864]{1,0:T(8,128)(2,1)} %param.10) | copy-start | bytes 2239492
  6.5 406.1 %all-reduce.3.cloned.1.call-start = ((), (), s32[]{:S(2)}) async-start(), calls=%async_computation | async-start | bytes 5308416 | tf_op jit(solution)/shard_map/psum | solution.py:28
  49.8 2.5 copy-start.2
  52.2 66.0 %copy-start.1 = (bf16[320,160]{0,1:T(8,128)(2,1)S(1)}, bf16[320,160]{0,1:T(8,128)(2,1)}, u32[]{:S(2)}) copy-start(bf16[320,160]{0,1:T(8,128)(2,1)} %param.11) | copy-start | bytes 307204
  52.2 141.6 %copy-start.3 = (s32[48]{0:T(128)S(1)}, s32[48]{0:T(128)}, u32[]{:S(2)}) copy-start(s32[48]{0:T(128)} %param.13) | copy-start | bytes 580
  414.6 1.1 copy-start.4
Sparse Core Ops, SparseCore 0:
  52.4 360.1 all-reduce.2
where the time goes:
time: 538 us
  blocking collectives  285 us (53%)
  waiting for transfers between devices  218 us (41%)
  matrix products  13.9 us (3%)
  between operations  13.5 us (3%)
    psum x1, waiting for transfers between devices, body(): summed_grad = lax.psum(partial_grad, 'basis')  218 us
    psum x1, blocking collectives, body(): return lax.psum(scaled, ('basis', 'ex'))  101 us
    psum x1, blocking collectives, body(): rot_act = lax.psum(partial_act, 'ex').astype(jnp.bfloat16)  75.2 us
    all_gather x1, blocking collectives, body(): lax.all_gather(acts, 'basis', axis=0, tiled=True)  65.9 us
    all_gather x1, blocking collectives, body(): lax.all_gather(grad_out, 'ex', axis=0, tiled=True)  43.3 us
    dot_general x16, matrix products, one_query(): lax.dot_general(train_act, precond, (((1,), (1,)), ((), ())), preferred_e...  11.2 us
  transfers between devices with their start and end apart: 1, of which 1 were waited for; matrix products, arithmetic and copies ran while one was open for 0% of the time, Pallas kernels for 0%

commit v1 on v0

v1 whole, which is shorter than its diff:
```python
import jax
import jax.numpy as jnp
from jax import lax
from jax.sharding import Mesh, PartitionSpec as P

D = 5120
FF = 13824
NQ = 16
NT = 32
TOKX = 16
NTOK = 768

SIZES = (8, 2, 2, 4, 4)
NAMES = ("y", "zh", "core", "zl", "x")
BASIS = ("y", "zh", "core")
EX = ("zl", "x")
SWAP = ((0, 1), (1, 0))
bf16 = jnp.bfloat16
f32 = jnp.float32


def spread(x, axes, n):
    return lax.all_to_all(
        jnp.broadcast_to(x[None], (n,) + x.shape), axes, 0, 0, tiled=True
    )


def swap(x, axis):
    return lax.ppermute(x, axis, SWAP)


def ordered(mine, other, second, axis):
    lo = jnp.where(second, other, mine)
    hi = jnp.where(second, mine, other)
    return lo, hi


def body(grad_out, acts, basis_out, basis_in, eigvals, counts):
    core = lax.axis_index("core")
    second = core == 1
    half = basis_out.shape[1] // 2

    grads = spread(grad_out, EX, 16).reshape(NTOK, -1)

    w_lo, w_hi = basis_out[:, :half], basis_out[:, half:]
    w_mine = jnp.where(second, w_hi, w_lo)
    w_other = swap(jnp.where(second, w_lo, w_hi), "core")
    eig_t = eigvals.T
    e_lo, e_hi = eig_t[:, :half], eig_t[:, half:]
    e_mine = jnp.where(second, e_hi, e_lo)
    e_other = swap(jnp.where(second, e_lo, e_hi), "core")
    eig = jnp.concatenate(ordered(e_mine, e_other, second, 0), axis=0)
    recip = 1.0 / eig

    b_other = swap(basis_in, "core")
    b_in = jnp.concatenate(ordered(basis_in, b_other, second, 1), axis=1)
    act = spread(acts, ("y", "zh"), 16).reshape(NTOK // 2, -1)
    part_act = jnp.dot(act, b_in, preferred_element_type=f32)
    part_act = lax.all_to_all(
        part_act.reshape(16, 24, -1), EX, 0, 0, tiled=True
    )
    act_piece = jnp.sum(part_act, axis=0).astype(bf16)
    act_half = spread(act_piece, EX, 16)
    act_other = swap(act_half, "core")
    rot_act = jnp.stack(
        ordered(
            act_half.reshape(16, 24, -1), act_other.reshape(16, 24, -1), second, 0
        ),
        axis=1,
    ).reshape(NTOK, -1)

    g_other = swap(grads, "core")
    partial = jnp.dot(grads, w_mine, preferred_element_type=f32) + jnp.dot(
        g_other, w_other, preferred_element_type=f32
    )
    rows = NTOK // 8
    pieces = lax.all_to_all(
        partial.astype(bf16).reshape(8, rows, -1), "y", 0, 0, tiled=True
    )
    piece = jnp.sum(pieces.astype(f32), axis=0)
    piece = piece + swap(piece, "zh")
    slots = lax.axis_index("y") * rows + jnp.arange(rows, dtype=jnp.int32)
    used = slots % TOKX < jnp.take(counts, slots // TOKX)
    piece = (piece * used.astype(f32)[:, None]).astype(bf16)
    rot_grad = spread(piece, "y", 8).reshape(NTOK, -1)

    cols_grad = rot_grad.shape[1]
    cols_act = rot_act.shape[1]
    query_grad = rot_grad[: NQ * TOKX].reshape(NQ, TOKX, cols_grad)
    query_act = rot_act[: NQ * TOKX].reshape(NQ, TOKX, cols_act)
    train_grad = rot_grad[NQ * TOKX :]
    train_act = rot_act[NQ * TOKX :]

    def one_query(pair):
        grad_q, act_q = pair
        outer = lax.dot_general(
            act_q, grad_q, (((0,), (0,)), ((), ())), preferred_element_type=f32
        )
        precond = (outer * recip).astype(bf16)
        projected = jnp.dot(train_act, precond, preferred_element_type=f32)
        return jnp.sum((projected * train_grad).reshape(NT, TOKX * cols_grad), axis=1)

    raw = lax.map(one_query, (query_grad, query_act))
    scaled = raw / (TOKX * jnp.sqrt(f32(FF) * f32(D)))
    flat = scaled.reshape(4, 128)
    flat = jnp.sum(spread(flat, ("core",) + EX, 32), axis=0)
    flat = jnp.sum(spread(flat, ("y", "zh"), 16), axis=0)
    return flat.reshape(NQ, NT)


def solution(mesh):
    fine = Mesh(mesh.devices.reshape(SIZES), NAMES)
    return jax.shard_map(
        body,
        mesh=fine,
        in_specs=(
            P(EX, BASIS),
            P(BASIS, EX),
            P(BASIS, EX),
            P(EX, BASIS),
            P(EX, BASIS),
            P(),
        ),
        out_specs=P(),
        check_vma=False,
    )
```

time: 538 us -> 204 us (0.38)
  blocking collectives: 285 us -> 76.4 us
  waiting for transfers between devices: 218 us -> 38.8 us
  starting transfers between devices: 0.01 us -> 62 us
  between operations: 13.5 us -> 0.32 us
  local copies, waits for them, and re-layouts: 3.32 us -> 9.96 us
    psum x1 -> x0, waiting for transfers between devices: 218 us -> none  [body(): summed_grad = lax.psum(partial_grad, 'basis')]
    psum x2 -> x0, blocking collectives: 176 us -> none  [the longest x1 101 us: body(): return lax.psum(scaled, ('basis', 'ex'))]
    all_gather x2 -> x0, blocking collectives: 109 us -> none  [the longest x1 65.9 us: body(): lax.all_gather(acts, 'basis', axis=0, tiled=True)]
    all_to_all x0 -> x3, blocking collectives: none -> 76.4 us  [spread(): lax.all_to_all(jnp.broadcast_to(x[None], (n,) + x.shape), axes, 0, 0, til...]
    all_to_all x0 -> x5, starting transfers between devices: none -> 34.5 us  [the longest x3 24.4 us: spread(): lax.all_to_all(jnp.broadcast_to(x[None], (n,) + x.shape), axes, 0, 0, til...]
    all_to_all x0 -> x5, waiting for transfers between devices: none -> 29.4 us  [the longest x1 18.6 us: body(): lax.all_to_all(partial.astype(bf16).reshape(8, rows, -1), 'y', 0, 0, tile...]
    ppermute x0 -> x6, starting transfers between devices: none -> 27.4 us  [swap(): return lax.ppermute(x, axis, SWAP)]
    ppermute x0 -> x6, waiting for transfers between devices: none -> 9.48 us  [swap(): return lax.ppermute(x, axis, SWAP)]
  transfers between devices with their start and end apart: 1 -> 11, of which waited for: 1 -> 8; matrix products, arithmetic and copies ran while one was open for 0% -> 3% of each run, Pallas kernels for 0% -> 0%
where the time goes in v1:
time: 204 us
  blocking collectives  76.4 us (37%)
  starting transfers between devices  62 us (30%)
  waiting for transfers between devices  38.8 us (19%)
  matrix products  12.7 us (6%)
  local copies, waits for them, and re-layouts  9.96 us (5%)
  other arithmetic  3.02 us (1%)
    all_to_all x3, blocking collectives, spread(): lax.all_to_all(jnp.broadcast_to(x[None], (n,) + x.shape), axes, 0, 0, til...  76.4 us
    ppermute x6, starting transfers between devices, swap(): return lax.ppermute(x, axis, SWAP)  27.4 us
    all_to_all x3, starting transfers between devices, spread(): lax.all_to_all(jnp.broadcast_to(x[None], (n,) + x.shape), axes, 0, 0, til...  24.4 us
    all_to_all x1, waiting for transfers between devices, body(): lax.all_to_all(partial.astype(bf16).reshape(8, rows, -1), 'y', 0, 0, tile...  18.6 us
    dot_general x16, matrix products, one_query(): projected = jnp.dot(train_act, precond, preferred_element_type=f32)  11 us
    ppermute x6, waiting for transfers between devices, swap(): return lax.ppermute(x, axis, SWAP)  9.48 us
    all_to_all x3, waiting for transfers between devices, spread(): lax.all_to_all(jnp.broadcast_to(x[None], (n,) + x.shape), axes, 0, 0, til...  7.27 us
    all_to_all x1, starting transfers between devices, body(): lax.all_to_all(partial.astype(bf16).reshape(8, rows, -1), 'y', 0, 0, tile...  5.43 us
  transfers between devices with their start and end apart: 11, of which 8 were waited for; matrix products, arithmetic and copies ran while one was open for 3% of the time, Pallas kernels for 0%

profile of v1, /device:TPU:1, one launch (start us, length us, event | category | flops | bytes accessed | tf_op | source)
XLA Modules:
  0.0 203.5 jit_solution(1207056817971391634)
XLA Ops:
  0.9 30.6 %all_to_all.40 = bf16[16,48,432]{2,1,0:T(8,128)(2,1)S(1)} all-to-all(bf16[16,48,432]{2,1,0:T(8,128)(2,1)S(1)} %broadcast_in_dim.29), channel_id=1, replica_groups=mesh['y'=8,'zh'=2,'core'=2,'zl'=4,'x'=4] {'zl','x'}, dimensions={0} | all-to-all | bytes 1327104 | tf_op jit(solution)/shard_map/all_to_all | solution.py:23
  32.2 12.7 %all-to-all-start = ((bf16[16,24,320]{2,1,0:T(8,128)(2,1)}), bf16[16,24,320]{2,1,0:T(8,128)(2,1)S(1)}, u32[]{:S(2)}, u32[]{:S(2)}) async-start(bf16[16,24,320]{2,1,0:T(8,128)(2,1)} %broadcast_in_dim.27), calls=%async_computation | async-start | bytes 589824 | tf_op jit(solution)/shard_map/all_to_all | solution.py:23
  44.9 4.5 %collective-permute-start = (bf16[320,160]{0,1:T(8,128)(2,1)S(1)}, bf16[320,160]{0,1:T(8,128)(2,1)S(1)}, u32[]{:S(2)}, u32[]{:S(2)}) collective-permute-start(bf16[320,160]{0,1:T(8,128)(2,1)S(1)} %copy-done.3), channel_id=1, source_target_pairs={{0,16},{16,0},{1,17},{17,1},{2,18},{18,2},{3,19},{19,3},{4,20},{20... | collective-permute-start | bytes 307208 | tf_op jit(solution)/shard_map/ppermute | solution.py:29
  50.6 2.3 %collective-permute-start.3 = (bf16[768,432]{0,1:T(8,128)(2,1)S(1)}, bf16[768,432]{0,1:T(8,128)(2,1)S(1)}, u32[]{:S(2)}, u32[]{:S(2)}) collective-permute-start(bf16[768,432]{0,1:T(8,128)(2,1)S(1)} %copy.29), channel_id=1, source_target_pairs={{0,16},{16,0},{1,17},{17,1},{2,18},{18,2},{3,19},{19,3},{4,20},{20... | collective-permute-start | bytes 1990664 | tf_op jit(solution)/shard_map/ppermute | solution.py:29
  52.9 6.3 %all-to-all-done = bf16[16,24,320]{2,1,0:T(8,128)(2,1)S(1)} async-done(((bf16[16,24,320]{2,1,0:T(8,128)(2,1)}), bf16[16,24,320]{2,1,0:T(8,128)(2,1)S(1)}, u32[]{:S(2)}, u32[]{:S(2)}) %all-to-all-start) | async-done | bytes 245792 | tf_op jit(solution)/shard_map/all_to_all | solution.py:23
  59.6 1.1 copy.27
  60.6 4.7 %all-to-all-start.1 = ((f32[16,24,320]{2,1,0:T(8,128)}), f32[16,24,320]{2,1,0:T(8,128)S(1)}, u32[]{:S(2)}, u32[]{:S(2)}) async-start(f32[16,24,320]{2,1,0:T(8,128)} %bitcast.6), calls=%async_computation.1 | async-start | bytes 1179648 | tf_op jit(solution)/shard_map/all_to_all | solution.py:59
  65.5 5.6 %collective-permute-start.2 = (bf16[432,432]{1,0:T(8,128)(2,1)S(1)}, bf16[432,432]{1,0:T(8,128)(2,1)S(1)}, u32[]{:S(2)}, u32[]{:S(2)}) collective-permute-start(bf16[432,432]{1,0:T(8,128)(2,1)S(1)} %broadcast_select_fusion), channel_id=1, source_target_pairs={{0,16},{16,0},{1,17},{17,1},{2,18},{18,2},{3,19},{19,3},{4,20},{20... | collective-permute-start | bytes 1119752 | tf_op jit(solution)/shard_map/ppermute | solution.py:29
  73.0 1.2 copy.30
  74.2 3.4 %all-to-all-done.1 = f32[16,24,320]{2,1,0:T(8,128)S(1)} async-done(((f32[16,24,320]{2,1,0:T(8,128)}), f32[16,24,320]{2,1,0:T(8,128)S(1)}, u32[]{:S(2)}, u32[]{:S(2)}) %all-to-all-start.1) | async-done | bytes 491552 | tf_op jit(solution)/shard_map/all_to_all | solution.py:59
  77.6 5.4 %all-to-all-start.4 = ((bf16[8,96,432]{2,1,0:T(8,128)(2,1)}), bf16[8,96,432]{2,1,0:T(8,128)(2,1)S(1)}, u32[]{:S(2)}, u32[]{:S(2)}) async-start(bf16[8,96,432]{2,1,0:T(8,128)(2,1)} %bitcast.14), calls=%async_computation.4 | async-start | bytes 1572864 | tf_op jit(solution)/shard_map/all_to_all | solution.py:77
  83.1 1.2 gather_fusion
  84.4 18.6 %all-to-all-done.4 = bf16[8,96,432]{2,1,0:T(8,128)(2,1)S(1)} async-done(((bf16[8,96,432]{2,1,0:T(8,128)(2,1)}), bf16[8,96,432]{2,1,0:T(8,128)(2,1)S(1)}, u32[]{:S(2)}, u32[]{:S(2)}) %all-to-all-start.4) | async-done | bytes 663584 | tf_op jit(solution)/shard_map/all_to_all | solution.py:77
  103.8 8.2 %all-to-all-start.2 = ((bf16[16,24,320]{2,1,0:T(8,128)(2,1)}), bf16[16,24,320]{2,1,0:T(8,128)(2,1)S(1)}, u32[]{:S(2)}, u32[]{:S(2)}) async-start(bf16[16,24,320]{2,1,0:T(8,128)(2,1)} %broadcast_in_dim.28), calls=%async_computation.2 | async-start | bytes 589824 | tf_op jit(solution)/shard_map/all_to_all | solution.py:23
  112.1 3.9 %collective-permute-start.4 = (f32[96,432]{1,0:T(8,128)S(1)}, f32[96,432]{1,0:T(8,128)S(1)}, u32[]{:S(2)}, u32[]{:S(2)}) collective-permute-start(f32[96,432]{1,0:T(8,128)S(1)} %convert_reduce_fusion), channel_id=1, source_target_pairs={{0,32},{32,0},{1,33},{33,1},{2,34},{34,2},{3,35},{35,3},{4,36},{36... | collective-permute-start | bytes 497672 | tf_op jit(solution)/shard_map/ppermute | solution.py:29
  116.0 6.7 %collective-permute-done.4 = f32[96,432]{1,0:T(8,128)S(1)} collective-permute-done((f32[96,432]{1,0:T(8,128)S(1)}, f32[96,432]{1,0:T(8,128)S(1)}, u32[]{:S(2)}, u32[]{:S(2)}) %collective-permute-start.4) | collective-permute-done | bytes 165920 | tf_op jit(solution)/shard_map/ppermute | solution.py:29
  123.8 3.5 %all-to-all-start.5 = ((bf16[8,96,432]{2,1,0:T(8,128)(2,1)}), bf16[8,96,432]{2,1,0:T(8,128)(2,1)S(1)}, u32[]{:S(2)}, u32[]{:S(2)}) async-start(bf16[8,96,432]{2,1,0:T(8,128)(2,1)} %broadcast_in_dim.56), calls=%async_computation.5 | async-start | bytes 1572864 | tf_op jit(solution)/shard_map/all_to_all | solution.py:23
  127.5 9.3 %collective-permute-start.5 = (f32[160,432]{1,0:T(8,128)S(1)}, f32[160,432]{1,0:T(8,128)S(1)}, u32[]{:S(2)}, u32[]{:S(2)}) collective-permute-start(f32[160,432]{1,0:T(8,128)S(1)} %slice_select_fusion.1), channel_id=1, source_target_pairs={{0,16},{16,0},{1,17},{17,1},{2,18},{18,2},{3,19},{19,3},{4,20},{20... | collective-permute-start | bytes 829448 | tf_op jit(solution)/shard_map/ppermute | solution.py:29
  136.8 1.9 collective-permute-start.1
  139.1 1.3 collective-permute-done.1
  140.6 1.0 all-to-all-done.5
  141.8 15.1 %while.10 = (s32[]{:T(128)}, f32[16,32]{1,0:T(8,128)S(1)}, bf16[16,16,320]{2,1,0:T(8,128)(2,1)S(1)}, bf16[16,16,432]{2,1,0:T(8,128)(2,1)S(1)}, f32[320,432]{1,0:...) while((s32[]{:T(128)}, f32[16,32]{1,0:T(8,128)S(1)}, ...), condition=%wide.region_5.6_spmd, body=%wide.region_2.5_spmd.sunk | while | flops 146921440 | bytes 1529325 | solution.py:103
  157.0 29.4 %all_to_all.41 = f32[32,4,128]{2,1,0:T(4,128)S(1)} all-to-all(f32[32,4,128]{2,1,0:T(4,128)S(1)} %broadcast_in_dim.58), channel_id=1, replica_groups=mesh['y'=8,'zh'=2,'core'=2,'zl'=4,'x'=4] {'core','zl','x'}, dimensions={0} | all-to-all | bytes 131072 | tf_op jit(solution)/shard_map/all_to_all | solution.py:23
  186.4 16.4 %all_to_all.42 = f32[16,4,128]{2,1,0:T(4,128)S(1)} all-to-all(f32[16,4,128]{2,1,0:T(4,128)S(1)} %broadcast_in_dim.59), channel_id=1, replica_groups=mesh['y'=8,'zh'=2,'core'=2,'zl'=4,'x'=4] {'y','zh'}, dimensions={0} | all-to-all | bytes 65536 | tf_op jit(solution)/shard_map/all_to_all | solution.py:23
  (113 shorter events, 23.8 us)
Async XLA Ops:
  0.0 83.1 %copy-start = (s32[48]{0:T(128)S(1)}, s32[48]{0:T(128)}, u32[]{:S(2)}) copy-start(s32[48]{0:T(128)} %param.13) | copy-start | bytes 580
  0.0 31.5 %copy-start.4 = (bf16[24,320]{1,0:T(8,128)(2,1)S(1)}, bf16[24,320]{1,0:T(8,128)(2,1)}, u32[]{:S(2)}) copy-start(bf16[24,320]{1,0:T(8,128)(2,1)} %param.9) | copy-start | bytes 46084
  0.9 44.0 %copy-start.3 = (bf16[320,160]{0,1:T(8,128)(2,1)S(1)}, bf16[320,160]{0,1:T(8,128)(2,1)}, u32[]{:S(2)}) copy-start(bf16[320,160]{0,1:T(8,128)(2,1)} %param.11) | copy-start | bytes 307204
  32.2 27.0 %all-to-all-start = ((bf16[16,24,320]{2,1,0:T(8,128)(2,1)}), bf16[16,24,320]{2,1,0:T(8,128)(2,1)S(1)}, u32[]{:S(2)}, u32[]{:S(2)}) async-start(bf16[16,24,320]{2,1,0:T(8,128)(2,1)} %broadcast_in_dim.27), calls=%async_computation | async-start | bytes 589824 | tf_op jit(solution)/shard_map/all_to_all | solution.py:23
  44.9 5.4 %collective-permute-start = (bf16[320,160]{0,1:T(8,128)(2,1)S(1)}, bf16[320,160]{0,1:T(8,128)(2,1)S(1)}, u32[]{:S(2)}, u32[]{:S(2)}) collective-permute-start(bf16[320,160]{0,1:T(8,128)(2,1)S(1)} %copy-done.3), channel_id=1, source_target_pairs={{0,16},{16,0},{1,17},{17,1},{2,18},{18,2},{3,19},{19,3},{4,20},{20... | collective-permute-start | bytes 307208 | tf_op jit(solution)/shard_map/ppermute | solution.py:29
  50.6 21.9 %collective-permute-start.3 = (bf16[768,432]{0,1:T(8,128)(2,1)S(1)}, bf16[768,432]{0,1:T(8,128)(2,1)S(1)}, u32[]{:S(2)}, u32[]{:S(2)}) collective-permute-start(bf16[768,432]{0,1:T(8,128)(2,1)S(1)} %copy.29), channel_id=1, source_target_pairs={{0,16},{16,0},{1,17},{17,1},{2,18},{18,2},{3,19},{19,3},{4,20},{20... | collective-permute-start | bytes 1990664 | tf_op jit(solution)/shard_map/ppermute | solution.py:29
  59.6 5.8 %copy-start.2 = (bf16[432,864]{1,0:T(8,128)(2,1)S(1)}, bf16[432,864]{1,0:T(8,128)(2,1)}, u32[]{:S(2)}) copy-start(bf16[432,864]{1,0:T(8,128)(2,1)} %param.10) | copy-start | bytes 2239492
  60.6 17.0 %all-to-all-start.1 = ((f32[16,24,320]{2,1,0:T(8,128)}), f32[16,24,320]{2,1,0:T(8,128)S(1)}, u32[]{:S(2)}, u32[]{:S(2)}) async-start(f32[16,24,320]{2,1,0:T(8,128)} %bitcast.6), calls=%async_computation.1 | async-start | bytes 1179648 | tf_op jit(solution)/shard_map/all_to_all | solution.py:59
  65.5 7.0 %collective-permute-start.2 = (bf16[432,432]{1,0:T(8,128)(2,1)S(1)}, bf16[432,432]{1,0:T(8,128)(2,1)S(1)}, u32[]{:S(2)}, u32[]{:S(2)}) collective-permute-start(bf16[432,432]{1,0:T(8,128)(2,1)S(1)} %broadcast_select_fusion), channel_id=1, source_target_pairs={{0,16},{16,0},{1,17},{17,1},{2,18},{18,2},{3,19},{19,3},{4,20},{20... | collective-permute-start | bytes 1119752 | tf_op jit(solution)/shard_map/ppermute | solution.py:29
  77.6 25.4 %all-to-all-start.4 = ((bf16[8,96,432]{2,1,0:T(8,128)(2,1)}), bf16[8,96,432]{2,1,0:T(8,128)(2,1)S(1)}, u32[]{:S(2)}, u32[]{:S(2)}) async-start(bf16[8,96,432]{2,1,0:T(8,128)(2,1)} %bitcast.14), calls=%async_computation.4 | async-start | bytes 1572864 | tf_op jit(solution)/shard_map/all_to_all | solution.py:77
  103.8 19.0 %all-to-all-start.2 = ((bf16[16,24,320]{2,1,0:T(8,128)(2,1)}), bf16[16,24,320]{2,1,0:T(8,128)(2,1)S(1)}, u32[]{:S(2)}, u32[]{:S(2)}) async-start(bf16[16,24,320]{2,1,0:T(8,128)(2,1)} %broadcast_in_dim.28), calls=%async_computation.2 | async-start | bytes 589824 | tf_op jit(solution)/shard_map/all_to_all | solution.py:23
  112.1 10.6 %collective-permute-start.4 = (f32[96,432]{1,0:T(8,128)S(1)}, f32[96,432]{1,0:T(8,128)S(1)}, u32[]{:S(2)}, u32[]{:S(2)}) collective-permute-start(f32[96,432]{1,0:T(8,128)S(1)} %convert_reduce_fusion), channel_id=1, source_target_pairs={{0,32},{32,0},{1,33},{33,1},{2,34},{34,2},{3,35},{35,3},{4,36},{36... | collective-permute-start | bytes 497672 | tf_op jit(solution)/shard_map/ppermute | solution.py:29
  122.8 4.5 %copy-start.1 = (f32[864,160]{0,1:T(8,128)S(1)}, f32[864,160]{0,1:T(8,128)}, u32[]{:S(2)}) copy-start(f32[864,160]{0,1:T(8,128)} %param.12) | copy-start | bytes 1658884
  123.8 17.8 %all-to-all-start.5 = ((bf16[8,96,432]{2,1,0:T(8,128)(2,1)}), bf16[8,96,432]{2,1,0:T(8,128)(2,1)S(1)}, u32[]{:S(2)}, u32[]{:S(2)}) async-start(bf16[8,96,432]{2,1,0:T(8,128)(2,1)} %broadcast_in_dim.56), calls=%async_computation.5 | async-start | bytes 1572864 | tf_op jit(solution)/shard_map/all_to_all | solution.py:23
  127.5 11.3 %collective-permute-start.5 = (f32[160,432]{1,0:T(8,128)S(1)}, f32[160,432]{1,0:T(8,128)S(1)}, u32[]{:S(2)}, u32[]{:S(2)}) collective-permute-start(f32[160,432]{1,0:T(8,128)S(1)} %slice_select_fusion.1), channel_id=1, source_target_pairs={{0,16},{16,0},{1,17},{17,1},{2,18},{18,2},{3,19},{19,3},{4,20},{20... | collective-permute-start | bytes 829448 | tf_op jit(solution)/shard_map/ppermute | solution.py:29
  136.8 3.5 %collective-permute-start.1 = (bf16[16,24,320]{2,1,0:T(8,128)(2,1)S(1)}, bf16[16,24,320]{2,1,0:T(8,128)(2,1)S(1)}, u32[]{:S(2)}, u32[]{:S(2)}) collective-permute-start(bf16[16,24,320]{2,1,0:T(8,128)(2,1)S(1)} %all-to-all-done.2), channel_id=1, source_target_pairs={{0,16},{16,0},{1,17},{17,1},{2,18},{18,2},{3,19},{19,3},{4,20},{20... | collective-permute-start | bytes 737288 | tf_op jit(solution)/shard_map/ppermute | solution.py:29

commit v2 on v1

--- a/solution.py
+++ b/solution.py
@@ -29,7 +29,11 @@
     return lax.ppermute(x, axis, SWAP)
 
 
-def ordered(mine, other, second, axis):
+def tie(*values):
+    return lax.optimization_barrier(values)
+
+
+def ordered(mine, other, second):
     lo = jnp.where(second, other, mine)
     hi = jnp.where(second, mine, other)
     return lo, hi
@@ -40,49 +44,56 @@
     second = core == 1
     half = basis_out.shape[1] // 2
 
-    grads = spread(grad_out, EX, 16).reshape(NTOK, -1)
+    act = spread(acts, ("y", "zh"), 16)
+    grads = lax.all_gather(grad_out, "x", axis=0, tiled=True)
 
     w_lo, w_hi = basis_out[:, :half], basis_out[:, half:]
     w_mine = jnp.where(second, w_hi, w_lo)
     w_other = swap(jnp.where(second, w_lo, w_hi), "core")
+    b_other = swap(basis_in, "core")
+    grads, act, w_other, b_other = tie(grads, act, w_other, b_other)
+
+    b_in = jnp.concatenate(ordered(basis_in, b_other, second), axis=1)
+    part_act = jnp.dot(
+        act.reshape(NTOK // 2, -1), b_in, preferred_element_type=f32
+    )
+    grads, part_act = tie(grads, part_act)
+    parts = lax.all_to_all(part_act.reshape(16, 24, -1), EX, 0, 0, tiled=True)
+    grads = lax.all_gather(grads, "zl", axis=0, tiled=True)
+    grads, parts = tie(grads, parts)
+    g_other = swap(grads, "core")
+    partial = jnp.dot(grads, w_mine, preferred_element_type=f32) + jnp.dot(
+        g_other, w_other, preferred_element_type=f32
+    )
+    partial = partial.astype(bf16)
+
+    rows = NTOK // 8
+    pieces = lax.all_to_all(
+        partial.reshape(8, rows, -1), "y", 0, 0, tiled=True
+    )
+    partial, act_piece = tie(partial, jnp.sum(parts, axis=0).astype(bf16))
+    act_x = lax.all_gather(act_piece, "x", axis=0, tiled=True)
+    pieces, act_x = tie(pieces, act_x)
+
+    piece = jnp.sum(pieces.astype(f32), axis=0)
+    piece_other = swap(piece, "zh")
+    act_half = lax.all_gather(act_x, "zl", axis=0, tiled=True)
+    slots = lax.axis_index("y") * rows + jnp.arange(rows, dtype=jnp.int32)
+    used = slots % TOKX < jnp.take(counts, slots // TOKX)
+    piece = ((piece + piece_other) * used.astype(f32)[:, None]).astype(bf16)
+    piece, act_half = tie(piece, act_half)
+
+    rot_grad = spread(piece, "y", 8).reshape(NTOK, -1)
+    act_other = swap(act_half, "core")
+    rot_act = jnp.stack(
+        ordered(act_half.reshape(16, 24, -1), act_other.reshape(16, 24, -1), second),
+        axis=1,
+    ).reshape(NTOK, -1)
     eig_t = eigvals.T
     e_lo, e_hi = eig_t[:, :half], eig_t[:, half:]
     e_mine = jnp.where(second, e_hi, e_lo)
     e_other = swap(jnp.where(second, e_lo, e_hi), "core")
-    eig = jnp.concatenate(ordered(e_mine, e_other, second, 0), axis=0)
-    recip = 1.0 / eig
-
-    b_other = swap(basis_in, "core")
-    b_in = jnp.concatenate(ordered(basis_in, b_other, second, 1), axis=1)
-    act = spread(acts, ("y", "zh"), 16).reshape(NTOK // 2, -1)
-    part_act = jnp.dot(act, b_in, preferred_element_type=f32)
-    part_act = lax.all_to_all(
-        part_act.reshape(16, 24, -1), EX, 0, 0, tiled=True
-    )
-    act_piece = jnp.sum(part_act, axis=0).astype(bf16)
-    act_half = spread(act_piece, EX, 16)
-    act_other = swap(act_half, "core")
-    rot_act = jnp.stack(
-        ordered(
-            act_half.reshape(16, 24, -1), act_other.reshape(16, 24, -1), second, 0
-        ),
-        axis=1,
-    ).reshape(NTOK, -1)
-
-    g_other = swap(grads, "core")
-    partial = jnp.dot(grads, w_mine, preferred_element_type=f32) + jnp.dot(
-        g_other, w_other, preferred_element_type=f32
-    )
-    rows = NTOK // 8
-    pieces = lax.all_to_all(
-        partial.astype(bf16).reshape(8, rows, -1), "y", 0, 0, tiled=True
-    )
-    piece = jnp.sum(pieces.astype(f32), axis=0)
-    piece = piece + swap(piece, "zh")
-    slots = lax.axis_index("y") * rows + jnp.arange(rows, dtype=jnp.int32)
-    used = slots % TOKX < jnp.take(counts, slots // TOKX)
-    piece = (piece * used.astype(f32)[:, None]).astype(bf16)
-    rot_grad = spread(piece, "y", 8).reshape(NTOK, -1)
+    recip = 1.0 / jnp.concatenate(ordered(e_mine, e_other, second), axis=0)
 
     cols_grad = rot_grad.shape[1]
     cols_act = rot_act.shape[1]

time: 204 us -> 205 us (level)
  blocking collectives: 76.4 us -> 94.6 us
  waiting for transfers between devices: 38.8 us -> 26.2 us
  starting transfers between devices: 62 us -> 57.9 us
    all_gather x0 -> x4, blocking collectives: none -> 63.4 us  [the longest x1 25.6 us: body(): grads = lax.all_gather(grads, 'zl', axis=0, tiled=True)]
    all_to_all x3 -> x2, blocking collectives: 76.4 us -> 31.2 us  [spread(): lax.all_to_all(jnp.broadcast_to(x[None], (n,) + x.shape), axes, 0, 0, til...]
    all_to_all x2, waiting for transfers between devices: 22.1 us -> 12.7 us  [the longest x1 12.7 us: body(): pieces = lax.all_to_all(partial.reshape(8, rows, -1), 'y', 0, 0, tiled=True)]
    ppermute x6, waiting for transfers between devices: 9.48 us -> 2.22 us  [swap(): return lax.ppermute(x, axis, SWAP)]
    all_to_all x3 -> x2, starting transfers between devices: 24.4 us -> 19.7 us  [spread(): lax.all_to_all(jnp.broadcast_to(x[None], (n,) + x.shape), axes, 0, 0, til...]
    all_to_all x3 -> x2, waiting for transfers between devices: 7.27 us -> 11.2 us  [spread(): lax.all_to_all(jnp.broadcast_to(x[None], (n,) + x.shape), axes, 0, 0, til...]
    all_to_all x2, starting transfers between devices: 10.1 us -> 12.7 us  [the longest x1 6.51 us: body(): parts = lax.all_to_all(part_act.reshape(16, 24, -1), EX, 0, 0, tiled=True)]
  transfers between devices with their start and end apart: 11 -> 10, of which waited for: 8 -> 4; matrix products, arithmetic and copies ran while one was open for 3% -> 1% of each run, Pallas kernels for 0% -> 0%
where the time goes in v2:
time: 205 us; the launch traced here: 204 us
  blocking collectives  94.6 us (46%)
  starting transfers between devices  57.9 us (28%)
  waiting for transfers between devices  26.2 us (13%)
  matrix products  12.7 us (6%)
  local copies, waits for them, and re-layouts  9.16 us (4%)
  other arithmetic  3.03 us (1%)
    all_to_all x2, blocking collectives, spread(): lax.all_to_all(jnp.broadcast_to(x[None], (n,) + x.shape), axes, 0, 0, til...  31.2 us
    all_gather x1, blocking collectives, body(): grads = lax.all_gather(grads, 'zl', axis=0, tiled=True)  25.6 us
    ppermute x6, starting transfers between devices, swap(): return lax.ppermute(x, axis, SWAP)  25.5 us
    all_to_all x2, starting transfers between devices, spread(): lax.all_to_all(jnp.broadcast_to(x[None], (n,) + x.shape), axes, 0, 0, til...  19.7 us
    all_gather x1, blocking collectives, body(): act_half = lax.all_gather(act_x, 'zl', axis=0, tiled=True)  17.9 us
    all_to_all x1, waiting for transfers between devices, body(): pieces = lax.all_to_all(partial.reshape(8, rows, -1), 'y', 0, 0, tiled=True)  12.7 us
    all_to_all x2, waiting for transfers between devices, spread(): lax.all_to_all(jnp.broadcast_to(x[None], (n,) + x.shape), axes, 0, 0, til...  11.2 us
    dot_general x16, matrix products, one_query(): projected = jnp.dot(train_act, precond, preferred_element_type=f32)  11 us
  transfers between devices with their start and end apart: 10, of which 4 were waited for; matrix products, arithmetic and copies ran while one was open for 1% of the time, Pallas kernels for 0%

profile of v2, /device:TPU:1, one launch (start us, length us, event | category | flops | bytes accessed | tf_op | source)
XLA Modules:
  0.0 204.2 jit_solution(2709151152537770197)
XLA Ops:
  0.0 1.5 broadcast_in_dim.40
  1.6 16.2 %all-to-all-start = ((bf16[16,24,320]{2,1,0:T(8,128)(2,1)}), bf16[16,24,320]{2,1,0:T(8,128)(2,1)S(1)}, u32[]{:S(2)}, u32[]{:S(2)}) async-start(bf16[16,24,320]{2,1,0:T(8,128)(2,1)} %broadcast_in_dim.40), calls=%async_computation | async-start | bytes 589824 | tf_op jit(solution)/shard_map/all_to_all | solution.py:23
  18.0 2.9 %collective-permute-start = (bf16[432,432]{1,0:T(8,128)(2,1)S(1)}, bf16[432,432]{1,0:T(8,128)(2,1)S(1)}, u32[]{:S(2)}, u32[]{:S(2)}) collective-permute-start(bf16[432,432]{1,0:T(8,128)(2,1)S(1)} %broadcast_select_fusion), channel_id=1, source_target_pairs={{0,16},{16,0},{1,17},{17,1},{2,18},{18,2},{3,19},{19,3},{4,20},{20... | collective-permute-start | bytes 1119752 | tf_op jit(solution)/shard_map/ppermute | solution.py:29
  20.9 1.9 collective-permute-start.1
  22.8 10.5 %all_gather.12 = bf16[192,432]{1,0:T(8,128)(2,1)S(1)} all-gather(bf16[48,432]{1,0:T(8,128)(2,1)S(1)} %copy-done.4), channel_id=1, replica_groups=mesh['y'=8,'zh'=2,'core'=2,'zl'=4,'x'=4] {'x'}, dimensions={0}, use_global_device_ids=true | all-gather | bytes 207360 | tf_op jit(solution)/shard_map/all_gather | solution.py:48
  33.6 1.1 copy.22
  34.7 6.5 %all-to-all-start.1 = ((f32[16,24,320]{2,1,0:T(8,128)}), f32[16,24,320]{2,1,0:T(8,128)S(1)}, u32[]{:S(2)}, u32[]{:S(2)}) async-start(f32[16,24,320]{2,1,0:T(8,128)} %bitcast.5), calls=%async_computation.1 | async-start | bytes 1179648 | tf_op jit(solution)/shard_map/all_to_all | solution.py:61
  41.2 25.6 %all_gather.13 = bf16[768,432]{1,0:T(8,128)(2,1)S(1)} all-gather(bf16[192,432]{1,0:T(8,128)(2,1)S(1)} %all_gather.12), channel_id=1, replica_groups=mesh['y'=8,'zh'=2,'core'=2,'zl'=4,'x'=4] {'zl'}, dimensions={0}, use_global_device_ids=true | all-gather | bytes 829440 | tf_op jit(solution)/shard_map/all_gather | solution.py:62
  67.0 6.7 %collective-permute-start.2 = (bf16[768,432]{0,1:T(8,128)(2,1)S(1)}, bf16[768,432]{0,1:T(8,128)(2,1)S(1)}, u32[]{:S(2)}, u32[]{:S(2)}) collective-permute-start(bf16[768,432]{0,1:T(8,128)(2,1)S(1)} %copy.23), channel_id=1, source_target_pairs={{0,16},{16,0},{1,17},{17,1},{2,18},{18,2},{3,19},{19,3},{4,20},{20... | collective-permute-start | bytes 1990664 | tf_op jit(solution)/shard_map/ppermute | solution.py:29
  76.1 1.2 copy.24
  77.2 6.2 %all-to-all-start.2 = ((bf16[8,96,432]{2,1,0:T(8,128)(2,1)}), bf16[8,96,432]{2,1,0:T(8,128)(2,1)S(1)}, u32[]{:S(2)}, u32[]{:S(2)}) async-start(bf16[8,96,432]{2,1,0:T(8,128)(2,1)} %bitcast.6), calls=%async_computation.2 | async-start | bytes 1572864 | tf_op jit(solution)/shard_map/all_to_all | solution.py:71
  83.4 1.2 gather_fusion
  84.7 9.5 %all_gather.14 = bf16[96,320]{1,0:T(8,128)(2,1)S(1)} all-gather(bf16[24,320]{1,0:T(8,128)(2,1)S(1)} %reduce_sum.52), channel_id=1, replica_groups=mesh['y'=8,'zh'=2,'core'=2,'zl'=4,'x'=4] {'x'}, dimensions={0}, use_global_device_ids=true | all-gather | bytes 76800 | tf_op jit(solution)/shard_map/all_gather | solution.py:75
  94.2 12.7 %all-to-all-done.2 = bf16[8,96,432]{2,1,0:T(8,128)(2,1)S(1)} async-done(((bf16[8,96,432]{2,1,0:T(8,128)(2,1)}), bf16[8,96,432]{2,1,0:T(8,128)(2,1)S(1)}, u32[]{:S(2)}, u32[]{:S(2)}) %all-to-all-start.2) | async-done | bytes 663584 | tf_op jit(solution)/shard_map/all_to_all | solution.py:71
  107.1 6.8 %collective-permute-start.3 = (f32[96,432]{1,0:T(8,128)S(1)}, f32[96,432]{1,0:T(8,128)S(1)}, u32[]{:S(2)}, u32[]{:S(2)}) collective-permute-start(f32[96,432]{1,0:T(8,128)S(1)} %convert_reduce_fusion), channel_id=1, source_target_pairs={{0,32},{32,0},{1,33},{33,1},{2,34},{34,2},{3,35},{35,3},{4,36},{36... | collective-permute-start | bytes 497672 | tf_op jit(solution)/shard_map/ppermute | solution.py:29
  113.9 17.9 %all_gather.15 = bf16[384,320]{1,0:T(8,128)(2,1)S(1)} all-gather(bf16[96,320]{1,0:T(8,128)(2,1)S(1)} %all_gather.14), channel_id=1, replica_groups=mesh['y'=8,'zh'=2,'core'=2,'zl'=4,'x'=4] {'zl'}, dimensions={0}, use_global_device_ids=true | all-gather | bytes 307200 | tf_op jit(solution)/shard_map/all_gather | solution.py:80
  132.9 3.5 %all-to-all-start.3 = ((bf16[8,96,432]{2,1,0:T(8,128)(2,1)}), bf16[8,96,432]{2,1,0:T(8,128)(2,1)S(1)}, u32[]{:S(2)}, u32[]{:S(2)}) async-start(bf16[8,96,432]{2,1,0:T(8,128)(2,1)} %broadcast_in_dim.42), calls=%async_computation.3 | async-start | bytes 1572864 | tf_op jit(solution)/shard_map/all_to_all | solution.py:23
  136.6 5.2 %collective-permute-start.5 = (f32[160,432]{1,0:T(8,128)S(1)}, f32[160,432]{1,0:T(8,128)S(1)}, u32[]{:S(2)}, u32[]{:S(2)}) collective-permute-start(f32[160,432]{1,0:T(8,128)S(1)} %slice_select_fusion.1), channel_id=1, source_target_pairs={{0,16},{16,0},{1,17},{17,1},{2,18},{18,2},{3,19},{19,3},{4,20},{20... | collective-permute-start | bytes 829448 | tf_op jit(solution)/shard_map/ppermute | solution.py:29
  141.9 1.9 collective-permute-start.4
  144.1 1.3 collective-permute-done.4
  145.6 11.2 %all-to-all-done.3 = bf16[8,96,432]{2,1,0:T(8,128)(2,1)S(1)} async-done(((bf16[8,96,432]{2,1,0:T(8,128)(2,1)}), bf16[8,96,432]{2,1,0:T(8,128)(2,1)S(1)}, u32[]{:S(2)}, u32[]{:S(2)}) %all-to-all-start.3) | async-done | bytes 663584 | tf_op jit(solution)/shard_map/all_to_all | solution.py:23
  157.1 15.1 %while.10 = (s32[]{:T(128)}, f32[16,32]{1,0:T(8,128)S(1)}, bf16[16,16,320]{2,1,0:T(8,128)(2,1)S(1)}, bf16[16,16,432]{2,1,0:T(8,128)(2,1)S(1)}, f32[320,432]{1,0:...) while((s32[]{:T(128)}, f32[16,32]{1,0:T(8,128)S(1)}, ...), condition=%wide.region_5.6_spmd, body=%wide.region_2.5_spmd.sunk | while | flops 146921440 | bytes 1529325 | solution.py:114
  172.3 15.9 %all_to_all.30 = f32[32,4,128]{2,1,0:T(4,128)S(1)} all-to-all(f32[32,4,128]{2,1,0:T(4,128)S(1)} %broadcast_in_dim.44), channel_id=1, replica_groups=mesh['y'=8,'zh'=2,'core'=2,'zl'=4,'x'=4] {'core','zl','x'}, dimensions={0} | all-to-all | bytes 131072 | tf_op jit(solution)/shard_map/all_to_all | solution.py:23
  188.2 15.3 %all_to_all.31 = f32[16,4,128]{2,1,0:T(4,128)S(1)} all-to-all(f32[16,4,128]{2,1,0:T(4,128)S(1)} %broadcast_in_dim.45), channel_id=1, replica_groups=mesh['y'=8,'zh'=2,'core'=2,'zl'=4,'x'=4] {'y','zh'}, dimensions={0} | all-to-all | bytes 65536 | tf_op jit(solution)/shard_map/all_to_all | solution.py:23
  (112 shorter events, 20.8 us)
Async XLA Ops:
  0.0 83.4 %copy-start = (s32[48]{0:T(128)S(1)}, s32[48]{0:T(128)}, u32[]{:S(2)}) copy-start(s32[48]{0:T(128)} %param.13) | copy-start | bytes 580
  0.0 17.8 %copy-start.2 = (bf16[432,864]{1,0:T(8,128)(2,1)S(1)}, bf16[432,864]{1,0:T(8,128)(2,1)}, u32[]{:S(2)}) copy-start(bf16[432,864]{1,0:T(8,128)(2,1)} %param.10) | copy-start | bytes 2239492
  0.0 20.8 %copy-start.3 = (bf16[320,160]{0,1:T(8,128)(2,1)S(1)}, bf16[320,160]{0,1:T(8,128)(2,1)}, u32[]{:S(2)}) copy-start(bf16[320,160]{0,1:T(8,128)(2,1)} %param.11) | copy-start | bytes 307204
  0.0 22.8 %copy-start.4 = (bf16[48,432]{1,0:T(8,128)(2,1)S(1)}, bf16[48,432]{1,0:T(8,128)(2,1)}, u32[]{:S(2)}) copy-start(bf16[48,432]{1,0:T(8,128)(2,1)} %param.8) | copy-start | bytes 124420
  1.6 31.7 %all-to-all-start = ((bf16[16,24,320]{2,1,0:T(8,128)(2,1)}), bf16[16,24,320]{2,1,0:T(8,128)(2,1)S(1)}, u32[]{:S(2)}, u32[]{:S(2)}) async-start(bf16[16,24,320]{2,1,0:T(8,128)(2,1)} %broadcast_in_dim.40), calls=%async_computation | async-start | bytes 589824 | tf_op jit(solution)/shard_map/all_to_all | solution.py:23
  18.0 15.3 %collective-permute-start = (bf16[432,432]{1,0:T(8,128)(2,1)S(1)}, bf16[432,432]{1,0:T(8,128)(2,1)S(1)}, u32[]{:S(2)}, u32[]{:S(2)}) collective-permute-start(bf16[432,432]{1,0:T(8,128)(2,1)S(1)} %broadcast_select_fusion), channel_id=1, source_target_pairs={{0,16},{16,0},{1,17},{17,1},{2,18},{18,2},{3,19},{19,3},{4,20},{20... | collective-permute-start | bytes 1119752 | tf_op jit(solution)/shard_map/ppermute | solution.py:29
  20.9 12.4 %collective-permute-start.1 = (bf16[320,160]{0,1:T(8,128)(2,1)S(1)}, bf16[320,160]{0,1:T(8,128)(2,1)S(1)}, u32[]{:S(2)}, u32[]{:S(2)}) collective-permute-start(bf16[320,160]{0,1:T(8,128)(2,1)S(1)} %copy-done.3), channel_id=1, source_target_pairs={{0,16},{16,0},{1,17},{17,1},{2,18},{18,2},{3,19},{19,3},{4,20},{20... | collective-permute-start | bytes 307208 | tf_op jit(solution)/shard_map/ppermute | solution.py:29
  34.7 32.1 %all-to-all-start.1 = ((f32[16,24,320]{2,1,0:T(8,128)}), f32[16,24,320]{2,1,0:T(8,128)S(1)}, u32[]{:S(2)}, u32[]{:S(2)}) async-start(f32[16,24,320]{2,1,0:T(8,128)} %bitcast.5), calls=%async_computation.1 | async-start | bytes 1179648 | tf_op jit(solution)/shard_map/all_to_all | solution.py:61
  67.0 8.4 %collective-permute-start.2 = (bf16[768,432]{0,1:T(8,128)(2,1)S(1)}, bf16[768,432]{0,1:T(8,128)(2,1)S(1)}, u32[]{:S(2)}, u32[]{:S(2)}) collective-permute-start(bf16[768,432]{0,1:T(8,128)(2,1)S(1)} %copy.23), channel_id=1, source_target_pairs={{0,16},{16,0},{1,17},{17,1},{2,18},{18,2},{3,19},{19,3},{4,20},{20... | collective-permute-start | bytes 1990664 | tf_op jit(solution)/shard_map/ppermute | solution.py:29
  77.2 29.7 %all-to-all-start.2 = ((bf16[8,96,432]{2,1,0:T(8,128)(2,1)}), bf16[8,96,432]{2,1,0:T(8,128)(2,1)S(1)}, u32[]{:S(2)}, u32[]{:S(2)}) async-start(bf16[8,96,432]{2,1,0:T(8,128)(2,1)} %bitcast.6), calls=%async_computation.2 | async-start | bytes 1572864 | tf_op jit(solution)/shard_map/all_to_all | solution.py:71
  107.1 24.8 %collective-permute-start.3 = (f32[96,432]{1,0:T(8,128)S(1)}, f32[96,432]{1,0:T(8,128)S(1)}, u32[]{:S(2)}, u32[]{:S(2)}) collective-permute-start(f32[96,432]{1,0:T(8,128)S(1)} %convert_reduce_fusion), channel_id=1, source_target_pairs={{0,32},{32,0},{1,33},{33,1},{2,34},{34,2},{3,35},{35,3},{4,36},{36... | collective-permute-start | bytes 497672 | tf_op jit(solution)/shard_map/ppermute | solution.py:29
  131.9 4.5 %copy-start.1 = (f32[864,160]{0,1:T(8,128)S(1)}, f32[864,160]{0,1:T(8,128)}, u32[]{:S(2)}) copy-start(f32[864,160]{0,1:T(8,128)} %param.12) | copy-start | bytes 1658884
  132.9 23.9 %all-to-all-start.3 = ((bf16[8,96,432]{2,1,0:T(8,128)(2,1)}), bf16[8,96,432]{2,1,0:T(8,128)(2,1)S(1)}, u32[]{:S(2)}, u32[]{:S(2)}) async-start(bf16[8,96,432]{2,1,0:T(8,128)(2,1)} %broadcast_in_dim.42), calls=%async_computation.3 | async-start | bytes 1572864 | tf_op jit(solution)/shard_map/all_to_all | solution.py:23
  136.6 7.2 %collective-permute-start.5 = (f32[160,432]{1,0:T(8,128)S(1)}, f32[160,432]{1,0:T(8,128)S(1)}, u32[]{:S(2)}, u32[]{:S(2)}) collective-permute-start(f32[160,432]{1,0:T(8,128)S(1)} %slice_select_fusion.1), channel_id=1, source_target_pairs={{0,16},{16,0},{1,17},{17,1},{2,18},{18,2},{3,19},{19,3},{4,20},{20... | collective-permute-start | bytes 829448 | tf_op jit(solution)/shard_map/ppermute | solution.py:29
  141.9 3.5 %collective-permute-start.4 = (bf16[384,320]{1,0:T(8,128)(2,1)S(1)}, bf16[384,320]{1,0:T(8,128)(2,1)S(1)}, u32[]{:S(2)}, u32[]{:S(2)}) collective-permute-start(bf16[384,320]{1,0:T(8,128)(2,1)S(1)} %all_gather.15), channel_id=1, source_target_pairs={{0,16},{16,0},{1,17},{17,1},{2,18},{18,2},{3,19},{19,3},{4,20},{20... | collective-permute-start | bytes 737288 | tf_op jit(solution)/shard_map/ppermute | solution.py:29

commit v3 on v2

--- a/solution.py
+++ b/solution.py
@@ -39,51 +39,65 @@
     return lo, hi
 
 
+def doubled(x, axis, bit):
+    n = SIZES[NAMES.index(axis)]
+    other = lax.ppermute(x, axis, [(i, i ^ bit) for i in range(n)])
+    second = lax.axis_index(axis) // bit % 2 == 1
+    return jnp.concatenate(ordered(x, other, second), axis=0)
+
+
+def scattered(x, axis, dim):
+    here = lax.axis_index(axis)
+    total = lax.dynamic_index_in_dim(x, here, dim, keepdims=False)
+    for bit in (1, 2, 3):
+        block = lax.dynamic_index_in_dim(x, here ^ bit, dim, keepdims=False)
+        total = total + lax.ppermute(block, axis, [(i, i ^ bit) for i in range(4)])
+    return total
+
+
 def body(grad_out, acts, basis_out, basis_in, eigvals, counts):
     core = lax.axis_index("core")
     second = core == 1
     half = basis_out.shape[1] // 2
 
-    act = spread(acts, ("y", "zh"), 16)
-    grads = lax.all_gather(grad_out, "x", axis=0, tiled=True)
-
+    grads = spread(grad_out, EX, 16).reshape(NTOK, -1)
+    act = doubled(acts, "zh", 1)
     w_lo, w_hi = basis_out[:, :half], basis_out[:, half:]
     w_mine = jnp.where(second, w_hi, w_lo)
     w_other = swap(jnp.where(second, w_lo, w_hi), "core")
     b_other = swap(basis_in, "core")
-    grads, act, w_other, b_other = tie(grads, act, w_other, b_other)
+    b_in = jnp.concatenate(ordered(basis_in, b_other, second), axis=1)
+    act = doubled(act, "y", 1)
+    act = doubled(act, "y", 2)
+    grads, w_other, act = tie(grads, w_other, act)
 
-    b_in = jnp.concatenate(ordered(basis_in, b_other, second), axis=1)
-    part_act = jnp.dot(
-        act.reshape(NTOK // 2, -1), b_in, preferred_element_type=f32
-    )
-    grads, part_act = tie(grads, part_act)
-    parts = lax.all_to_all(part_act.reshape(16, 24, -1), EX, 0, 0, tiled=True)
-    grads = lax.all_gather(grads, "zl", axis=0, tiled=True)
-    grads, parts = tie(grads, parts)
     g_other = swap(grads, "core")
+    act = doubled(act, "y", 4)
     partial = jnp.dot(grads, w_mine, preferred_element_type=f32) + jnp.dot(
         g_other, w_other, preferred_element_type=f32
     )
-    partial = partial.astype(bf16)
+    partial, act, b_in = tie(partial.astype(bf16), act, b_in)
 
     rows = NTOK // 8
     pieces = lax.all_to_all(
         partial.reshape(8, rows, -1), "y", 0, 0, tiled=True
     )
-    partial, act_piece = tie(partial, jnp.sum(parts, axis=0).astype(bf16))
-    act_x = lax.all_gather(act_piece, "x", axis=0, tiled=True)
-    pieces, act_x = tie(pieces, act_x)
+    part_act = jnp.dot(act, b_in, preferred_element_type=f32)
+    part_act = part_act.reshape(4, 4, 24, -1)
+    part_act = scattered(part_act, "x", 1)
+    act_piece = scattered(part_act, "zl", 0).astype(bf16)
+    pieces, act_piece = tie(pieces, act_piece)
 
     piece = jnp.sum(pieces.astype(f32), axis=0)
     piece_other = swap(piece, "zh")
-    act_half = lax.all_gather(act_x, "zl", axis=0, tiled=True)
+    act_x = lax.all_gather(act_piece, "x", axis=0, tiled=True)
     slots = lax.axis_index("y") * rows + jnp.arange(rows, dtype=jnp.int32)
     used = slots % TOKX < jnp.take(counts, slots // TOKX)
     piece = ((piece + piece_other) * used.astype(f32)[:, None]).astype(bf16)
-    piece, act_half = tie(piece, act_half)
+    piece, act_x = tie(piece, act_x)
 
     rot_grad = spread(piece, "y", 8).reshape(NTOK, -1)
+    act_half = lax.all_gather(act_x, "zl", axis=0, tiled=True)
     act_other = swap(act_half, "core")
     rot_act = jnp.stack(
         ordered(act_half.reshape(16, 24, -1), act_other.reshape(16, 24, -1), second),

time: 205 us -> 194 us (0.946)
  starting transfers between devices: 57.9 us -> 92.8 us
  blocking collectives: 94.6 us -> 61 us
  waiting for transfers between devices: 26.2 us -> 13.1 us
    ppermute x0 -> x10, starting transfers between devices: none -> 44.7 us  [the longest x4 26.5 us: doubled(): other = lax.ppermute(x, axis, [(i, i ^ bit) for i in range(n)])]
    all_gather x2 -> x0, blocking collectives: 36 us -> none  [the longest x1 25.6 us: body(): grads = lax.all_gather(grads, 'zl', axis=0, tiled=True)]
    all_to_all x1, waiting for transfers between devices: 12.7 us -> 0.01 us  [body(): pieces = lax.all_to_all(partial.reshape(8, rows, -1), 'y', 0, 0, tiled=True)]
    ppermute x0 -> x10, waiting for transfers between devices: none -> 9.57 us  [the longest x4 4.89 us: doubled(): other = lax.ppermute(x, axis, [(i, i ^ bit) for i in range(n)])]
    all_to_all x2, waiting for transfers between devices: 11.2 us -> 1.86 us  [spread(): lax.all_to_all(jnp.broadcast_to(x[None], (n,) + x.shape), axes, 0, 0, til...]
    all_to_all x2, starting transfers between devices: 19.7 us -> 12.7 us  [spread(): lax.all_to_all(jnp.broadcast_to(x[None], (n,) + x.shape), axes, 0, 0, til...]
    all_to_all x2, blocking collectives: 31.2 us -> 37.8 us  [spread(): lax.all_to_all(jnp.broadcast_to(x[None], (n,) + x.shape), axes, 0, 0, til...]
    all_to_all x1 -> x0, starting transfers between devices: 6.51 us -> none  [body(): parts = lax.all_to_all(part_act.reshape(16, 24, -1), EX, 0, 0, tiled=True)]
  transfers between devices with their start and end apart: 10 -> 19, of which waited for: 4 -> 8; matrix products, arithmetic and copies ran while one was open for 1% -> 3% of each run, Pallas kernels for 0% -> 0%
where the time goes in v3:
time: 194 us; the launch traced here: 193 us
  starting transfers between devices  92.8 us (48%)
  blocking collectives  61 us (31%)
  waiting for transfers between devices  13.1 us (7%)
  matrix products  12.7 us (7%)
  local copies, waits for them, and re-layouts  8.42 us (4%)
  other arithmetic  4.14 us (2%)
    all_to_all x2, blocking collectives, spread(): lax.all_to_all(jnp.broadcast_to(x[None], (n,) + x.shape), axes, 0, 0, til...  37.8 us
    ppermute x6, starting transfers between devices, swap(): return lax.ppermute(x, axis, SWAP)  26.7 us
    ppermute x4, starting transfers between devices, doubled(): other = lax.ppermute(x, axis, [(i, i ^ bit) for i in range(n)])  26.5 us
    ppermute x6, starting transfers between devices, scattered(): total = total + lax.ppermute(block, axis, [(i, i ^ bit) for i in range(4)])  18.3 us
    all_gather x1, blocking collectives, body(): act_half = lax.all_gather(act_x, 'zl', axis=0, tiled=True)  13.9 us
    all_to_all x2, starting transfers between devices, spread(): lax.all_to_all(jnp.broadcast_to(x[None], (n,) + x.shape), axes, 0, 0, til...  12.7 us
    dot_general x16, matrix products, one_query(): projected = jnp.dot(train_act, precond, preferred_element_type=f32)  11 us
    all_gather x1, blocking collectives, body(): act_x = lax.all_gather(act_piece, 'x', axis=0, tiled=True)  9.24 us
  transfers between devices with their start and end apart: 19, of which 8 were waited for; matrix products, arithmetic and copies ran while one was open for 3% of the time, Pallas kernels for 0%

profile of v3, /device:TPU:1, one launch (start us, length us, event | category | flops | bytes accessed | tf_op | source)
XLA Modules:
  0.0 193.2 jit_solution(1545791599613500930)
XLA Ops:
  0.0 11.6 %collective-permute-start.1 = (bf16[24,320]{1,0:T(8,128)(2,1)}, bf16[24,320]{1,0:T(8,128)(2,1)S(1)}, u32[]{:S(2)}, u32[]{:S(2)}) collective-permute-start(bf16[24,320]{1,0:T(8,128)(2,1)} %param.9), channel_id=1, source_target_pairs={{0,32},{32,0},{1,33},{33,1},{2,34},{34,2},{3,35},{35,3},{4,36},{36... | collective-permute-start | bytes 46088 | tf_op jit(solution)/shard_map/ppermute | solution.py:44
  13.4 7.0 %all-to-all-start = ((bf16[16,48,432]{2,1,0:T(8,128)(2,1)}), bf16[16,48,432]{2,1,0:T(8,128)(2,1)S(1)}, u32[]{:S(2)}, u32[]{:S(2)}) async-start(bf16[16,48,432]{2,1,0:T(8,128)(2,1)} %broadcast_in_dim.40), calls=%async_computation | async-start | bytes 1572864 | tf_op jit(solution)/shard_map/all_to_all | solution.py:23
  20.4 3.2 %collective-permute-start.2 = (bf16[48,320]{1,0:T(8,128)(2,1)S(1)}, bf16[48,320]{1,0:T(8,128)(2,1)S(1)}, u32[]{:S(2)}, u32[]{:S(2)}) collective-permute-start(bf16[48,320]{1,0:T(8,128)(2,1)S(1)} %pad_maximum_fusion.5), channel_id=1, source_target_pairs={{0,64},{64,0},{128,192},{192,128},{256,320},{320,256},{384,448},{4... | collective-permute-start | bytes 92168 | tf_op jit(solution)/shard_map/ppermute | solution.py:44
  25.5 4.2 %collective-permute-start.3 = (bf16[96,320]{1,0:T(8,128)(2,1)S(1)}, bf16[96,320]{1,0:T(8,128)(2,1)S(1)}, u32[]{:S(2)}, u32[]{:S(2)}) collective-permute-start(bf16[96,320]{1,0:T(8,128)(2,1)S(1)} %pad_maximum_fusion.4), channel_id=1, source_target_pairs={{0,128},{64,192},{128,0},{192,64},{256,384},{320,448},{384,256},{4... | collective-permute-start | bytes 184328 | tf_op jit(solution)/shard_map/ppermute | solution.py:44
  29.9 4.3 %collective-permute-start = (bf16[432,432]{1,0:T(8,128)(2,1)S(1)}, bf16[432,432]{1,0:T(8,128)(2,1)S(1)}, u32[]{:S(2)}, u32[]{:S(2)}) collective-permute-start(bf16[432,432]{1,0:T(8,128)(2,1)S(1)} %broadcast_select_fusion), channel_id=1, source_target_pairs={{0,16},{16,0},{1,17},{17,1},{2,18},{18,2},{3,19},{19,3},{4,20},{20... | collective-permute-start | bytes 1119752 | tf_op jit(solution)/shard_map/ppermute | solution.py:29
  38.4 5.3 %collective-permute-start.4 = (bf16[768,432]{0,1:T(8,128)(2,1)S(1)}, bf16[768,432]{0,1:T(8,128)(2,1)S(1)}, u32[]{:S(2)}, u32[]{:S(2)}) collective-permute-start(bf16[768,432]{0,1:T(8,128)(2,1)S(1)} %copy.26), channel_id=1, source_target_pairs={{0,16},{16,0},{1,17},{17,1},{2,18},{18,2},{3,19},{19,3},{4,20},{20... | collective-permute-start | bytes 1990664 | tf_op jit(solution)/shard_map/ppermute | solution.py:29
  43.7 7.5 %collective-permute-start.5 = (bf16[192,320]{1,0:T(8,128)(2,1)S(1)}, bf16[192,320]{1,0:T(8,128)(2,1)S(1)}, u32[]{:S(2)}, u32[]{:S(2)}) collective-permute-start(bf16[192,320]{1,0:T(8,128)(2,1)S(1)} %pad_maximum_fusion.3), channel_id=1, source_target_pairs={{0,256},{64,320},{128,384},{192,448},{256,0},{320,64},{384,128},{4... | collective-permute-start | bytes 368648 | tf_op jit(solution)/shard_map/ppermute | solution.py:44
  52.2 3.1 %collective-permute-done.5 = bf16[192,320]{1,0:T(8,128)(2,1)S(1)} collective-permute-done((bf16[192,320]{1,0:T(8,128)(2,1)S(1)}, bf16[192,320]{1,0:T(8,128)(2,1)S(1)}, u32[]{:S(2)}, u32[]{:S(2)}) %collective-permute-start.5) | collective-permute-done | bytes 122912 | tf_op jit(solution)/shard_map/ppermute | solution.py:44
  57.9 8.7 %all-to-all-start.1 = ((bf16[8,96,432]{2,1,0:T(8,128)(2,1)}), bf16[8,96,432]{2,1,0:T(8,128)(2,1)S(1)}, u32[]{:S(2)}, u32[]{:S(2)}) async-start(bf16[8,96,432]{2,1,0:T(8,128)(2,1)} %bitcast.5), calls=%async_computation.1 | async-start | bytes 1572864 | tf_op jit(solution)/shard_map/all_to_all | solution.py:82
  67.0 3.5 %collective-permute-start.9 = (f32[4,24,320]{2,1,0:T(8,128)S(1)}, f32[4,24,320]{2,1,0:T(8,128)S(1)}, u32[]{:S(2)}, u32[]{:S(2)}) collective-permute-start(f32[4,24,320]{2,1,0:T(8,128)S(1)} %get-tuple-element.117), channel_id=1, source_target_pairs={{0,3},{1,2},{2,1},{3,0},{4,7},{5,6},{6,5},{7,4},{8,11},{9,10},{10,... | collective-permute-start | bytes 368648 | tf_op jit(solution)/shard_map/ppermute | solution.py:54
  70.5 2.5 %collective-permute-start.8 = (f32[4,24,320]{2,1,0:T(8,128)S(1)}, f32[4,24,320]{2,1,0:T(8,128)S(1)}, u32[]{:S(2)}, u32[]{:S(2)}) collective-permute-start(f32[4,24,320]{2,1,0:T(8,128)S(1)} %get-tuple-element.118), channel_id=1, source_target_pairs={{0,2},{1,3},{2,0},{3,1},{4,6},{5,7},{6,4},{7,5},{8,10},{9,11},{10,... | collective-permute-start | bytes 368648 | tf_op jit(solution)/shard_map/ppermute | solution.py:54
  73.1 2.9 %collective-permute-start.7 = (f32[4,24,320]{2,1,0:T(8,128)S(1)}, f32[4,24,320]{2,1,0:T(8,128)S(1)}, u32[]{:S(2)}, u32[]{:S(2)}) collective-permute-start(f32[4,24,320]{2,1,0:T(8,128)S(1)} %get-tuple-element.116), channel_id=1, source_target_pairs={{0,1},{1,0},{2,3},{3,2},{4,5},{5,4},{6,7},{7,6},{8,9},{9,8},{10,11... | collective-permute-start | bytes 368648 | tf_op jit(solution)/shard_map/ppermute | solution.py:54
  78.3 2.2 %collective-permute-done.7 = f32[4,24,320]{2,1,0:T(8,128)S(1)} collective-permute-done((f32[4,24,320]{2,1,0:T(8,128)S(1)}, f32[4,24,320]{2,1,0:T(8,128)S(1)}, u32[]{:S(2)}, u32[]{:S(2)}) %collective-permute-start.7) | collective-permute-done | bytes 122912 | tf_op jit(solution)/shard_map/ppermute | solution.py:54
  80.5 3.4 %collective-permute-start.12 = (f32[24,320]{1,0:T(8,128)S(1)}, f32[24,320]{1,0:T(8,128)S(1)}, u32[]{:S(2)}, u32[]{:S(2)}) collective-permute-start(f32[24,320]{1,0:T(8,128)S(1)} %get-tuple-element.124), channel_id=1, source_target_pairs={{0,12},{4,8},{8,4},{12,0},{1,13},{5,9},{9,5},{13,1},{2,14},{6,10},... | collective-permute-start | bytes 92168 | tf_op jit(solution)/shard_map/ppermute | solution.py:54
  83.9 2.7 %collective-permute-start.11 = (f32[24,320]{1,0:T(8,128)S(1)}, f32[24,320]{1,0:T(8,128)S(1)}, u32[]{:S(2)}, u32[]{:S(2)}) collective-permute-start(f32[24,320]{1,0:T(8,128)S(1)} %get-tuple-element.125), channel_id=1, source_target_pairs={{0,8},{4,12},{8,0},{12,4},{1,9},{5,13},{9,1},{13,5},{2,10},{6,14},... | collective-permute-start | bytes 92168 | tf_op jit(solution)/shard_map/ppermute | solution.py:54
  86.6 3.2 %collective-permute-start.10 = (f32[24,320]{1,0:T(8,128)S(1)}, f32[24,320]{1,0:T(8,128)S(1)}, u32[]{:S(2)}, u32[]{:S(2)}) collective-permute-start(f32[24,320]{1,0:T(8,128)S(1)} %get-tuple-element.123), channel_id=1, source_target_pairs={{0,4},{4,0},{8,12},{12,8},{1,5},{5,1},{9,13},{13,9},{2,6},{6,2},{1... | collective-permute-start | bytes 92168 | tf_op jit(solution)/shard_map/ppermute | solution.py:54
  93.5 9.2 %all_gather.6 = bf16[96,320]{1,0:T(8,128)(2,1)S(1)} all-gather(bf16[24,320]{1,0:T(8,128)(2,1)S(1)} %fusion.22), channel_id=1, replica_groups=mesh['y'=8,'zh'=2,'core'=2,'zl'=4,'x'=4] {'x'}, dimensions={0}, use_global_device_ids=true | all-gather | bytes 76800 | tf_op jit(solution)/shard_map/all_gather | solution.py:93
  104.5 5.7 %all-to-all-start.2 = ((bf16[8,96,432]{2,1,0:T(8,128)(2,1)}), bf16[8,96,432]{2,1,0:T(8,128)(2,1)S(1)}, u32[]{:S(2)}, u32[]{:S(2)}) async-start(bf16[8,96,432]{2,1,0:T(8,128)(2,1)} %broadcast_in_dim.42), calls=%async_computation.2 | async-start | bytes 1572864 | tf_op jit(solution)/shard_map/all_to_all | solution.py:23
  110.4 9.8 %collective-permute-start.15 = (f32[160,432]{1,0:T(8,128)S(1)}, f32[160,432]{1,0:T(8,128)S(1)}, u32[]{:S(2)}, u32[]{:S(2)}) collective-permute-start(f32[160,432]{1,0:T(8,128)S(1)} %slice_select_fusion.1), channel_id=1, source_target_pairs={{0,16},{16,0},{1,17},{17,1},{2,18},{18,2},{3,19},{19,3},{4,20},{20... | collective-permute-start | bytes 829448 | tf_op jit(solution)/shard_map/ppermute | solution.py:29
  120.2 13.9 %all_gather.7 = bf16[384,320]{1,0:T(8,128)(2,1)S(1)} all-gather(bf16[96,320]{1,0:T(8,128)(2,1)S(1)} %all_gather.6), channel_id=1, replica_groups=mesh['y'=8,'zh'=2,'core'=2,'zl'=4,'x'=4] {'zl'}, dimensions={0}, use_global_device_ids=true | all-gather | bytes 307200 | tf_op jit(solution)/shard_map/all_gather | solution.py:100
  134.1 3.5 %collective-permute-start.14 = (bf16[384,320]{1,0:T(8,128)(2,1)S(1)}, bf16[384,320]{1,0:T(8,128)(2,1)S(1)}, u32[]{:S(2)}, u32[]{:S(2)}) collective-permute-start(bf16[384,320]{1,0:T(8,128)(2,1)S(1)} %all_gather.7), channel_id=1, source_target_pairs={{0,16},{16,0},{1,17},{17,1},{2,18},{18,2},{3,19},{19,3},{4,20},{20... | collective-permute-start | bytes 737288 | tf_op jit(solution)/shard_map/ppermute | solution.py:29
  139.4 15.1 %while.10 = (s32[]{:T(128)}, f32[16,32]{1,0:T(8,128)S(1)}, bf16[16,16,320]{2,1,0:T(8,128)(2,1)S(1)}, bf16[16,16,432]{2,1,0:T(8,128)(2,1)S(1)}, f32[320,432]{1,0:...) while((s32[]{:T(128)}, f32[16,32]{1,0:T(8,128)S(1)}, ...), condition=%wide.region_4.5_spmd, body=%wide.region_1.4_spmd.sunk | while | flops 146921440 | bytes 1529333 | solution.py:128
  154.6 14.0 %all_to_all.25 = f32[32,4,128]{2,1,0:T(4,128)S(1)} all-to-all(f32[32,4,128]{2,1,0:T(4,128)S(1)} %broadcast_in_dim.44), channel_id=1, replica_groups=mesh['y'=8,'zh'=2,'core'=2,'zl'=4,'x'=4] {'core','zl','x'}, dimensions={0} | all-to-all | bytes 131072 | tf_op jit(solution)/shard_map/all_to_all | solution.py:23
  168.7 23.8 %all_to_all.26 = f32[16,4,128]{2,1,0:T(4,128)S(1)} all-to-all(f32[16,4,128]{2,1,0:T(4,128)S(1)} %broadcast_in_dim.45), channel_id=1, replica_groups=mesh['y'=8,'zh'=2,'core'=2,'zl'=4,'x'=4] {'y','zh'}, dimensions={0} | all-to-all | bytes 65536 | tf_op jit(solution)/shard_map/all_to_all | solution.py:23
  (144 shorter events, 36.9 us)
Async XLA Ops:
  0.0 89.8 %copy-start = (s32[48]{0:T(128)S(1)}, s32[48]{0:T(128)}, u32[]{:S(2)}) copy-start(s32[48]{0:T(128)} %param.13) | copy-start | bytes 580
  0.0 20.4 %copy-start.6 = (bf16[24,320]{1,0:T(8,128)(2,1)S(1)}, bf16[24,320]{1,0:T(8,128)(2,1)}, u32[]{:S(2)}) copy-start(bf16[24,320]{1,0:T(8,128)(2,1)} %param.9) | copy-start | bytes 46084
  0.0 29.7 %copy-start.2 = (bf16[432,864]{1,0:T(8,128)(2,1)S(1)}, bf16[432,864]{1,0:T(8,128)(2,1)}, u32[]{:S(2)}) copy-start(bf16[432,864]{1,0:T(8,128)(2,1)} %param.10) | copy-start | bytes 2239492
  0.0 20.4 %collective-permute-start.1 = (bf16[24,320]{1,0:T(8,128)(2,1)}, bf16[24,320]{1,0:T(8,128)(2,1)S(1)}, u32[]{:S(2)}, u32[]{:S(2)}) collective-permute-start(bf16[24,320]{1,0:T(8,128)(2,1)} %param.9), channel_id=1, source_target_pairs={{0,32},{32,0},{1,33},{33,1},{2,34},{34,2},{3,35},{35,3},{4,36},{36... | collective-permute-start | bytes 46088 | tf_op jit(solution)/shard_map/ppermute | solution.py:44
  13.4 20.8 %copy-start.5 = (bf16[320,160]{0,1:T(8,128)(2,1)S(1)}, bf16[320,160]{0,1:T(8,128)(2,1)}, u32[]{:S(2)}) copy-start(bf16[320,160]{0,1:T(8,128)(2,1)} %param.11) | copy-start | bytes 307204
  13.4 24.8 %all-to-all-start = ((bf16[16,48,432]{2,1,0:T(8,128)(2,1)}), bf16[16,48,432]{2,1,0:T(8,128)(2,1)S(1)}, u32[]{:S(2)}, u32[]{:S(2)}) async-start(bf16[16,48,432]{2,1,0:T(8,128)(2,1)} %broadcast_in_dim.40), calls=%async_computation | async-start | bytes 1572864 | tf_op jit(solution)/shard_map/all_to_all | solution.py:23
  20.4 5.0 %collective-permute-start.2 = (bf16[48,320]{1,0:T(8,128)(2,1)S(1)}, bf16[48,320]{1,0:T(8,128)(2,1)S(1)}, u32[]{:S(2)}, u32[]{:S(2)}) collective-permute-start(bf16[48,320]{1,0:T(8,128)(2,1)S(1)} %pad_maximum_fusion.5), channel_id=1, source_target_pairs={{0,64},{64,0},{128,192},{192,128},{256,320},{320,256},{384,448},{4... | collective-permute-start | bytes 92168 | tf_op jit(solution)/shard_map/ppermute | solution.py:44
  25.5 10.7 %collective-permute-start.3 = (bf16[96,320]{1,0:T(8,128)(2,1)S(1)}, bf16[96,320]{1,0:T(8,128)(2,1)S(1)}, u32[]{:S(2)}, u32[]{:S(2)}) collective-permute-start(bf16[96,320]{1,0:T(8,128)(2,1)S(1)} %pad_maximum_fusion.4), channel_id=1, source_target_pairs={{0,128},{64,192},{128,0},{192,64},{256,384},{320,448},{384,256},{4... | collective-permute-start | bytes 184328 | tf_op jit(solution)/shard_map/ppermute | solution.py:44
  29.9 6.4 %collective-permute-start = (bf16[432,432]{1,0:T(8,128)(2,1)S(1)}, bf16[432,432]{1,0:T(8,128)(2,1)S(1)}, u32[]{:S(2)}, u32[]{:S(2)}) collective-permute-start(bf16[432,432]{1,0:T(8,128)(2,1)S(1)} %broadcast_select_fusion), channel_id=1, source_target_pairs={{0,16},{16,0},{1,17},{17,1},{2,18},{18,2},{3,19},{19,3},{4,20},{20... | collective-permute-start | bytes 1119752 | tf_op jit(solution)/shard_map/ppermute | solution.py:29
  34.2 17.0 %collective-permute-start.6 = (bf16[320,160]{0,1:T(8,128)(2,1)S(1)}, bf16[320,160]{0,1:T(8,128)(2,1)}, u32[]{:S(2)}, u32[]{:S(2)}) collective-permute-start(bf16[320,160]{0,1:T(8,128)(2,1)S(1)} %copy-done.5), channel_id=1, source_target_pairs={{0,16},{16,0},{1,17},{17,1},{2,18},{18,2},{3,19},{19,3},{4,20},{20... | collective-permute-start | bytes 307208 | tf_op jit(solution)/shard_map/ppermute | solution.py:29
  38.4 16.9 %copy-start.4 = (bf16[432,432]{1,0:T(8,128)(2,1)S(1)}, bf16[432,432]{1,0:T(8,128)(2,1)}, u32[]{:S(2)}) copy-start(bf16[432,432]{1,0:T(8,128)(2,1)} %copy-done.3) | copy-start | bytes 1119748
  38.4 16.9 %collective-permute-start.4 = (bf16[768,432]{0,1:T(8,128)(2,1)S(1)}, bf16[768,432]{0,1:T(8,128)(2,1)S(1)}, u32[]{:S(2)}, u32[]{:S(2)}) collective-permute-start(bf16[768,432]{0,1:T(8,128)(2,1)S(1)} %copy.26), channel_id=1, source_target_pairs={{0,16},{16,0},{1,17},{17,1},{2,18},{18,2},{3,19},{19,3},{4,20},{20... | collective-permute-start | bytes 1990664 | tf_op jit(solution)/shard_map/ppermute | solution.py:29
  43.7 11.6 %collective-permute-start.5 = (bf16[192,320]{1,0:T(8,128)(2,1)S(1)}, bf16[192,320]{1,0:T(8,128)(2,1)S(1)}, u32[]{:S(2)}, u32[]{:S(2)}) collective-permute-start(bf16[192,320]{1,0:T(8,128)(2,1)S(1)} %pad_maximum_fusion.3), channel_id=1, source_target_pairs={{0,256},{64,320},{128,384},{192,448},{256,0},{320,64},{384,128},{4... | collective-permute-start | bytes 368648 | tf_op jit(solution)/shard_map/ppermute | solution.py:44
  57.9 33.5 %all-to-all-start.1 = ((bf16[8,96,432]{2,1,0:T(8,128)(2,1)}), bf16[8,96,432]{2,1,0:T(8,128)(2,1)S(1)}, u32[]{:S(2)}, u32[]{:S(2)}) async-start(bf16[8,96,432]{2,1,0:T(8,128)(2,1)} %bitcast.5), calls=%async_computation.1 | async-start | bytes 1572864 | tf_op jit(solution)/shard_map/all_to_all | solution.py:82
  67.0 9.0 %collective-permute-start.9 = (f32[4,24,320]{2,1,0:T(8,128)S(1)}, f32[4,24,320]{2,1,0:T(8,128)S(1)}, u32[]{:S(2)}, u32[]{:S(2)}) collective-permute-start(f32[4,24,320]{2,1,0:T(8,128)S(1)} %get-tuple-element.117), channel_id=1, source_target_pairs={{0,3},{1,2},{2,1},{3,0},{4,7},{5,6},{6,5},{7,4},{8,11},{9,10},{10,... | collective-permute-start | bytes 368648 | tf_op jit(solution)/shard_map/ppermute | solution.py:54
  70.5 7.7 %collective-permute-start.8 = (f32[4,24,320]{2,1,0:T(8,128)S(1)}, f32[4,24,320]{2,1,0:T(8,128)S(1)}, u32[]{:S(2)}, u32[]{:S(2)}) collective-permute-start(f32[4,24,320]{2,1,0:T(8,128)S(1)} %get-tuple-element.118), channel_id=1, source_target_pairs={{0,2},{1,3},{2,0},{3,1},{4,6},{5,7},{6,4},{7,5},{8,10},{9,11},{10,... | collective-permute-start | bytes 368648 | tf_op jit(solution)/shard_map/ppermute | solution.py:54
  73.1 7.4 %collective-permute-start.7 = (f32[4,24,320]{2,1,0:T(8,128)S(1)}, f32[4,24,320]{2,1,0:T(8,128)S(1)}, u32[]{:S(2)}, u32[]{:S(2)}) collective-permute-start(f32[4,24,320]{2,1,0:T(8,128)S(1)} %get-tuple-element.116), channel_id=1, source_target_pairs={{0,1},{1,0},{2,3},{3,2},{4,5},{5,4},{6,7},{7,6},{8,9},{9,8},{10,11... | collective-permute-start | bytes 368648 | tf_op jit(solution)/shard_map/ppermute | solution.py:54
  80.5 10.6 %collective-permute-start.12 = (f32[24,320]{1,0:T(8,128)S(1)}, f32[24,320]{1,0:T(8,128)S(1)}, u32[]{:S(2)}, u32[]{:S(2)}) collective-permute-start(f32[24,320]{1,0:T(8,128)S(1)} %get-tuple-element.124), channel_id=1, source_target_pairs={{0,12},{4,8},{8,4},{12,0},{1,13},{5,9},{9,5},{13,1},{2,14},{6,10},... | collective-permute-start | bytes 92168 | tf_op jit(solution)/shard_map/ppermute | solution.py:54
  83.9 7.2 %collective-permute-start.11 = (f32[24,320]{1,0:T(8,128)S(1)}, f32[24,320]{1,0:T(8,128)S(1)}, u32[]{:S(2)}, u32[]{:S(2)}) collective-permute-start(f32[24,320]{1,0:T(8,128)S(1)} %get-tuple-element.125), channel_id=1, source_target_pairs={{0,8},{4,12},{8,0},{12,4},{1,9},{5,13},{9,1},{13,5},{2,10},{6,14},... | collective-permute-start | bytes 92168 | tf_op jit(solution)/shard_map/ppermute | solution.py:54
  86.6 4.7 %collective-permute-start.10 = (f32[24,320]{1,0:T(8,128)S(1)}, f32[24,320]{1,0:T(8,128)S(1)}, u32[]{:S(2)}, u32[]{:S(2)}) collective-permute-start(f32[24,320]{1,0:T(8,128)S(1)} %get-tuple-element.123), channel_id=1, source_target_pairs={{0,4},{4,0},{8,12},{12,8},{1,5},{5,1},{9,13},{13,9},{2,6},{6,2},{1... | collective-permute-start | bytes 92168 | tf_op jit(solution)/shard_map/ppermute | solution.py:54
  91.5 11.9 %collective-permute-start.13 = (f32[96,432]{1,0:T(8,128)S(1)}, f32[96,432]{1,0:T(8,128)S(1)}, u32[]{:S(2)}, u32[]{:S(2)}) collective-permute-start(f32[96,432]{1,0:T(8,128)S(1)} %convert_reduce_fusion), channel_id=1, source_target_pairs={{0,32},{32,0},{1,33},{33,1},{2,34},{34,2},{3,35},{35,3},{4,36},{36... | collective-permute-start | bytes 497672 | tf_op jit(solution)/shard_map/ppermute | solution.py:29
  104.5 34.6 %all-to-all-start.2 = ((bf16[8,96,432]{2,1,0:T(8,128)(2,1)}), bf16[8,96,432]{2,1,0:T(8,128)(2,1)S(1)}, u32[]{:S(2)}, u32[]{:S(2)}) async-start(bf16[8,96,432]{2,1,0:T(8,128)(2,1)} %broadcast_in_dim.42), calls=%async_computation.2 | async-start | bytes 1572864 | tf_op jit(solution)/shard_map/all_to_all | solution.py:23
  110.4 27.2 %collective-permute-start.15 = (f32[160,432]{1,0:T(8,128)S(1)}, f32[160,432]{1,0:T(8,128)S(1)}, u32[]{:S(2)}, u32[]{:S(2)}) collective-permute-start(f32[160,432]{1,0:T(8,128)S(1)} %slice_select_fusion.1), channel_id=1, source_target_pairs={{0,16},{16,0},{1,17},{17,1},{2,18},{18,2},{3,19},{19,3},{4,20},{20... | collective-permute-start | bytes 829448 | tf_op jit(solution)/shard_map/ppermute | solution.py:29
  134.1 4.7 %collective-permute-start.14 = (bf16[384,320]{1,0:T(8,128)(2,1)S(1)}, bf16[384,320]{1,0:T(8,128)(2,1)S(1)}, u32[]{:S(2)}, u32[]{:S(2)}) collective-permute-start(bf16[384,320]{1,0:T(8,128)(2,1)S(1)} %all_gather.7), channel_id=1, source_target_pairs={{0,16},{16,0},{1,17},{17,1},{2,18},{18,2},{3,19},{19,3},{4,20},{20... | collective-permute-start | bytes 737288 | tf_op jit(solution)/shard_map/ppermute | solution.py:29
  (2 other events, 8.6 us)

commit v4 on v3

--- a/solution.py
+++ b/solution.py
@@ -55,6 +55,13 @@
     return total
 
 
+def summed(x, axis):
+    one, two, three = (
+        lax.ppermute(x, axis, [(i, i ^ bit) for i in range(4)]) for bit in (1, 2, 3)
+    )
+    return (x + one) + (two + three)
+
+
 def body(grad_out, acts, basis_out, basis_in, eigvals, counts):
     core = lax.axis_index("core")
     second = core == 1
@@ -69,44 +76,40 @@
     b_in = jnp.concatenate(ordered(basis_in, b_other, second), axis=1)
     act = doubled(act, "y", 1)
     act = doubled(act, "y", 2)
-    grads, w_other, act = tie(grads, w_other, act)
+    grads, w_other, b_in, act = tie(grads, w_other, b_in, act)
 
     g_other = swap(grads, "core")
-    act = doubled(act, "y", 4)
-    partial = jnp.dot(grads, w_mine, preferred_element_type=f32) + jnp.dot(
-        g_other, w_other, preferred_element_type=f32
-    )
-    partial, act, b_in = tie(partial.astype(bf16), act, b_in)
+    partial = jnp.dot(grads, w_mine, preferred_element_type=f32)
+    g_other, partial = tie(g_other, partial)
+    partial = partial + jnp.dot(g_other, w_other, preferred_element_type=f32)
+    partial, act = tie(partial.astype(bf16), act)
 
     rows = NTOK // 8
     pieces = lax.all_to_all(
         partial.reshape(8, rows, -1), "y", 0, 0, tiled=True
     )
+    act = doubled(act, "y", 4)
     part_act = jnp.dot(act, b_in, preferred_element_type=f32)
-    part_act = part_act.reshape(4, 4, 24, -1)
-    part_act = scattered(part_act, "x", 1)
-    act_piece = scattered(part_act, "zl", 0).astype(bf16)
-    pieces, act_piece = tie(pieces, act_piece)
-
-    piece = jnp.sum(pieces.astype(f32), axis=0)
-    piece_other = swap(piece, "zh")
-    act_x = lax.all_gather(act_piece, "x", axis=0, tiled=True)
-    slots = lax.axis_index("y") * rows + jnp.arange(rows, dtype=jnp.int32)
-    used = slots % TOKX < jnp.take(counts, slots // TOKX)
-    piece = ((piece + piece_other) * used.astype(f32)[:, None]).astype(bf16)
-    piece, act_x = tie(piece, act_x)
-
-    rot_grad = spread(piece, "y", 8).reshape(NTOK, -1)
-    act_half = lax.all_gather(act_x, "zl", axis=0, tiled=True)
-    act_other = swap(act_half, "core")
-    rot_act = jnp.stack(
-        ordered(act_half.reshape(16, 24, -1), act_other.reshape(16, 24, -1), second),
-        axis=1,
-    ).reshape(NTOK, -1)
+    part_act = scattered(part_act.reshape(4, 4, 24, -1), "x", 1)
     eig_t = eigvals.T
     e_lo, e_hi = eig_t[:, :half], eig_t[:, half:]
     e_mine = jnp.where(second, e_hi, e_lo)
     e_other = swap(jnp.where(second, e_lo, e_hi), "core")
+    slots = lax.axis_index("y") * rows + jnp.arange(rows, dtype=jnp.int32)
+    used = slots % TOKX < jnp.take(counts, slots // TOKX)
+    used = used.astype(f32)[:, None]
+    pieces, part_act, used, e_other = tie(pieces, part_act, used, e_other)
+
+    piece = jnp.sum(pieces.astype(f32), axis=0)
+    piece_other = swap(piece, "zh")
+    act_piece = summed(part_act, "zl").astype(bf16)
+    piece = ((piece + piece_other) * used).astype(bf16)
+
+    rot_grad = spread(piece, "y", 8).reshape(NTOK, -1)
+    act_half = lax.all_gather(act_piece, "x", axis=0)
+    act_half = jnp.swapaxes(act_half, 0, 1).reshape(16, 24, -1)
+    act_other = swap(act_half, "core")
+    rot_act = jnp.stack(ordered(act_half, act_other, second), axis=1).reshape(NTOK, -1)
     recip = 1.0 / jnp.concatenate(ordered(e_mine, e_other, second), axis=0)
 
     cols_grad = rot_grad.shape[1]

time: 194 us -> 177 us (0.912)
  blocking collectives: 61 us -> 41.6 us
  starting transfers between devices: 92.8 us -> 78.6 us
  waiting for transfers between devices: 13.1 us -> 27.3 us
    all_gather x2 -> x1, blocking collectives: 23.1 us -> 10.7 us  [body(): act_half = lax.all_gather(act_piece, 'x', axis=0)]
    ppermute x0 -> x3, starting transfers between devices: none -> 10 us  [summed(): lax.ppermute(x, axis, [(i, i ^ bit) for i in range(4)])]
    ppermute x6 -> x3, starting transfers between devices: 18.3 us -> 9.58 us  [scattered(): total = total + lax.ppermute(block, axis, [(i, i ^ bit) for i in range(4)])]
    ppermute x6, starting transfers between devices: 26.7 us -> 18.6 us  [swap(): return lax.ppermute(x, axis, SWAP)]
    ppermute x0 -> x3, waiting for transfers between devices: none -> 7.71 us  [summed(): lax.ppermute(x, axis, [(i, i ^ bit) for i in range(4)])]
    all_to_all x1, waiting for transfers between devices: 0.01 us -> 7.67 us  [body(): pieces = lax.all_to_all(partial.reshape(8, rows, -1), 'y', 0, 0, tiled=True)]
    all_to_all x2, blocking collectives: 37.8 us -> 30.9 us  [spread(): lax.all_to_all(jnp.broadcast_to(x[None], (n,) + x.shape), axes, 0, 0, til...]
    all_to_all x1, starting transfers between devices: 8.69 us -> 3.55 us  [body(): pieces = lax.all_to_all(partial.reshape(8, rows, -1), 'y', 0, 0, tiled=True)]
  transfers between devices with their start and end apart: 19 -> 19, of which waited for: 8 -> 7; matrix products, arithmetic and copies ran while one was open for 3% -> 6% of each run, Pallas kernels for 0% -> 0%
where the time goes in v4:
time: 177 us; the launch traced here: 176 us
  starting transfers between devices  78.6 us (44%)
  blocking collectives  41.6 us (24%)
  waiting for transfers between devices  27.3 us (15%)
  matrix products  12.7 us (7%)
  local copies, waits for them, and re-layouts  9.58 us (5%)
  other arithmetic  5.18 us (3%)
    all_to_all x2, blocking collectives, spread(): lax.all_to_all(jnp.broadcast_to(x[None], (n,) + x.shape), axes, 0, 0, til...  30.9 us
    ppermute x4, starting transfers between devices, doubled(): other = lax.ppermute(x, axis, [(i, i ^ bit) for i in range(n)])  26.5 us
    ppermute x6, starting transfers between devices, swap(): return lax.ppermute(x, axis, SWAP)  18.6 us
    dot_general x16, matrix products, one_query(): projected = jnp.dot(train_act, precond, preferred_element_type=f32)  11 us
    all_gather x1, blocking collectives, body(): act_half = lax.all_gather(act_piece, 'x', axis=0)  10.7 us
    all_to_all x2, starting transfers between devices, spread(): lax.all_to_all(jnp.broadcast_to(x[None], (n,) + x.shape), axes, 0, 0, til...  10.4 us
    ppermute x3, starting transfers between devices, summed(): lax.ppermute(x, axis, [(i, i ^ bit) for i in range(4)])  10 us
    ppermute x3, starting transfers between devices, scattered(): total = total + lax.ppermute(block, axis, [(i, i ^ bit) for i in range(4)])  9.58 us
  transfers between devices with their start and end apart: 19, of which 7 were waited for; matrix products, arithmetic and copies ran while one was open for 6% of the time, Pallas kernels for 0%

profile of v4, /device:TPU:1, one launch (start us, length us, event | category | flops | bytes accessed | tf_op | source)
XLA Modules:
  0.0 176.0 jit_solution(7387280591329774701)
XLA Ops:
  0.0 11.6 %collective-permute-start.2 = (bf16[24,320]{1,0:T(8,128)(2,1)}, bf16[24,320]{1,0:T(8,128)(2,1)S(1)}, u32[]{:S(2)}, u32[]{:S(2)}) collective-permute-start(bf16[24,320]{1,0:T(8,128)(2,1)} %param.9), channel_id=1, source_target_pairs={{0,32},{32,0},{1,33},{33,1},{2,34},{34,2},{3,35},{35,3},{4,36},{36... | collective-permute-start | bytes 46088 | tf_op jit(solution)/shard_map/ppermute | solution.py:44
  11.6 2.9 %collective-permute-start.1 = (bf16[320,160]{0,1:T(8,128)(2,1)}, bf16[320,160]{0,1:T(8,128)(2,1)S(1)}, u32[]{:S(2)}, u32[]{:S(2)}) collective-permute-start(bf16[320,160]{0,1:T(8,128)(2,1)} %param.11), channel_id=1, source_target_pairs={{0,16},{16,0},{1,17},{17,1},{2,18},{18,2},{3,19},{19,3},{4,20},{20... | collective-permute-start | bytes 307208 | tf_op jit(solution)/shard_map/ppermute | solution.py:29
  16.3 6.9 %all-to-all-start = ((bf16[16,48,432]{2,1,0:T(8,128)(2,1)}), bf16[16,48,432]{2,1,0:T(8,128)(2,1)S(1)}, u32[]{:S(2)}, u32[]{:S(2)}) async-start(bf16[16,48,432]{2,1,0:T(8,128)(2,1)} %broadcast_in_dim.40), calls=%async_computation | async-start | bytes 1572864 | tf_op jit(solution)/shard_map/all_to_all | solution.py:23
  23.2 3.2 %collective-permute-start.3 = (bf16[48,320]{1,0:T(8,128)(2,1)S(1)}, bf16[48,320]{1,0:T(8,128)(2,1)S(1)}, u32[]{:S(2)}, u32[]{:S(2)}) collective-permute-start(bf16[48,320]{1,0:T(8,128)(2,1)S(1)} %pad_maximum_fusion.4), channel_id=1, source_target_pairs={{0,64},{64,0},{128,192},{192,128},{256,320},{320,256},{384,448},{4... | collective-permute-start | bytes 92168 | tf_op jit(solution)/shard_map/ppermute | solution.py:44
  29.9 4.2 %collective-permute-start.4 = (bf16[96,320]{1,0:T(8,128)(2,1)S(1)}, bf16[96,320]{1,0:T(8,128)(2,1)S(1)}, u32[]{:S(2)}, u32[]{:S(2)}) collective-permute-start(bf16[96,320]{1,0:T(8,128)(2,1)S(1)} %pad_maximum_fusion.3), channel_id=1, source_target_pairs={{0,128},{64,192},{128,0},{192,64},{256,384},{320,448},{384,256},{4... | collective-permute-start | bytes 184328 | tf_op jit(solution)/shard_map/ppermute | solution.py:44
  34.3 4.2 %collective-permute-done.4 = bf16[96,320]{1,0:T(8,128)(2,1)S(1)} collective-permute-done((bf16[96,320]{1,0:T(8,128)(2,1)S(1)}, bf16[96,320]{1,0:T(8,128)(2,1)S(1)}, u32[]{:S(2)}, u32[]{:S(2)}) %collective-permute-start.4) | collective-permute-done | bytes 61472 | tf_op jit(solution)/shard_map/ppermute | solution.py:44
  38.5 3.4 %all-to-all-done = bf16[16,48,432]{2,1,0:T(8,128)(2,1)S(1)} async-done(((bf16[16,48,432]{2,1,0:T(8,128)(2,1)}), bf16[16,48,432]{2,1,0:T(8,128)(2,1)S(1)}, u32[]{:S(2)}, u32[]{:S(2)}) %all-to-all-start) | async-done | bytes 663584 | tf_op jit(solution)/shard_map/all_to_all | solution.py:23
  43.0 3.8 %collective-permute-start.5 = (bf16[768,432]{0,1:T(8,128)(2,1)}, bf16[768,432]{0,1:T(8,128)(2,1)S(1)}, u32[]{:S(2)}, u32[]{:S(2)}) collective-permute-start(bf16[768,432]{0,1:T(8,128)(2,1)} %copy.39), channel_id=1, source_target_pairs={{0,16},{16,0},{1,17},{17,1},{2,18},{18,2},{3,19},{19,3},{4,20},{20... | collective-permute-start | bytes 1990664 | tf_op jit(solution)/shard_map/ppermute | solution.py:29
  50.7 7.5 %collective-permute-start.6 = (bf16[192,320]{1,0:T(8,128)(2,1)S(1)}, bf16[192,320]{1,0:T(8,128)(2,1)S(1)}, u32[]{:S(2)}, u32[]{:S(2)}) collective-permute-start(bf16[192,320]{1,0:T(8,128)(2,1)S(1)} %pad_maximum_fusion.2), channel_id=1, source_target_pairs={{0,256},{64,320},{128,384},{192,448},{256,0},{320,64},{384,128},{4... | collective-permute-start | bytes 368648 | tf_op jit(solution)/shard_map/ppermute | solution.py:44
  59.4 3.5 %all-to-all-start.1 = ((bf16[8,96,432]{2,1,0:T(8,128)(2,1)}), bf16[8,96,432]{2,1,0:T(8,128)(2,1)S(1)}, u32[]{:S(2)}, u32[]{:S(2)}) async-start(bf16[8,96,432]{2,1,0:T(8,128)(2,1)} %bitcast.5), calls=%async_computation.1 | async-start | bytes 1572864 | tf_op jit(solution)/shard_map/all_to_all | solution.py:88
  66.7 4.5 %collective-permute-start.8 = (f32[4,24,320]{2,1,0:T(8,128)S(1)}, f32[4,24,320]{2,1,0:T(8,128)S(1)}, u32[]{:S(2)}, u32[]{:S(2)}) collective-permute-start(f32[4,24,320]{2,1,0:T(8,128)S(1)} %get-tuple-element.136), channel_id=1, source_target_pairs={{0,2},{1,3},{2,0},{3,1},{4,6},{5,7},{6,4},{7,5},{8,10},{9,11},{10,... | collective-permute-start | bytes 368648 | tf_op jit(solution)/shard_map/ppermute | solution.py:54
  71.3 3.0 %collective-permute-start.9 = (f32[4,24,320]{2,1,0:T(8,128)S(1)}, f32[4,24,320]{2,1,0:T(8,128)S(1)}, u32[]{:S(2)}, u32[]{:S(2)}) collective-permute-start(f32[4,24,320]{2,1,0:T(8,128)S(1)} %get-tuple-element.135), channel_id=1, source_target_pairs={{0,3},{1,2},{2,1},{3,0},{4,7},{5,6},{6,5},{7,4},{8,11},{9,10},{10,... | collective-permute-start | bytes 368648 | tf_op jit(solution)/shard_map/ppermute | solution.py:54
  76.0 2.7 %collective-permute-done.9 = f32[4,24,320]{2,1,0:T(8,128)S(1)} collective-permute-done((f32[4,24,320]{2,1,0:T(8,128)S(1)}, f32[4,24,320]{2,1,0:T(8,128)S(1)}, u32[]{:S(2)}, u32[]{:S(2)}) %collective-permute-start.9) | collective-permute-done | bytes 122912 | tf_op jit(solution)/shard_map/ppermute | solution.py:54
  78.7 7.7 %all-to-all-done.1 = bf16[8,96,432]{2,1,0:T(8,128)(2,1)S(1)} async-done(((bf16[8,96,432]{2,1,0:T(8,128)(2,1)}), bf16[8,96,432]{2,1,0:T(8,128)(2,1)S(1)}, u32[]{:S(2)}, u32[]{:S(2)}) %all-to-all-start.1) | async-done | bytes 663584 | tf_op jit(solution)/shard_map/all_to_all | solution.py:88
  88.4 4.1 %collective-permute-start.11 = (f32[4,24,320]{2,1,0:T(8,128)S(1)}, f32[4,24,320]{2,1,0:T(8,128)S(1)}, u32[]{:S(2)}, u32[]{:S(2)}) collective-permute-start(f32[4,24,320]{2,1,0:T(8,128)S(1)} %fusion.23), channel_id=1, source_target_pairs={{0,4},{4,0},{8,12},{12,8},{1,5},{5,1},{9,13},{13,9},{2,6},{6,2},{1... | collective-permute-start | bytes 368648 | tf_op jit(solution)/shard_map/ppermute | solution.py:60
  92.6 2.7 %collective-permute-start.12 = (f32[4,24,320]{2,1,0:T(8,128)S(1)}, f32[4,24,320]{2,1,0:T(8,128)S(1)}, u32[]{:S(2)}, u32[]{:S(2)}) collective-permute-start(f32[4,24,320]{2,1,0:T(8,128)S(1)} %fusion.23), channel_id=1, source_target_pairs={{0,8},{4,12},{8,0},{12,4},{1,9},{5,13},{9,1},{13,5},{2,10},{6,14},... | collective-permute-start | bytes 368648 | tf_op jit(solution)/shard_map/ppermute | solution.py:60
  95.2 3.2 %collective-permute-start.13 = (f32[4,24,320]{2,1,0:T(8,128)S(1)}, f32[4,24,320]{2,1,0:T(8,128)S(1)}, u32[]{:S(2)}, u32[]{:S(2)}) collective-permute-start(f32[4,24,320]{2,1,0:T(8,128)S(1)} %fusion.23), channel_id=1, source_target_pairs={{0,12},{4,8},{8,4},{12,0},{1,13},{5,9},{9,5},{13,1},{2,14},{6,10},... | collective-permute-start | bytes 368648 | tf_op jit(solution)/shard_map/ppermute | solution.py:60
  99.5 3.5 %all-to-all-start.2 = ((bf16[8,96,432]{2,1,0:T(8,128)(2,1)}), bf16[8,96,432]{2,1,0:T(8,128)(2,1)S(1)}, u32[]{:S(2)}, u32[]{:S(2)}) async-start(bf16[8,96,432]{2,1,0:T(8,128)(2,1)} %broadcast_in_dim.42), calls=%async_computation.2 | async-start | bytes 1572864 | tf_op jit(solution)/shard_map/all_to_all | solution.py:23
  104.5 6.3 %collective-permute-done.12 = f32[4,24,320]{2,1,0:T(8,128)S(1)} collective-permute-done((f32[4,24,320]{2,1,0:T(8,128)S(1)}, f32[4,24,320]{2,1,0:T(8,128)S(1)}, u32[]{:S(2)}, u32[]{:S(2)}) %collective-permute-start.12) | collective-permute-done | bytes 122912 | tf_op jit(solution)/shard_map/ppermute | solution.py:60
  110.8 10.7 %all-gather = bf16[16,24,320]{2,1,0:T(8,128)(2,1)S(1)} all-gather(bf16[4,24,320]{2,1,0:T(8,128)(2,1)S(1)} %add_convert_fusion.1), channel_id=2, replica_groups=mesh['y'=8,'zh'=2,'core'=2,'zl'=4,'x'=4] {'x'}, dimensions={0}, use_global_device_ids=true | all-gather | bytes 307200 | tf_op jit(solution)/shard_map/all_gather | solution.py:109
  121.6 5.6 %collective-permute-start.14 = (bf16[16,24,320]{2,1,0:T(8,128)(2,1)S(1)}, bf16[16,24,320]{2,1,0:T(8,128)(2,1)S(1)}, u32[]{:S(2)}, u32[]{:S(2)}) collective-permute-start(bf16[16,24,320]{2,1,0:T(8,128)(2,1)S(1)} %bitcast.76), channel_id=1, source_target_pairs={{0,16},{16,0},{1,17},{17,1},{2,18},{18,2},{3,19},{19,3},{4,20},{20... | collective-permute-start | bytes 737288 | tf_op jit(solution)/shard_map/ppermute | solution.py:29
  129.1 15.1 %while.10 = (s32[]{:T(128)}, f32[16,32]{1,0:T(8,128)S(1)}, bf16[16,16,320]{2,1,0:T(8,128)(2,1)S(1)}, bf16[16,16,432]{2,1,0:T(8,128)(2,1)S(1)}, f32[320,432]{1,0:...) while((s32[]{:T(128)}, f32[16,32]{1,0:T(8,128)S(1)}, ...), condition=%wide.region_4.5_spmd, body=%wide.region_1.4_spmd.sunk | while | flops 146921440 | bytes 1529325 | solution.py:131
  144.3 16.7 %all_to_all.25 = f32[32,4,128]{2,1,0:T(4,128)S(1)} all-to-all(f32[32,4,128]{2,1,0:T(4,128)S(1)} %broadcast_in_dim.44), channel_id=1, replica_groups=mesh['y'=8,'zh'=2,'core'=2,'zl'=4,'x'=4] {'core','zl','x'}, dimensions={0} | all-to-all | bytes 131072 | tf_op jit(solution)/shard_map/all_to_all | solution.py:23
  161.1 14.2 %all_to_all.26 = f32[16,4,128]{2,1,0:T(4,128)S(1)} all-to-all(f32[16,4,128]{2,1,0:T(4,128)S(1)} %broadcast_in_dim.45), channel_id=1, replica_groups=mesh['y'=8,'zh'=2,'core'=2,'zl'=4,'x'=4] {'y','zh'}, dimensions={0} | all-to-all | bytes 65536 | tf_op jit(solution)/shard_map/all_to_all | solution.py:23
  (143 shorter events, 39.1 us)
Async XLA Ops:
  0.0 62.9 %copy-start = (s32[48]{0:T(128)S(1)}, s32[48]{0:T(128)}, u32[]{:S(2)}) copy-start(s32[48]{0:T(128)} %param.13) | copy-start | bytes 580
  0.0 23.1 %copy-start.6 = (bf16[24,320]{1,0:T(8,128)(2,1)S(1)}, bf16[24,320]{1,0:T(8,128)(2,1)}, u32[]{:S(2)}) copy-start(bf16[24,320]{1,0:T(8,128)(2,1)} %param.9) | copy-start | bytes 46084
  0.0 26.4 %copy-start.2 = (bf16[432,864]{1,0:T(8,128)(2,1)S(1)}, bf16[432,864]{1,0:T(8,128)(2,1)}, u32[]{:S(2)}) copy-start(bf16[432,864]{1,0:T(8,128)(2,1)} %param.10) | copy-start | bytes 2239492
  0.0 23.1 %collective-permute-start.2 = (bf16[24,320]{1,0:T(8,128)(2,1)}, bf16[24,320]{1,0:T(8,128)(2,1)S(1)}, u32[]{:S(2)}, u32[]{:S(2)}) collective-permute-start(bf16[24,320]{1,0:T(8,128)(2,1)} %param.9), channel_id=1, source_target_pairs={{0,32},{32,0},{1,33},{33,1},{2,34},{34,2},{3,35},{35,3},{4,36},{36... | collective-permute-start | bytes 46088 | tf_op jit(solution)/shard_map/ppermute | solution.py:44
  11.6 22.6 %collective-permute-start.1 = (bf16[320,160]{0,1:T(8,128)(2,1)}, bf16[320,160]{0,1:T(8,128)(2,1)S(1)}, u32[]{:S(2)}, u32[]{:S(2)}) collective-permute-start(bf16[320,160]{0,1:T(8,128)(2,1)} %param.11), channel_id=1, source_target_pairs={{0,16},{16,0},{1,17},{17,1},{2,18},{18,2},{3,19},{19,3},{4,20},{20... | collective-permute-start | bytes 307208 | tf_op jit(solution)/shard_map/ppermute | solution.py:29
  16.3 25.6 %all-to-all-start = ((bf16[16,48,432]{2,1,0:T(8,128)(2,1)}), bf16[16,48,432]{2,1,0:T(8,128)(2,1)S(1)}, u32[]{:S(2)}, u32[]{:S(2)}) async-start(bf16[16,48,432]{2,1,0:T(8,128)(2,1)} %broadcast_in_dim.40), calls=%async_computation | async-start | bytes 1572864 | tf_op jit(solution)/shard_map/all_to_all | solution.py:23
  23.1 11.1 %copy-start.5 = (bf16[320,160]{0,1:T(8,128)(2,1)S(1)}, bf16[320,160]{0,1:T(8,128)(2,1)}, u32[]{:S(2)}) copy-start(bf16[320,160]{0,1:T(8,128)(2,1)} %param.11) | copy-start | bytes 307204
  23.2 6.7 %collective-permute-start.3 = (bf16[48,320]{1,0:T(8,128)(2,1)S(1)}, bf16[48,320]{1,0:T(8,128)(2,1)S(1)}, u32[]{:S(2)}, u32[]{:S(2)}) collective-permute-start(bf16[48,320]{1,0:T(8,128)(2,1)S(1)} %pad_maximum_fusion.4), channel_id=1, source_target_pairs={{0,64},{64,0},{128,192},{192,128},{256,320},{320,256},{384,448},{4... | collective-permute-start | bytes 92168 | tf_op jit(solution)/shard_map/ppermute | solution.py:44
  27.4 11.1 %collective-permute-start = (bf16[432,432]{1,0:T(8,128)(2,1)}, bf16[432,432]{1,0:T(8,128)(2,1)S(1)}, u32[]{:S(2)}, u32[]{:S(2)}) collective-permute-start(bf16[432,432]{1,0:T(8,128)(2,1)} %broadcast_select_fusion), channel_id=1, source_target_pairs={{0,16},{16,0},{1,17},{17,1},{2,18},{18,2},{3,19},{19,3},{4,20},{20... | collective-permute-start | bytes 1119752 | tf_op jit(solution)/shard_map/ppermute | solution.py:29
  29.9 8.5 %collective-permute-start.4 = (bf16[96,320]{1,0:T(8,128)(2,1)S(1)}, bf16[96,320]{1,0:T(8,128)(2,1)S(1)}, u32[]{:S(2)}, u32[]{:S(2)}) collective-permute-start(bf16[96,320]{1,0:T(8,128)(2,1)S(1)} %pad_maximum_fusion.3), channel_id=1, source_target_pairs={{0,128},{64,192},{128,0},{192,64},{256,384},{320,448},{384,256},{4... | collective-permute-start | bytes 184328 | tf_op jit(solution)/shard_map/ppermute | solution.py:44
  34.2 12.6 %copy-start.1 = (f32[864,160]{0,1:T(8,128)S(1)}, f32[864,160]{0,1:T(8,128)}, u32[]{:S(2)}) copy-start(f32[864,160]{0,1:T(8,128)} %param.12) | copy-start | bytes 1658884
  43.0 6.7 %collective-permute-start.5 = (bf16[768,432]{0,1:T(8,128)(2,1)}, bf16[768,432]{0,1:T(8,128)(2,1)S(1)}, u32[]{:S(2)}, u32[]{:S(2)}) collective-permute-start(bf16[768,432]{0,1:T(8,128)(2,1)} %copy.39), channel_id=1, source_target_pairs={{0,16},{16,0},{1,17},{17,1},{2,18},{18,2},{3,19},{19,3},{4,20},{20... | collective-permute-start | bytes 1990664 | tf_op jit(solution)/shard_map/ppermute | solution.py:29
  47.0 31.7 %collective-permute-start.10 = (f32[160,432]{1,0:T(8,128)S(1)}, f32[160,432]{1,0:T(8,128)}, u32[]{:S(2)}, u32[]{:S(2)}) collective-permute-start(f32[160,432]{1,0:T(8,128)S(1)} %slice_select_fusion.1), channel_id=1, source_target_pairs={{0,16},{16,0},{1,17},{17,1},{2,18},{18,2},{3,19},{19,3},{4,20},{20... | collective-permute-start | bytes 829448 | tf_op jit(solution)/shard_map/ppermute | solution.py:29
  50.7 13.5 %collective-permute-start.6 = (bf16[192,320]{1,0:T(8,128)(2,1)S(1)}, bf16[192,320]{1,0:T(8,128)(2,1)S(1)}, u32[]{:S(2)}, u32[]{:S(2)}) collective-permute-start(bf16[192,320]{1,0:T(8,128)(2,1)S(1)} %pad_maximum_fusion.2), channel_id=1, source_target_pairs={{0,256},{64,320},{128,384},{192,448},{256,0},{320,64},{384,128},{4... | collective-permute-start | bytes 368648 | tf_op jit(solution)/shard_map/ppermute | solution.py:44
  59.4 27.0 %all-to-all-start.1 = ((bf16[8,96,432]{2,1,0:T(8,128)(2,1)}), bf16[8,96,432]{2,1,0:T(8,128)(2,1)S(1)}, u32[]{:S(2)}, u32[]{:S(2)}) async-start(bf16[8,96,432]{2,1,0:T(8,128)(2,1)} %bitcast.5), calls=%async_computation.1 | async-start | bytes 1572864 | tf_op jit(solution)/shard_map/all_to_all | solution.py:88
  64.6 9.6 %collective-permute-start.7 = (f32[4,24,320]{2,1,0:T(8,128)S(1)}, f32[4,24,320]{2,1,0:T(8,128)S(1)}, u32[]{:S(2)}, u32[]{:S(2)}) collective-permute-start(f32[4,24,320]{2,1,0:T(8,128)S(1)} %get-tuple-element.134), channel_id=1, source_target_pairs={{0,1},{1,0},{2,3},{3,2},{4,5},{5,4},{6,7},{7,6},{8,9},{9,8},{10,11... | collective-permute-start | bytes 368648 | tf_op jit(solution)/shard_map/ppermute | solution.py:54
  66.7 9.3 %collective-permute-start.8 = (f32[4,24,320]{2,1,0:T(8,128)S(1)}, f32[4,24,320]{2,1,0:T(8,128)S(1)}, u32[]{:S(2)}, u32[]{:S(2)}) collective-permute-start(f32[4,24,320]{2,1,0:T(8,128)S(1)} %get-tuple-element.136), channel_id=1, source_target_pairs={{0,2},{1,3},{2,0},{3,1},{4,6},{5,7},{6,4},{7,5},{8,10},{9,11},{10,... | collective-permute-start | bytes 368648 | tf_op jit(solution)/shard_map/ppermute | solution.py:54
  71.3 7.4 %collective-permute-start.9 = (f32[4,24,320]{2,1,0:T(8,128)S(1)}, f32[4,24,320]{2,1,0:T(8,128)S(1)}, u32[]{:S(2)}, u32[]{:S(2)}) collective-permute-start(f32[4,24,320]{2,1,0:T(8,128)S(1)} %get-tuple-element.135), channel_id=1, source_target_pairs={{0,3},{1,2},{2,1},{3,0},{4,7},{5,6},{6,5},{7,4},{8,11},{9,10},{10,... | collective-permute-start | bytes 368648 | tf_op jit(solution)/shard_map/ppermute | solution.py:54
  86.5 12.0 %collective-permute-start.15 = (f32[96,432]{1,0:T(8,128)S(1)}, f32[96,432]{1,0:T(8,128)S(1)}, u32[]{:S(2)}, u32[]{:S(2)}) collective-permute-start(f32[96,432]{1,0:T(8,128)S(1)} %convert_reduce_fusion), channel_id=1, source_target_pairs={{0,32},{32,0},{1,33},{33,1},{2,34},{34,2},{3,35},{35,3},{4,36},{36... | collective-permute-start | bytes 497672 | tf_op jit(solution)/shard_map/ppermute | solution.py:29
  88.4 16.1 %collective-permute-start.11 = (f32[4,24,320]{2,1,0:T(8,128)S(1)}, f32[4,24,320]{2,1,0:T(8,128)S(1)}, u32[]{:S(2)}, u32[]{:S(2)}) collective-permute-start(f32[4,24,320]{2,1,0:T(8,128)S(1)} %fusion.23), channel_id=1, source_target_pairs={{0,4},{4,0},{8,12},{12,8},{1,5},{5,1},{9,13},{13,9},{2,6},{6,2},{1... | collective-permute-start | bytes 368648 | tf_op jit(solution)/shard_map/ppermute | solution.py:60
  92.6 18.3 %collective-permute-start.12 = (f32[4,24,320]{2,1,0:T(8,128)S(1)}, f32[4,24,320]{2,1,0:T(8,128)S(1)}, u32[]{:S(2)}, u32[]{:S(2)}) collective-permute-start(f32[4,24,320]{2,1,0:T(8,128)S(1)} %fusion.23), channel_id=1, source_target_pairs={{0,8},{4,12},{8,0},{12,4},{1,9},{5,13},{9,1},{13,5},{2,10},{6,14},... | collective-permute-start | bytes 368648 | tf_op jit(solution)/shard_map/ppermute | solution.py:60
  95.2 15.6 %collective-permute-start.13 = (f32[4,24,320]{2,1,0:T(8,128)S(1)}, f32[4,24,320]{2,1,0:T(8,128)S(1)}, u32[]{:S(2)}, u32[]{:S(2)}) collective-permute-start(f32[4,24,320]{2,1,0:T(8,128)S(1)} %fusion.23), channel_id=1, source_target_pairs={{0,12},{4,8},{8,4},{12,0},{1,13},{5,9},{9,5},{13,1},{2,14},{6,10},... | collective-permute-start | bytes 368648 | tf_op jit(solution)/shard_map/ppermute | solution.py:60
  99.5 29.3 %all-to-all-start.2 = ((bf16[8,96,432]{2,1,0:T(8,128)(2,1)}), bf16[8,96,432]{2,1,0:T(8,128)(2,1)S(1)}, u32[]{:S(2)}, u32[]{:S(2)}) async-start(bf16[8,96,432]{2,1,0:T(8,128)(2,1)} %broadcast_in_dim.42), calls=%async_computation.2 | async-start | bytes 1572864 | tf_op jit(solution)/shard_map/all_to_all | solution.py:23
  121.6 6.9 %collective-permute-start.14 = (bf16[16,24,320]{2,1,0:T(8,128)(2,1)S(1)}, bf16[16,24,320]{2,1,0:T(8,128)(2,1)S(1)}, u32[]{:S(2)}, u32[]{:S(2)}) collective-permute-start(bf16[16,24,320]{2,1,0:T(8,128)(2,1)S(1)} %bitcast.76), channel_id=1, source_target_pairs={{0,16},{16,0},{1,17},{17,1},{2,18},{18,2},{3,19},{19,3},{4,20},{20... | collective-permute-start | bytes 737288 | tf_op jit(solution)/shard_map/ppermute | solution.py:29
  (2 other events, 4.4 us)

commit v5 on v4

--- a/solution.py
+++ b/solution.py
@@ -1,6 +1,8 @@
 import jax
 import jax.numpy as jnp
 from jax import lax
+from jax.experimental import pallas as pl
+from jax.experimental.pallas import tpu as pltpu
 from jax.sharding import Mesh, PartitionSpec as P
 
 D = 5120
@@ -62,6 +64,61 @@
     return (x + one) + (two + three)
 
 
+def score_kernel(grad_ref, act_ref, recip_ref, out_ref, grad_t, act_t, rows):
+    first = NQ * TOKX
+    grad_t[...] = grad_ref[first:, :].T
+    act_t[...] = act_ref[first:, :].astype(f32).T
+
+    def one_query(q, carry):
+        here = pl.ds(pl.multiple_of(q * TOKX, TOKX), TOKX)
+        outer = lax.dot_general(
+            act_ref[here, :],
+            grad_ref[here, :],
+            (((0,), (0,)), ((), ())),
+            preferred_element_type=f32,
+        )
+        precond = (outer * recip_ref[...]).astype(bf16)
+        projected = jnp.dot(precond, grad_t[...], preferred_element_type=f32)
+        rows[pl.ds(q, 1), :] = jnp.sum(projected * act_t[...], axis=0, keepdims=True)
+        return carry
+
+    lax.fori_loop(0, NQ, one_query, 0, unroll=2)
+
+    slot = lax.broadcasted_iota(jnp.int32, (NT * TOKX, 128), 0)
+    lane = lax.broadcasted_iota(jnp.int32, (NT * TOKX, 128), 1)
+    pick = (slot // TOKX == lane % NT).astype(f32)
+    sums = jnp.dot(
+        rows[...], pick, preferred_element_type=f32, precision=lax.Precision.HIGHEST
+    )
+    query = lax.broadcasted_iota(jnp.int32, (NQ, 128), 0)
+    place = lax.broadcasted_iota(jnp.int32, (NQ, 128), 1)
+    sums = jnp.where(place // NT == query % 4, sums, 0.0)
+    scale = TOKX * (float(FF) * float(D)) ** 0.5
+    out_ref[...] = jnp.sum(sums.reshape(4, 4, 128), axis=1) / scale
+
+
+def scores(rot_grad, rot_act, recip):
+    cols_act, cols_grad = recip.shape
+    vmem = pl.BlockSpec(memory_space=pltpu.VMEM)
+    return pl.pallas_call(
+        score_kernel,
+        out_shape=jax.ShapeDtypeStruct((4, 128), f32),
+        in_specs=[vmem] * 3,
+        out_specs=vmem,
+        scratch_shapes=[
+            pltpu.VMEM((cols_grad, NT * TOKX), bf16),
+            pltpu.VMEM((cols_act, NT * TOKX), f32),
+            pltpu.VMEM((NQ, NT * TOKX), f32),
+        ],
+        compiler_params=pltpu.CompilerParams(vmem_limit_bytes=40 * 1024 * 1024),
+        cost_estimate=pl.CostEstimate(
+            flops=2 * NQ * cols_act * cols_grad * (NT * TOKX + TOKX),
+            bytes_accessed=2 * NTOK * (cols_act + cols_grad) + 4 * cols_act * cols_grad,
+            transcendentals=0,
+        ),
+    )(rot_grad, rot_act, recip)
+
+
 def body(grad_out, acts, basis_out, basis_in, eigvals, counts):
     core = lax.axis_index("core")
     second = core == 1
@@ -112,25 +169,7 @@
     rot_act = jnp.stack(ordered(act_half, act_other, second), axis=1).reshape(NTOK, -1)
     recip = 1.0 / jnp.concatenate(ordered(e_mine, e_other, second), axis=0)
 
-    cols_grad = rot_grad.shape[1]
-    cols_act = rot_act.shape[1]
-    query_grad = rot_grad[: NQ * TOKX].reshape(NQ, TOKX, cols_grad)
-    query_act = rot_act[: NQ * TOKX].reshape(NQ, TOKX, cols_act)
-    train_grad = rot_grad[NQ * TOKX :]
-    train_act = rot_act[NQ * TOKX :]
-
-    def one_query(pair):
-        grad_q, act_q = pair
-        outer = lax.dot_general(
-            act_q, grad_q, (((0,), (0,)), ((), ())), preferred_element_type=f32
-        )
-        precond = (outer * recip).astype(bf16)
-        projected = jnp.dot(train_act, precond, preferred_element_type=f32)
-        return jnp.sum((projected * train_grad).reshape(NT, TOKX * cols_grad), axis=1)
-
-    raw = lax.map(one_query, (query_grad, query_act))
-    scaled = raw / (TOKX * jnp.sqrt(f32(FF) * f32(D)))
-    flat = scaled.reshape(4, 128)
+    flat = scores(rot_grad, rot_act, recip)
     flat = jnp.sum(spread(flat, ("core",) + EX, 32), axis=0)
     flat = jnp.sum(spread(flat, ("y", "zh"), 16), axis=0)
     return flat.reshape(NQ, NT)

time: 177 us -> 166 us (0.938)
  matrix products: 12.7 us -> 1.66 us
  Pallas kernels: 0 us -> 7.03 us
  waiting for transfers between devices: 27.3 us -> 23.4 us
  blocking collectives: 41.6 us -> 43.5 us
  other arithmetic: 5.18 us -> 3.33 us
    dot_general x16 -> x0, matrix products: 11 us -> none  [one_query(): projected = jnp.dot(train_act, precond, preferred_element_type=f32)]
    pallas_call x0 -> x1, Pallas kernels: none -> 7.03 us  [scores(): pl.pallas_call(score_kernel, out_shape=jax.ShapeDtypeStruct((4, 128), f32...]
    all_to_all x2, waiting for transfers between devices: 3.36 us -> 0.01 us  [spread(): lax.all_to_all(jnp.broadcast_to(x[None], (n,) + x.shape), axes, 0, 0, til...]
    all_to_all x2, blocking collectives: 30.9 us -> 33.4 us  [spread(): lax.all_to_all(jnp.broadcast_to(x[None], (n,) + x.shape), axes, 0, 0, til...]
    reduce_sum x16 -> x0, other arithmetic: 1.85 us -> none  [one_query(): jnp.sum((projected * train_grad).reshape(NT, TOKX * cols_grad), axis=1)]
  transfers between devices with their start and end apart: 19 -> 19, of which waited for: 7 -> 6; matrix products, arithmetic and copies ran while one was open for 6% -> 6% of each run, Pallas kernels for 0% -> 0%
where the time goes in v5:
time: 166 us; the launch traced here: 165 us
  starting transfers between devices  77 us (46%)
  blocking collectives  43.5 us (26%)
  waiting for transfers between devices  23.4 us (14%)
  local copies, waits for them, and re-layouts  8.08 us (5%)
  Pallas kernels  7.03 us (4%)
  other arithmetic  3.33 us (2%)
    all_to_all x2, blocking collectives, spread(): lax.all_to_all(jnp.broadcast_to(x[None], (n,) + x.shape), axes, 0, 0, til...  33.4 us
    ppermute x4, starting transfers between devices, doubled(): other = lax.ppermute(x, axis, [(i, i ^ bit) for i in range(n)])  26.5 us
    ppermute x6, starting transfers between devices, swap(): return lax.ppermute(x, axis, SWAP)  17.8 us
    all_to_all x2, starting transfers between devices, spread(): lax.all_to_all(jnp.broadcast_to(x[None], (n,) + x.shape), axes, 0, 0, til...  10.5 us
    all_gather x1, blocking collectives, body(): act_half = lax.all_gather(act_piece, 'x', axis=0)  10.2 us
    ppermute x3, starting transfers between devices, summed(): lax.ppermute(x, axis, [(i, i ^ bit) for i in range(4)])  9.67 us
    ppermute x3, starting transfers between devices, scattered(): total = total + lax.ppermute(block, axis, [(i, i ^ bit) for i in range(4)])  8.98 us
    all_to_all x1, waiting for transfers between devices, body(): pieces = lax.all_to_all(partial.reshape(8, rows, -1), 'y', 0, 0, tiled=True)  7.89 us
  transfers between devices with their start and end apart: 19, of which 6 were waited for; matrix products, arithmetic and copies ran while one was open for 6% of the time, Pallas kernels for 0%

profile of v5, /device:TPU:1, one launch (start us, length us, event | category | flops | bytes accessed | tf_op | source)
XLA Modules:
  0.0 164.6 jit_solution(13100682298236415152)
XLA Ops:
  0.0 11.6 %collective-permute-start.2 = (bf16[24,320]{1,0:T(8,128)(2,1)}, bf16[24,320]{1,0:T(8,128)(2,1)S(1)}, u32[]{:S(2)}, u32[]{:S(2)}) collective-permute-start(bf16[24,320]{1,0:T(8,128)(2,1)} %param.7), channel_id=1, source_target_pairs={{0,32},{32,0},{1,33},{33,1},{2,34},{34,2},{3,35},{35,3},{4,36},{36... | collective-permute-start | bytes 46088 | tf_op jit(solution)/shard_map/ppermute | solution.py:46
  13.4 7.0 %all-to-all-start = ((bf16[16,48,432]{2,1,0:T(8,128)(2,1)}), bf16[16,48,432]{2,1,0:T(8,128)(2,1)S(1)}, u32[]{:S(2)}, u32[]{:S(2)}) async-start(bf16[16,48,432]{2,1,0:T(8,128)(2,1)} %broadcast_in_dim.14), calls=%async_computation | async-start | bytes 1572864 | tf_op jit(solution)/shard_map/all_to_all | solution.py:25
  20.4 3.2 %collective-permute-start.3 = (bf16[48,320]{1,0:T(8,128)(2,1)S(1)}, bf16[48,320]{1,0:T(8,128)(2,1)S(1)}, u32[]{:S(2)}, u32[]{:S(2)}) collective-permute-start(bf16[48,320]{1,0:T(8,128)(2,1)S(1)} %pad_maximum_fusion.4), channel_id=1, source_target_pairs={{0,64},{64,0},{128,192},{192,128},{256,320},{320,256},{384,448},{4... | collective-permute-start | bytes 92168 | tf_op jit(solution)/shard_map/ppermute | solution.py:46
  24.6 3.4 %collective-permute-start = (bf16[432,432]{1,0:T(8,128)(2,1)}, bf16[432,432]{1,0:T(8,128)(2,1)S(1)}, u32[]{:S(2)}, u32[]{:S(2)}) collective-permute-start(bf16[432,432]{1,0:T(8,128)(2,1)} %broadcast_select_fusion), channel_id=1, source_target_pairs={{0,16},{16,0},{1,17},{17,1},{2,18},{18,2},{3,19},{19,3},{4,20},{20... | collective-permute-start | bytes 1119752 | tf_op jit(solution)/shard_map/ppermute | solution.py:31
  30.1 4.2 %collective-permute-start.4 = (bf16[96,320]{1,0:T(8,128)(2,1)S(1)}, bf16[96,320]{1,0:T(8,128)(2,1)S(1)}, u32[]{:S(2)}, u32[]{:S(2)}) collective-permute-start(bf16[96,320]{1,0:T(8,128)(2,1)S(1)} %pad_maximum_fusion.3), channel_id=1, source_target_pairs={{0,128},{64,192},{128,0},{192,64},{256,384},{320,448},{384,256},{4... | collective-permute-start | bytes 184328 | tf_op jit(solution)/shard_map/ppermute | solution.py:46
  34.4 4.1 %collective-permute-done.4 = bf16[96,320]{1,0:T(8,128)(2,1)S(1)} collective-permute-done((bf16[96,320]{1,0:T(8,128)(2,1)S(1)}, bf16[96,320]{1,0:T(8,128)(2,1)S(1)}, u32[]{:S(2)}, u32[]{:S(2)}) %collective-permute-start.4) | collective-permute-done | bytes 61472 | tf_op jit(solution)/shard_map/ppermute | solution.py:46
  40.4 4.0 %collective-permute-start.5 = (bf16[768,432]{0,1:T(8,128)(2,1)}, bf16[768,432]{0,1:T(8,128)(2,1)S(1)}, u32[]{:S(2)}, u32[]{:S(2)}) collective-permute-start(bf16[768,432]{0,1:T(8,128)(2,1)} %copy.30), channel_id=1, source_target_pairs={{0,16},{16,0},{1,17},{17,1},{2,18},{18,2},{3,19},{19,3},{4,20},{20... | collective-permute-start | bytes 1990664 | tf_op jit(solution)/shard_map/ppermute | solution.py:31
  48.3 7.5 %collective-permute-start.6 = (bf16[192,320]{1,0:T(8,128)(2,1)S(1)}, bf16[192,320]{1,0:T(8,128)(2,1)S(1)}, u32[]{:S(2)}, u32[]{:S(2)}) collective-permute-start(bf16[192,320]{1,0:T(8,128)(2,1)S(1)} %pad_maximum_fusion.2), channel_id=1, source_target_pairs={{0,256},{64,320},{128,384},{192,448},{256,0},{320,64},{384,128},{4... | collective-permute-start | bytes 368648 | tf_op jit(solution)/shard_map/ppermute | solution.py:46
  57.0 3.5 %all-to-all-start.1 = ((bf16[8,96,432]{2,1,0:T(8,128)(2,1)}), bf16[8,96,432]{2,1,0:T(8,128)(2,1)S(1)}, u32[]{:S(2)}, u32[]{:S(2)}) async-start(bf16[8,96,432]{2,1,0:T(8,128)(2,1)} %bitcast.1), calls=%async_computation.1 | async-start | bytes 1572864 | tf_op jit(solution)/shard_map/all_to_all | solution.py:145
  62.2 3.5 %collective-permute-start.9 = (f32[4,24,320]{2,1,0:T(8,128)S(1)}, f32[4,24,320]{2,1,0:T(8,128)S(1)}, u32[]{:S(2)}, u32[]{:S(2)}) collective-permute-start(f32[4,24,320]{2,1,0:T(8,128)S(1)} %get-tuple-element.34), channel_id=1, source_target_pairs={{0,3},{1,2},{2,1},{3,0},{4,7},{5,6},{6,5},{7,4},{8,11},{9,10},{10,... | collective-permute-start | bytes 368648 | tf_op jit(solution)/shard_map/ppermute | solution.py:56
  65.8 2.5 %collective-permute-start.8 = (f32[4,24,320]{2,1,0:T(8,128)S(1)}, f32[4,24,320]{2,1,0:T(8,128)S(1)}, u32[]{:S(2)}, u32[]{:S(2)}) collective-permute-start(f32[4,24,320]{2,1,0:T(8,128)S(1)} %get-tuple-element.35), channel_id=1, source_target_pairs={{0,2},{1,3},{2,0},{3,1},{4,6},{5,7},{6,4},{7,5},{8,10},{9,11},{10,... | collective-permute-start | bytes 368648 | tf_op jit(solution)/shard_map/ppermute | solution.py:56
  68.3 2.9 %collective-permute-start.7 = (f32[4,24,320]{2,1,0:T(8,128)S(1)}, f32[4,24,320]{2,1,0:T(8,128)S(1)}, u32[]{:S(2)}, u32[]{:S(2)}) collective-permute-start(f32[4,24,320]{2,1,0:T(8,128)S(1)} %get-tuple-element.33), channel_id=1, source_target_pairs={{0,1},{1,0},{2,3},{3,2},{4,5},{5,4},{6,7},{7,6},{8,9},{9,8},{10,11... | collective-permute-start | bytes 368648 | tf_op jit(solution)/shard_map/ppermute | solution.py:56
  71.3 2.2 %collective-permute-done.8 = f32[4,24,320]{2,1,0:T(8,128)S(1)} collective-permute-done((f32[4,24,320]{2,1,0:T(8,128)S(1)}, f32[4,24,320]{2,1,0:T(8,128)S(1)}, u32[]{:S(2)}, u32[]{:S(2)}) %collective-permute-start.8) | collective-permute-done | bytes 122912 | tf_op jit(solution)/shard_map/ppermute | solution.py:56
  73.5 2.6 %collective-permute-done.7 = f32[4,24,320]{2,1,0:T(8,128)S(1)} collective-permute-done((f32[4,24,320]{2,1,0:T(8,128)S(1)}, f32[4,24,320]{2,1,0:T(8,128)S(1)}, u32[]{:S(2)}, u32[]{:S(2)}) %collective-permute-start.7) | collective-permute-done | bytes 122912 | tf_op jit(solution)/shard_map/ppermute | solution.py:56
  76.1 7.9 %all-to-all-done.1 = bf16[8,96,432]{2,1,0:T(8,128)(2,1)S(1)} async-done(((bf16[8,96,432]{2,1,0:T(8,128)(2,1)}), bf16[8,96,432]{2,1,0:T(8,128)(2,1)S(1)}, u32[]{:S(2)}, u32[]{:S(2)}) %all-to-all-start.1) | async-done | bytes 663584 | tf_op jit(solution)/shard_map/all_to_all | solution.py:145
  86.0 4.5 %collective-permute-start.13 = (f32[4,24,320]{2,1,0:T(8,128)S(1)}, f32[4,24,320]{2,1,0:T(8,128)S(1)}, u32[]{:S(2)}, u32[]{:S(2)}) collective-permute-start(f32[4,24,320]{2,1,0:T(8,128)S(1)} %fusion.10), channel_id=1, source_target_pairs={{0,8},{4,12},{8,0},{12,4},{1,9},{5,13},{9,1},{13,5},{2,10},{6,14},... | collective-permute-start | bytes 368648 | tf_op jit(solution)/shard_map/ppermute | solution.py:62
  90.6 3.2 %collective-permute-start.14 = (f32[4,24,320]{2,1,0:T(8,128)S(1)}, f32[4,24,320]{2,1,0:T(8,128)S(1)}, u32[]{:S(2)}, u32[]{:S(2)}) collective-permute-start(f32[4,24,320]{2,1,0:T(8,128)S(1)} %fusion.10), channel_id=1, source_target_pairs={{0,12},{4,8},{8,4},{12,0},{1,13},{5,9},{9,5},{13,1},{2,14},{6,10},... | collective-permute-start | bytes 368648 | tf_op jit(solution)/shard_map/ppermute | solution.py:62
  97.1 3.5 %all-to-all-start.2 = ((bf16[8,96,432]{2,1,0:T(8,128)(2,1)}), bf16[8,96,432]{2,1,0:T(8,128)(2,1)S(1)}, u32[]{:S(2)}, u32[]{:S(2)}) async-start(bf16[8,96,432]{2,1,0:T(8,128)(2,1)} %broadcast_in_dim.16), calls=%async_computation.2 | async-start | bytes 1572864 | tf_op jit(solution)/shard_map/all_to_all | solution.py:25
  100.6 6.3 %collective-permute-done.13 = f32[4,24,320]{2,1,0:T(8,128)S(1)} collective-permute-done((f32[4,24,320]{2,1,0:T(8,128)S(1)}, f32[4,24,320]{2,1,0:T(8,128)S(1)}, u32[]{:S(2)}, u32[]{:S(2)}) %collective-permute-start.13) | collective-permute-done | bytes 122912 | tf_op jit(solution)/shard_map/ppermute | solution.py:62
  107.0 10.2 %all-gather = bf16[16,24,320]{2,1,0:T(8,128)(2,1)S(1)} all-gather(bf16[4,24,320]{2,1,0:T(8,128)(2,1)S(1)} %add_convert_fusion.1), channel_id=2, replica_groups=mesh['y'=8,'zh'=2,'core'=2,'zl'=4,'x'=4] {'x'}, dimensions={0}, use_global_device_ids=true | all-gather | bytes 307200 | tf_op jit(solution)/shard_map/all_gather | solution.py:166
  117.2 4.6 %collective-permute-start.15 = (bf16[16,24,320]{2,1,0:T(8,128)(2,1)S(1)}, bf16[16,24,320]{2,1,0:T(8,128)(2,1)S(1)}, u32[]{:S(2)}, u32[]{:S(2)}) collective-permute-start(bf16[16,24,320]{2,1,0:T(8,128)(2,1)S(1)} %bitcast.46), channel_id=1, source_target_pairs={{0,16},{16,0},{1,17},{17,1},{2,18},{18,2},{3,19},{19,3},{4,20},{20... | collective-permute-start | bytes 737288 | tf_op jit(solution)/shard_map/ppermute | solution.py:31
  123.4 7.0 %shard_map.64 = f32[4,128]{1,0:T(4,128)S(1)} custom-call(bf16[768,432]{1,0:T(8,128)(2,1)S(1)} %bitcast.37, bf16[768,320]{1,0:T(8,128)(2,1)S(1)} %bitcast.38, f32[320,432]{1,0:T(8,128)S(1)} %maximum_divide_fusion.recip_ref), custom_call_target="tpu_custom_call" | custom-call | flops 2335703040 | bytes 1708032 | tf_op jit(solution)/shard_map/pallas_call | solution.py:103
  130.5 18.0 %all_to_all.25 = f32[32,4,128]{2,1,0:T(4,128)S(1)} all-to-all(f32[32,4,128]{2,1,0:T(4,128)S(1)} %broadcast_in_dim.17), channel_id=1, replica_groups=mesh['y'=8,'zh'=2,'core'=2,'zl'=4,'x'=4] {'core','zl','x'}, dimensions={0} | all-to-all | bytes 131072 | tf_op jit(solution)/shard_map/all_to_all | solution.py:25
  148.5 15.4 %all_to_all.26 = f32[16,4,128]{2,1,0:T(4,128)S(1)} all-to-all(f32[16,4,128]{2,1,0:T(4,128)S(1)} %broadcast_in_dim.18), channel_id=1, replica_groups=mesh['y'=8,'zh'=2,'core'=2,'zl'=4,'x'=4] {'y','zh'}, dimensions={0} | all-to-all | bytes 65536 | tf_op jit(solution)/shard_map/all_to_all | solution.py:25
  (71 shorter events, 21.1 us)
Async XLA Ops:
  0.0 60.5 %copy-start = (s32[48]{0:T(128)S(1)}, s32[48]{0:T(128)}, u32[]{:S(2)}) copy-start(s32[48]{0:T(128)} %param.11) | copy-start | bytes 580
  0.0 20.4 %copy-start.6 = (bf16[24,320]{1,0:T(8,128)(2,1)S(1)}, bf16[24,320]{1,0:T(8,128)(2,1)}, u32[]{:S(2)}) copy-start(bf16[24,320]{1,0:T(8,128)(2,1)} %param.7) | copy-start | bytes 46084
  0.0 23.7 %copy-start.2 = (bf16[432,864]{1,0:T(8,128)(2,1)S(1)}, bf16[432,864]{1,0:T(8,128)(2,1)}, u32[]{:S(2)}) copy-start(bf16[432,864]{1,0:T(8,128)(2,1)} %param.8) | copy-start | bytes 2239492
  0.0 20.4 %collective-permute-start.2 = (bf16[24,320]{1,0:T(8,128)(2,1)}, bf16[24,320]{1,0:T(8,128)(2,1)S(1)}, u32[]{:S(2)}, u32[]{:S(2)}) collective-permute-start(bf16[24,320]{1,0:T(8,128)(2,1)} %param.7), channel_id=1, source_target_pairs={{0,32},{32,0},{1,33},{33,1},{2,34},{34,2},{3,35},{35,3},{4,36},{36... | collective-permute-start | bytes 46088 | tf_op jit(solution)/shard_map/ppermute | solution.py:46
  13.4 14.7 %copy-start.5 = (bf16[320,160]{0,1:T(8,128)(2,1)S(1)}, bf16[320,160]{0,1:T(8,128)(2,1)}, u32[]{:S(2)}) copy-start(bf16[320,160]{0,1:T(8,128)(2,1)} %param.9) | copy-start | bytes 307204
  13.4 25.2 %all-to-all-start = ((bf16[16,48,432]{2,1,0:T(8,128)(2,1)}), bf16[16,48,432]{2,1,0:T(8,128)(2,1)S(1)}, u32[]{:S(2)}, u32[]{:S(2)}) async-start(bf16[16,48,432]{2,1,0:T(8,128)(2,1)} %broadcast_in_dim.14), calls=%async_computation | async-start | bytes 1572864 | tf_op jit(solution)/shard_map/all_to_all | solution.py:25
  20.4 9.6 %collective-permute-start.3 = (bf16[48,320]{1,0:T(8,128)(2,1)S(1)}, bf16[48,320]{1,0:T(8,128)(2,1)S(1)}, u32[]{:S(2)}, u32[]{:S(2)}) collective-permute-start(bf16[48,320]{1,0:T(8,128)(2,1)S(1)} %pad_maximum_fusion.4), channel_id=1, source_target_pairs={{0,64},{64,0},{128,192},{192,128},{256,320},{320,256},{384,448},{4... | collective-permute-start | bytes 92168 | tf_op jit(solution)/shard_map/ppermute | solution.py:46
  24.6 13.9 %collective-permute-start = (bf16[432,432]{1,0:T(8,128)(2,1)}, bf16[432,432]{1,0:T(8,128)(2,1)S(1)}, u32[]{:S(2)}, u32[]{:S(2)}) collective-permute-start(bf16[432,432]{1,0:T(8,128)(2,1)} %broadcast_select_fusion), channel_id=1, source_target_pairs={{0,16},{16,0},{1,17},{17,1},{2,18},{18,2},{3,19},{19,3},{4,20},{20... | collective-permute-start | bytes 1119752 | tf_op jit(solution)/shard_map/ppermute | solution.py:31
  28.1 6.3 %collective-permute-start.1 = (bf16[320,160]{0,1:T(8,128)(2,1)S(1)}, bf16[320,160]{0,1:T(8,128)(2,1)S(1)}, u32[]{:S(2)}, u32[]{:S(2)}) collective-permute-start(bf16[320,160]{0,1:T(8,128)(2,1)S(1)} %copy-done.5), channel_id=1, source_target_pairs={{0,16},{16,0},{1,17},{17,1},{2,18},{18,2},{3,19},{19,3},{4,20},{20... | collective-permute-start | bytes 307208 | tf_op jit(solution)/shard_map/ppermute | solution.py:31
  30.1 8.4 %collective-permute-start.4 = (bf16[96,320]{1,0:T(8,128)(2,1)S(1)}, bf16[96,320]{1,0:T(8,128)(2,1)S(1)}, u32[]{:S(2)}, u32[]{:S(2)}) collective-permute-start(bf16[96,320]{1,0:T(8,128)(2,1)S(1)} %pad_maximum_fusion.3), channel_id=1, source_target_pairs={{0,128},{64,192},{128,0},{192,64},{256,384},{320,448},{384,256},{4... | collective-permute-start | bytes 184328 | tf_op jit(solution)/shard_map/ppermute | solution.py:46
  34.4 10.1 %copy-start.1 = (f32[864,160]{0,1:T(8,128)S(1)}, f32[864,160]{0,1:T(8,128)}, u32[]{:S(2)}) copy-start(f32[864,160]{0,1:T(8,128)} %param.10) | copy-start | bytes 1658884
  40.4 6.9 %collective-permute-start.5 = (bf16[768,432]{0,1:T(8,128)(2,1)}, bf16[768,432]{0,1:T(8,128)(2,1)S(1)}, u32[]{:S(2)}, u32[]{:S(2)}) collective-permute-start(bf16[768,432]{0,1:T(8,128)(2,1)} %copy.30), channel_id=1, source_target_pairs={{0,16},{16,0},{1,17},{17,1},{2,18},{18,2},{3,19},{19,3},{4,20},{20... | collective-permute-start | bytes 1990664 | tf_op jit(solution)/shard_map/ppermute | solution.py:31
  44.6 31.5 %collective-permute-start.10 = (f32[160,432]{1,0:T(8,128)S(1)}, f32[160,432]{1,0:T(8,128)}, u32[]{:S(2)}, u32[]{:S(2)}) collective-permute-start(f32[160,432]{1,0:T(8,128)S(1)} %slice_select_fusion.1), channel_id=1, source_target_pairs={{0,16},{16,0},{1,17},{17,1},{2,18},{18,2},{3,19},{19,3},{4,20},{20... | collective-permute-start | bytes 829448 | tf_op jit(solution)/shard_map/ppermute | solution.py:31
  48.3 13.5 %collective-permute-start.6 = (bf16[192,320]{1,0:T(8,128)(2,1)S(1)}, bf16[192,320]{1,0:T(8,128)(2,1)S(1)}, u32[]{:S(2)}, u32[]{:S(2)}) collective-permute-start(bf16[192,320]{1,0:T(8,128)(2,1)S(1)} %pad_maximum_fusion.2), channel_id=1, source_target_pairs={{0,256},{64,320},{128,384},{192,448},{256,0},{320,64},{384,128},{4... | collective-permute-start | bytes 368648 | tf_op jit(solution)/shard_map/ppermute | solution.py:46
  57.0 27.0 %all-to-all-start.1 = ((bf16[8,96,432]{2,1,0:T(8,128)(2,1)}), bf16[8,96,432]{2,1,0:T(8,128)(2,1)S(1)}, u32[]{:S(2)}, u32[]{:S(2)}) async-start(bf16[8,96,432]{2,1,0:T(8,128)(2,1)} %bitcast.1), calls=%async_computation.1 | async-start | bytes 1572864 | tf_op jit(solution)/shard_map/all_to_all | solution.py:145
  62.2 9.0 %collective-permute-start.9 = (f32[4,24,320]{2,1,0:T(8,128)S(1)}, f32[4,24,320]{2,1,0:T(8,128)S(1)}, u32[]{:S(2)}, u32[]{:S(2)}) collective-permute-start(f32[4,24,320]{2,1,0:T(8,128)S(1)} %get-tuple-element.34), channel_id=1, source_target_pairs={{0,3},{1,2},{2,1},{3,0},{4,7},{5,6},{6,5},{7,4},{8,11},{9,10},{10,... | collective-permute-start | bytes 368648 | tf_op jit(solution)/shard_map/ppermute | solution.py:56
  65.8 7.7 %collective-permute-start.8 = (f32[4,24,320]{2,1,0:T(8,128)S(1)}, f32[4,24,320]{2,1,0:T(8,128)S(1)}, u32[]{:S(2)}, u32[]{:S(2)}) collective-permute-start(f32[4,24,320]{2,1,0:T(8,128)S(1)} %get-tuple-element.35), channel_id=1, source_target_pairs={{0,2},{1,3},{2,0},{3,1},{4,6},{5,7},{6,4},{7,5},{8,10},{9,11},{10,... | collective-permute-start | bytes 368648 | tf_op jit(solution)/shard_map/ppermute | solution.py:56
  68.3 7.7 %collective-permute-start.7 = (f32[4,24,320]{2,1,0:T(8,128)S(1)}, f32[4,24,320]{2,1,0:T(8,128)S(1)}, u32[]{:S(2)}, u32[]{:S(2)}) collective-permute-start(f32[4,24,320]{2,1,0:T(8,128)S(1)} %get-tuple-element.33), channel_id=1, source_target_pairs={{0,1},{1,0},{2,3},{3,2},{4,5},{5,4},{6,7},{7,6},{8,9},{9,8},{10,11... | collective-permute-start | bytes 368648 | tf_op jit(solution)/shard_map/ppermute | solution.py:56
  84.1 11.9 %collective-permute-start.11 = (f32[96,432]{1,0:T(8,128)S(1)}, f32[96,432]{1,0:T(8,128)S(1)}, u32[]{:S(2)}, u32[]{:S(2)}) collective-permute-start(f32[96,432]{1,0:T(8,128)S(1)} %convert_reduce_fusion), channel_id=1, source_target_pairs={{0,32},{32,0},{1,33},{33,1},{2,34},{34,2},{3,35},{35,3},{4,36},{36... | collective-permute-start | bytes 497672 | tf_op jit(solution)/shard_map/ppermute | solution.py:31
  86.0 20.9 %collective-permute-start.13 = (f32[4,24,320]{2,1,0:T(8,128)S(1)}, f32[4,24,320]{2,1,0:T(8,128)S(1)}, u32[]{:S(2)}, u32[]{:S(2)}) collective-permute-start(f32[4,24,320]{2,1,0:T(8,128)S(1)} %fusion.10), channel_id=1, source_target_pairs={{0,8},{4,12},{8,0},{12,4},{1,9},{5,13},{9,1},{13,5},{2,10},{6,14},... | collective-permute-start | bytes 368648 | tf_op jit(solution)/shard_map/ppermute | solution.py:62
  90.6 16.4 %collective-permute-start.14 = (f32[4,24,320]{2,1,0:T(8,128)S(1)}, f32[4,24,320]{2,1,0:T(8,128)S(1)}, u32[]{:S(2)}, u32[]{:S(2)}) collective-permute-start(f32[4,24,320]{2,1,0:T(8,128)S(1)} %fusion.10), channel_id=1, source_target_pairs={{0,12},{4,8},{8,4},{12,0},{1,13},{5,9},{9,5},{13,1},{2,14},{6,10},... | collective-permute-start | bytes 368648 | tf_op jit(solution)/shard_map/ppermute | solution.py:62
  93.8 13.2 %collective-permute-start.12 = (f32[4,24,320]{2,1,0:T(8,128)S(1)}, f32[4,24,320]{2,1,0:T(8,128)S(1)}, u32[]{:S(2)}, u32[]{:S(2)}) collective-permute-start(f32[4,24,320]{2,1,0:T(8,128)S(1)} %fusion.10), channel_id=1, source_target_pairs={{0,4},{4,0},{8,12},{12,8},{1,5},{5,1},{9,13},{13,9},{2,6},{6,2},{1... | collective-permute-start | bytes 368648 | tf_op jit(solution)/shard_map/ppermute | solution.py:62
  97.1 26.3 %all-to-all-start.2 = ((bf16[8,96,432]{2,1,0:T(8,128)(2,1)}), bf16[8,96,432]{2,1,0:T(8,128)(2,1)S(1)}, u32[]{:S(2)}, u32[]{:S(2)}) async-start(bf16[8,96,432]{2,1,0:T(8,128)(2,1)} %broadcast_in_dim.16), calls=%async_computation.2 | async-start | bytes 1572864 | tf_op jit(solution)/shard_map/all_to_all | solution.py:25
  117.2 5.9 %collective-permute-start.15 = (bf16[16,24,320]{2,1,0:T(8,128)(2,1)S(1)}, bf16[16,24,320]{2,1,0:T(8,128)(2,1)S(1)}, u32[]{:S(2)}, u32[]{:S(2)}) collective-permute-start(bf16[16,24,320]{2,1,0:T(8,128)(2,1)S(1)} %bitcast.46), channel_id=1, source_target_pairs={{0,16},{16,0},{1,17},{17,1},{2,18},{18,2},{3,19},{19,3},{4,20},{20... | collective-permute-start | bytes 737288 | tf_op jit(solution)/shard_map/ppermute | solution.py:31
  (2 other events, 1.8 us)

commit v6 on v5

v6 whole, which is shorter than its diff:
```python
import jax
import jax.numpy as jnp
from jax import lax
from jax.experimental import pallas as pl
from jax.experimental.pallas import tpu as pltpu
from jax.sharding import Mesh, PartitionSpec as P

D = 5120
FF = 13824
NQ = 16
NT = 32
TOKX = 16
NTOK = 768

SIZES = (8, 2, 2, 4, 4)
NAMES = ("y", "zh", "core", "zl", "x")
BASIS = ("y", "zh", "core")
EX = ("zl", "x")
SWAP = ((0, 1), (1, 0))
bf16 = jnp.bfloat16
f32 = jnp.float32


def spread(x, axes, n):
    return lax.all_to_all(
        jnp.broadcast_to(x[None], (n,) + x.shape), axes, 0, 0, tiled=True
    )


def swap(x, axis):
    return lax.ppermute(x, axis, SWAP)


def tie(*values):
    return lax.optimization_barrier(values)


def padded(x, value):
    return jnp.pad(x, ((0, 0), (0, -x.shape[1] % 64)), constant_values=value)


def transposed_product(w, x):
    x = x.reshape(-1, x.shape[-1])
    return lax.dot_general(w, x, (((0,), (1,)), ((), ())), preferred_element_type=f32)


def ordered(mine, other, second):
    lo = jnp.where(second, other, mine)
    hi = jnp.where(second, mine, other)
    return lo, hi


def partner(x, axis, bit):
    n = SIZES[NAMES.index(axis)]
    return lax.ppermute(x, axis, [(i, i ^ bit) for i in range(n)])


def doubled(x, axis, bit):
    return jnp.concatenate([x, partner(x, axis, bit)], axis=0)


def input_kernel(x_ref, other_ref, w_ref, out_ref):
    n = x_ref.shape[0]
    out_ref[:n] = jnp.dot(x_ref[...], w_ref[...], preferred_element_type=f32)
    out_ref[n:] = jnp.dot(other_ref[...], w_ref[...], preferred_element_type=f32)


def input_product(x, other, w):
    x, other = (v.reshape(-1, v.shape[-1]) for v in (x, other))
    vmem = pl.BlockSpec(memory_space=pltpu.VMEM)
    return pl.pallas_call(
        input_kernel,
        out_shape=jax.ShapeDtypeStruct((2 * x.shape[0], w.shape[1]), f32),
        in_specs=[vmem] * 3,
        out_specs=vmem,
        compiler_params=pltpu.CompilerParams(vmem_limit_bytes=40 * 1024 * 1024),
        cost_estimate=pl.CostEstimate(
            flops=6000000000, bytes_accessed=8 * x.size, transcendentals=0
        ),
    )(x, other, w)


def scattered(x, axis, dim):
    here = lax.axis_index(axis)
    total = lax.dynamic_index_in_dim(x, here, dim, keepdims=False)
    for bit in (1, 2, 3):
        block = lax.dynamic_index_in_dim(x, here ^ bit, dim, keepdims=False)
        total = total + lax.ppermute(block, axis, [(i, i ^ bit) for i in range(4)])
    return total


def summed(x, axis):
    one, two, three = (
        lax.ppermute(x, axis, [(i, i ^ bit) for i in range(4)]) for bit in (1, 2, 3)
    )
    return (x + one) + (two + three)


def arrange_kernel(place_ref, half_ref, other_ref, query_ref, train_ref, act):
    here_yz, core = place_ref[0], place_ref[1]
    for block in range(NTOK // 48):
        far = here_yz ^ block
        zh, y1, y2, y4 = far & 1, (far >> 1) & 1, (far >> 2) & 1, (far >> 3) & 1
        at = 4 * (y4 + 2 * y2) + y1 + 2 * zh
        for ref, side in ((half_ref, core), (other_ref, 1 - core)):
            start = pl.multiple_of(48 * block + 24 * side, 8)
            act[pl.ds(start, 24), :] = ref[at].astype(f32)
    query_ref[...] = act[: NQ * TOKX, :].astype(bf16)
    train_ref[...] = act[NQ * TOKX :, :].T


def arranged(place, act_half, act_other):
    cols = act_half.shape[-1]
    vmem = pl.BlockSpec(memory_space=pltpu.VMEM)
    return pl.pallas_call(
        arrange_kernel,
        out_shape=(
            jax.ShapeDtypeStruct((NQ * TOKX, cols), bf16),
            jax.ShapeDtypeStruct((cols, NT * TOKX), f32),
        ),
        in_specs=[pl.BlockSpec(memory_space=pltpu.SMEM), vmem, vmem],
        out_specs=(vmem, vmem),
        scratch_shapes=[pltpu.VMEM((NTOK, cols), f32)],
        compiler_params=pltpu.CompilerParams(vmem_limit_bytes=40 * 1024 * 1024),
        cost_estimate=pl.CostEstimate(
            flops=5000000000, bytes_accessed=12 * NTOK * cols, transcendentals=0
        ),
    )(place, act_half, act_other)


def score_kernel(grad_ref, query_ref, train_ref, recip_ref, out_ref, grad_q, rows):
    grad_q[...] = grad_ref[:, : NQ * TOKX].T

    def one_query(q, carry):
        here = pl.ds(pl.multiple_of(q * TOKX, TOKX), TOKX)
        outer = lax.dot_general(
            query_ref[here, :],
            grad_q[here, :],
            (((0,), (0,)), ((), ())),
            preferred_element_type=f32,
        )
        precond = (outer * recip_ref[...]).astype(bf16)
        projected = jnp.dot(
            precond, grad_ref[:, NQ * TOKX :], preferred_element_type=f32
        )
        rows[pl.ds(q, 1), :] = jnp.sum(projected * train_ref[...], axis=0, keepdims=True)
        return carry

    lax.fori_loop(0, NQ, one_query, 0, unroll=2)

    slot = lax.broadcasted_iota(jnp.int32, (NT * TOKX, 128), 0)
    lane = lax.broadcasted_iota(jnp.int32, (NT * TOKX, 128), 1)
    pick = (slot // TOKX == lane % NT).astype(f32)
    sums = jnp.dot(
        rows[...], pick, preferred_element_type=f32, precision=lax.Precision.HIGHEST
    )
    query = lax.broadcasted_iota(jnp.int32, (NQ, 128), 0)
    place = lax.broadcasted_iota(jnp.int32, (NQ, 128), 1)
    sums = jnp.where(place // NT == query % 4, sums, 0.0)
    scale = TOKX * (float(FF) * float(D)) ** 0.5
    out_ref[...] = jnp.sum(sums.reshape(4, 4, 128), axis=1) / scale


def scores(rot_grad, query_act, train_act, recip):
    cols_act, cols_grad = recip.shape
    vmem = pl.BlockSpec(memory_space=pltpu.VMEM)
    return pl.pallas_call(
        score_kernel,
        out_shape=jax.ShapeDtypeStruct((4, 128), f32),
        in_specs=[vmem] * 4,
        out_specs=vmem,
        scratch_shapes=[
            pltpu.VMEM((NQ * TOKX, cols_grad), bf16),
            pltpu.VMEM((NQ, NT * TOKX), f32),
        ],
        compiler_params=pltpu.CompilerParams(vmem_limit_bytes=40 * 1024 * 1024),
        cost_estimate=pl.CostEstimate(
            flops=2 * NQ * cols_act * cols_grad * (NT * TOKX + TOKX),
            bytes_accessed=2 * NTOK * (cols_act + cols_grad) + 4 * cols_act * cols_grad,
            transcendentals=0,
        ),
    )(rot_grad, query_act, train_act, recip)


def body(grad_out, acts, basis_out, basis_in, eigvals, counts):
    core = lax.axis_index("core")
    second = core == 1
    half = basis_out.shape[1] // 2

    grads = spread(grad_out, EX, 16)
    act = doubled(acts[None], "y", 4)
    w_lo, w_hi = basis_out[:, :half], basis_out[:, half:]
    w_mine = padded(jnp.where(second, w_hi, w_lo), 0)
    w_other = swap(padded(jnp.where(second, w_lo, w_hi), 0), "core")
    b_other = swap(basis_in, "core")
    b_in = jnp.concatenate(ordered(basis_in, b_other, second), axis=1)
    act = doubled(act, "y", 2)
    act = doubled(act, "y", 1)
    grads, w_other, b_in, act = tie(grads, w_other, b_in, act)

    g_other = swap(grads, "core")
    partial = transposed_product(w_mine, grads)
    g_other, partial = tie(g_other, partial)
    partial = partial + transposed_product(w_other, g_other)
    partial = partial.astype(bf16)
    act_far = partner(act, "zh", 1)

    pieces = lax.all_to_all(
        partial.reshape(8, -1, NTOK), "y", 0, 0, tiled=True
    )
    product_act = input_product(act, act_far, b_in)
    eig_t = eigvals.T
    e_lo, e_hi = eig_t[:, :half], eig_t[:, half:]
    e_mine = jnp.where(second, e_hi, e_lo)
    e_send = jnp.where(second, e_lo, e_hi)
    e_send, in_use, product_act = tie(e_send, counts, product_act)
    e_other = swap(e_send, "core")
    part_act = scattered(product_act.reshape(4, 4, 24, -1), "x", 1)
    slots = lax.broadcasted_iota(jnp.int32, (NQ + NT, TOKX), 1)
    used = (slots < in_use[:, None]).astype(f32).reshape(1, NTOK)
    pieces, part_act, used, e_other = tie(pieces, part_act, used, e_other)

    piece = jnp.sum(pieces.astype(f32), axis=0)
    piece_other = swap(piece, "zh")
    act_piece = summed(part_act, "zl").astype(bf16)
    piece = ((piece + piece_other) * used).astype(bf16)

    rot_grad = spread(piece, "y", 8).reshape(-1, NTOK)
    act_half = lax.all_gather(act_piece, "x", axis=0)
    act_half = act_half.reshape(16, 24, -1)
    act_other = swap(act_half, "core")
    recip = 1.0 / jnp.concatenate(ordered(e_mine, e_other, second), axis=0)
    recip = padded(recip, 1)

    place = jnp.stack([2 * lax.axis_index("y") + lax.axis_index("zh"), core])
    query_act, train_act = arranged(place, act_half, act_other)
    flat = scores(rot_grad, query_act, train_act, recip)
    flat = jnp.sum(spread(flat, ("core",) + EX, 32), axis=0)
    flat = jnp.sum(spread(flat, ("y", "zh"), 16), axis=0)
    return flat.reshape(NQ, NT)


def solution(mesh):
    fine = Mesh(mesh.devices.reshape(SIZES), NAMES)
    return jax.shard_map(
        body,
        mesh=fine,
        in_specs=(
            P(EX, BASIS),
            P(BASIS, EX),
            P(BASIS, EX),
            P(EX, BASIS),
            P(EX, BASIS),
            P(),
        ),
        out_specs=P(),
        check_vma=False,
    )
```

time: 166 us -> 159 us (0.958)
  local copies, waits for them, and re-layouts: 8.08 us -> 3.83 us
  waiting for transfers between devices: 23.4 us -> 19.3 us
  starting transfers between devices: 77 us -> 80.1 us
    ppermute x3, waiting for transfers between devices: 4.77 us -> 1.04 us  [scattered(): total = total + lax.ppermute(block, axis, [(i, i ^ bit) for i in range(4)])]
    ppermute x4, starting transfers between devices: 26.5 us -> 22.9 us  [partner(): return lax.ppermute(x, axis, [(i, i ^ bit) for i in range(n)])]
    all_to_all x2, starting transfers between devices: 10.5 us -> 13.9 us  [spread(): lax.all_to_all(jnp.broadcast_to(x[None], (n,) + x.shape), axes, 0, 0, til...]
    optimization_barrier x2 -> x0, local copies, waits for them, and re-layouts: 2.27 us -> none  [tie(): return lax.optimization_barrier(values)]
  transfers between devices with their start and end apart: 19 -> 19, of which waited for: 6 -> 7; matrix products, arithmetic and copies ran while one was open for 6% -> 3% of each run, Pallas kernels for 0% -> 1%
where the time goes in v6:
time: 159 us; the launch traced here: 158 us
  starting transfers between devices  80.1 us (50%)
  blocking collectives  42.3 us (27%)
  waiting for transfers between devices  19.3 us (12%)
  Pallas kernels  8.15 us (5%)
  local copies, waits for them, and re-layouts  3.83 us (2%)
  other arithmetic  2.25 us (1%)
    all_to_all x2, blocking collectives, spread(): lax.all_to_all(jnp.broadcast_to(x[None], (n,) + x.shape), axes, 0, 0, til...  31.7 us
    ppermute x4, starting transfers between devices, partner(): return lax.ppermute(x, axis, [(i, i ^ bit) for i in range(n)])  22.9 us
    ppermute x6, starting transfers between devices, swap(): return lax.ppermute(x, axis, SWAP)  19.1 us
    all_to_all x2, starting transfers between devices, spread(): lax.all_to_all(jnp.broadcast_to(x[None], (n,) + x.shape), axes, 0, 0, til...  13.9 us
    all_gather x1, blocking collectives, body(): act_half = lax.all_gather(act_piece, 'x', axis=0)  10.6 us
    ppermute x3, starting transfers between devices, summed(): lax.ppermute(x, axis, [(i, i ^ bit) for i in range(4)])  9.64 us
    ppermute x3, starting transfers between devices, scattered(): total = total + lax.ppermute(block, axis, [(i, i ^ bit) for i in range(4)])  9.37 us
    ppermute x3, waiting for transfers between devices, summed(): lax.ppermute(x, axis, [(i, i ^ bit) for i in range(4)])  7.37 us
  transfers between devices with their start and end apart: 19, of which 7 were waited for; matrix products, arithmetic and copies ran while one was open for 3% of the time, Pallas kernels for 1%

profile of v6, /device:TPU:1, one launch (start us, length us, event | category | flops | bytes accessed | tf_op | source)
XLA Modules:
  0.0 157.7 jit_solution(11148562683903021766)
XLA Ops:
  1.8 10.4 %all-to-all-start = ((bf16[16,48,432]{2,1,0:T(8,128)(2,1)}), bf16[16,48,432]{2,1,0:T(8,128)(2,1)S(1)}, u32[]{:S(2)}, u32[]{:S(2)}) async-start(bf16[16,48,432]{2,1,0:T(8,128)(2,1)} %broadcast_in_dim.10), calls=%async_computation | async-start | bytes 1572864 | tf_op jit(solution)/shard_map/all_to_all | solution.py:25
  12.2 7.6 %collective-permute-start.2 = (bf16[1,24,320]{2,1,0:T(8,128)(2,1)S(1)}, bf16[1,24,320]{2,1,0:T(8,128)(2,1)S(1)}, u32[]{:S(2)}, u32[]{:S(2)}) collective-permute-start(bf16[1,24,320]{2,1,0:T(8,128)(2,1)S(1)} %bitcast.35), channel_id=1, source_target_pairs={{0,256},{64,320},{128,384},{192,448},{256,0},{320,64},{384,128},{4... | collective-permute-start | bytes 46088 | tf_op jit(solution)/shard_map/ppermute | solution.py:55
  21.0 4.2 %collective-permute-start.3 = (bf16[2,24,320]{2,1,0:T(8,128)(2,1)S(1)}, bf16[2,24,320]{2,1,0:T(8,128)(2,1)S(1)}, u32[]{:S(2)}, u32[]{:S(2)}) collective-permute-start(bf16[2,24,320]{2,1,0:T(8,128)(2,1)S(1)} %pad_maximum_fusion.3), channel_id=1, source_target_pairs={{0,128},{64,192},{128,0},{192,64},{256,384},{320,448},{384,256},{4... | collective-permute-start | bytes 92168 | tf_op jit(solution)/shard_map/ppermute | solution.py:55
  25.5 4.1 %collective-permute-start = (bf16[432,448]{1,0:T(8,128)(2,1)S(1)}, bf16[432,448]{1,0:T(8,128)(2,1)S(1)}, u32[]{:S(2)}, u32[]{:S(2)}) collective-permute-start(bf16[432,448]{1,0:T(8,128)(2,1)S(1)} %pad.11), channel_id=1, source_target_pairs={{0,16},{16,0},{1,17},{17,1},{2,18},{18,2},{3,19},{19,3},{4,20},{20... | collective-permute-start | bytes 1161224 | tf_op jit(solution)/shard_map/ppermute | solution.py:31
  31.7 3.2 %collective-permute-start.4 = (bf16[4,24,320]{2,1,0:T(8,128)(2,1)S(1)}, bf16[4,24,320]{2,1,0:T(8,128)(2,1)S(1)}, u32[]{:S(2)}, u32[]{:S(2)}) collective-permute-start(bf16[4,24,320]{2,1,0:T(8,128)(2,1)S(1)} %pad_maximum_fusion.2), channel_id=1, source_target_pairs={{0,64},{64,0},{128,192},{192,128},{256,320},{320,256},{384,448},{4... | collective-permute-start | bytes 184328 | tf_op jit(solution)/shard_map/ppermute | solution.py:55
  36.9 3.6 %collective-permute-start.5 = (bf16[16,48,432]{2,1,0:T(8,128)(2,1)S(1)}, bf16[16,48,432]{2,1,0:T(8,128)(2,1)S(1)}, u32[]{:S(2)}, u32[]{:S(2)}) collective-permute-start(bf16[16,48,432]{2,1,0:T(8,128)(2,1)S(1)} %all-to-all-done), channel_id=1, source_target_pairs={{0,16},{16,0},{1,17},{17,1},{2,18},{18,2},{3,19},{19,3},{4,20},{20... | collective-permute-start | bytes 1990664 | tf_op jit(solution)/shard_map/ppermute | solution.py:31
  40.4 7.9 %collective-permute-start.6 = (bf16[8,24,320]{2,1,0:T(8,128)(2,1)S(1)}, bf16[8,24,320]{2,1,0:T(8,128)(2,1)S(1)}, u32[]{:S(2)}, u32[]{:S(2)}) collective-permute-start(bf16[8,24,320]{2,1,0:T(8,128)(2,1)S(1)} %pad_maximum_fusion.1), channel_id=1, source_target_pairs={{0,32},{32,0},{1,33},{33,1},{2,34},{34,2},{3,35},{35,3},{4,36},{36... | collective-permute-start | bytes 368648 | tf_op jit(solution)/shard_map/ppermute | solution.py:55
  50.7 5.1 %all-to-all-start.1 = ((bf16[8,56,768]{2,1,0:T(8,128)(2,1)}), bf16[8,56,768]{2,1,0:T(8,128)(2,1)S(1)}, u32[]{:S(2)}, u32[]{:S(2)}) async-start(bf16[8,56,768]{2,1,0:T(8,128)(2,1)} %bitcast.3), calls=%async_computation.1 | async-start | bytes 1376256 | tf_op jit(solution)/shard_map/all_to_all | solution.py:208
  56.4 5.0 %collective-permute-start.9 = (f32[4,24,320]{2,1,0:T(8,128)S(1)}, f32[4,24,320]{2,1,0:T(8,128)S(1)}, u32[]{:S(2)}, u32[]{:S(2)}) collective-permute-start(f32[4,24,320]{2,1,0:T(8,128)S(1)} %get-tuple-element.40), channel_id=1, source_target_pairs={{0,3},{1,2},{2,1},{3,0},{4,7},{5,6},{6,5},{7,4},{8,11},{9,10},{10,... | collective-permute-start | bytes 368648 | tf_op jit(solution)/shard_map/ppermute | solution.py:88
  61.4 2.5 %collective-permute-start.8 = (f32[4,24,320]{2,1,0:T(8,128)S(1)}, f32[4,24,320]{2,1,0:T(8,128)S(1)}, u32[]{:S(2)}, u32[]{:S(2)}) collective-permute-start(f32[4,24,320]{2,1,0:T(8,128)S(1)} %get-tuple-element.41), channel_id=1, source_target_pairs={{0,2},{1,3},{2,0},{3,1},{4,6},{5,7},{6,4},{7,5},{8,10},{9,11},{10,... | collective-permute-start | bytes 368648 | tf_op jit(solution)/shard_map/ppermute | solution.py:88
  63.9 1.9 %collective-permute-start.7 = (f32[4,24,320]{2,1,0:T(8,128)S(1)}, f32[4,24,320]{2,1,0:T(8,128)S(1)}, u32[]{:S(2)}, u32[]{:S(2)}) collective-permute-start(f32[4,24,320]{2,1,0:T(8,128)S(1)} %get-tuple-element.39), channel_id=1, source_target_pairs={{0,1},{1,0},{2,3},{3,2},{4,5},{5,4},{6,7},{7,6},{8,9},{9,8},{10,11... | collective-permute-start | bytes 368648 | tf_op jit(solution)/shard_map/ppermute | solution.py:88
  65.8 3.0 %collective-permute-start.10 = (f32[160,432]{1,0:T(8,128)S(1)}, f32[160,432]{1,0:T(8,128)S(1)}, u32[]{:S(2)}, u32[]{:S(2)}) collective-permute-start(f32[160,432]{1,0:T(8,128)S(1)} %slice_select_fusion.1), channel_id=1, source_target_pairs={{0,16},{16,0},{1,17},{17,1},{2,18},{18,2},{3,19},{19,3},{4,20},{20... | collective-permute-start | bytes 829448 | tf_op jit(solution)/shard_map/ppermute | solution.py:31
  70.1 7.2 %all-to-all-done.1 = bf16[8,56,768]{2,1,0:T(8,128)(2,1)S(1)} async-done(((bf16[8,56,768]{2,1,0:T(8,128)(2,1)}), bf16[8,56,768]{2,1,0:T(8,128)(2,1)S(1)}, u32[]{:S(2)}, u32[]{:S(2)}) %all-to-all-start.1) | async-done | bytes 688160 | tf_op jit(solution)/shard_map/all_to_all | solution.py:208
  77.4 2.0 %collective-permute-start.11 = (f32[56,768]{1,0:T(8,128)S(1)}, f32[56,768]{1,0:T(8,128)S(1)}, u32[]{:S(2)}, u32[]{:S(2)}) collective-permute-start(f32[56,768]{1,0:T(8,128)S(1)} %convert_reduce_fusion), channel_id=1, source_target_pairs={{0,32},{32,0},{1,33},{33,1},{2,34},{34,2},{3,35},{35,3},{4,36},{36... | collective-permute-start | bytes 516104 | tf_op jit(solution)/shard_map/ppermute | solution.py:31
  79.3 4.6 %collective-permute-start.13 = (f32[4,24,320]{2,1,0:T(8,128)S(1)}, f32[4,24,320]{2,1,0:T(8,128)S(1)}, u32[]{:S(2)}, u32[]{:S(2)}) collective-permute-start(f32[4,24,320]{2,1,0:T(8,128)S(1)} %fusion.3), channel_id=1, source_target_pairs={{0,8},{4,12},{8,0},{12,4},{1,9},{5,13},{9,1},{13,5},{2,10},{6,14},... | collective-permute-start | bytes 368648 | tf_op jit(solution)/shard_map/ppermute | solution.py:94
  84.0 3.1 %collective-permute-start.14 = (f32[4,24,320]{2,1,0:T(8,128)S(1)}, f32[4,24,320]{2,1,0:T(8,128)S(1)}, u32[]{:S(2)}, u32[]{:S(2)}) collective-permute-start(f32[4,24,320]{2,1,0:T(8,128)S(1)} %fusion.3), channel_id=1, source_target_pairs={{0,12},{4,8},{8,4},{12,0},{1,13},{5,9},{9,5},{13,1},{2,14},{6,10},... | collective-permute-start | bytes 368648 | tf_op jit(solution)/shard_map/ppermute | solution.py:94
  87.1 1.9 %collective-permute-start.12 = (f32[4,24,320]{2,1,0:T(8,128)S(1)}, f32[4,24,320]{2,1,0:T(8,128)S(1)}, u32[]{:S(2)}, u32[]{:S(2)}) collective-permute-start(f32[4,24,320]{2,1,0:T(8,128)S(1)} %fusion.3), channel_id=1, source_target_pairs={{0,4},{4,0},{8,12},{12,8},{1,5},{5,1},{9,13},{13,9},{2,6},{6,2},{1... | collective-permute-start | bytes 368648 | tf_op jit(solution)/shard_map/ppermute | solution.py:94
  90.0 3.5 %all-to-all-start.2 = ((bf16[8,56,768]{2,1,0:T(8,128)(2,1)}), bf16[8,56,768]{2,1,0:T(8,128)(2,1)S(1)}, u32[]{:S(2)}, u32[]{:S(2)}) async-start(bf16[8,56,768]{2,1,0:T(8,128)(2,1)} %broadcast_in_dim.12), calls=%async_computation.2 | async-start | bytes 1376256 | tf_op jit(solution)/shard_map/all_to_all | solution.py:25
  93.6 7.4 %collective-permute-done.13 = f32[4,24,320]{2,1,0:T(8,128)S(1)} collective-permute-done((f32[4,24,320]{2,1,0:T(8,128)S(1)}, f32[4,24,320]{2,1,0:T(8,128)S(1)}, u32[]{:S(2)}, u32[]{:S(2)}) %collective-permute-start.13) | collective-permute-done | bytes 122912 | tf_op jit(solution)/shard_map/ppermute | solution.py:94
  101.0 10.6 %all-gather.half_ref = bf16[16,24,320]{2,1,0:T(8,128)(2,1)S(1)} all-gather(bf16[4,24,320]{2,1,0:T(8,128)(2,1)S(1)} %add_convert_fusion.1), channel_id=2, replica_groups=mesh['y'=8,'zh'=2,'core'=2,'zl'=4,'x'=4] {'x'}, dimensions={0}, use_global_device_ids=true | all-gather | bytes 307200 | tf_op jit(solution)/shard_map/all_gather | solution.py:229
  111.6 4.5 %collective-permute-start.15 = (bf16[16,24,320]{2,1,0:T(8,128)(2,1)S(1)}, bf16[16,24,320]{2,1,0:T(8,128)(2,1)S(1)}, u32[]{:S(2)}, u32[]{:S(2)}) collective-permute-start(bf16[16,24,320]{2,1,0:T(8,128)(2,1)S(1)} %all-gather.half_ref), channel_id=1, source_target_pairs={{0,16},{16,0},{1,17},{17,1},{2,18},{18,2},{3,19},{19,3},{4,20},{20... | collective-permute-start | bytes 737288 | tf_op jit(solution)/shard_map/ppermute | solution.py:31
  118.3 6.9 %shard_map.66 = f32[4,128]{1,0:T(4,128)S(1)} custom-call(bf16[448,768]{1,0:T(8,128)(2,1)S(1)} %bitcast.26, bf16[256,320]{1,0:T(8,128)(2,1)S(1)} %get-tuple-element.32.query_ref, f32[320,512]{1,0:T(8,128)S(1)} %get-tuple-element.33.train_ref, f32[320,448]{1,0:T(8,128)S(1)} %pad.13.recip_ref), custom_call_target="tpu_custom_call" | custom-call | flops 2422210560 | bytes 1753088 | tf_op jit(solution)/shard_map/pallas_call | solution.py:167
  125.2 15.5 %all_to_all.25 = f32[32,4,128]{2,1,0:T(4,128)S(1)} all-to-all(f32[32,4,128]{2,1,0:T(4,128)S(1)} %broadcast_in_dim.13), channel_id=1, replica_groups=mesh['y'=8,'zh'=2,'core'=2,'zl'=4,'x'=4] {'core','zl','x'}, dimensions={0} | all-to-all | bytes 131072 | tf_op jit(solution)/shard_map/all_to_all | solution.py:25
  140.7 16.3 %all_to_all.26 = f32[16,4,128]{2,1,0:T(4,128)S(1)} all-to-all(f32[16,4,128]{2,1,0:T(4,128)S(1)} %broadcast_in_dim.14), channel_id=1, replica_groups=mesh['y'=8,'zh'=2,'core'=2,'zl'=4,'x'=4] {'y','zh'}, dimensions={0} | all-to-all | bytes 65536 | tf_op jit(solution)/shard_map/all_to_all | solution.py:25
  (61 shorter events, 15.3 us)
Async XLA Ops:
  0.0 12.2 %copy-start.2 = (bf16[24,320]{1,0:T(8,128)(2,1)S(1)}, bf16[24,320]{1,0:T(8,128)(2,1)}, u32[]{:S(2)}) copy-start(bf16[24,320]{1,0:T(8,128)(2,1)} %param.7) | copy-start | bytes 46084
  0.0 25.2 %copy-start.1 = (bf16[432,864]{1,0:T(8,128)(2,1)S(1)}, bf16[432,864]{1,0:T(8,128)(2,1)}, u32[]{:S(2)}) copy-start(bf16[432,864]{1,0:T(8,128)(2,1)} %param.8) | copy-start | bytes 2239492
  1.8 35.0 %all-to-all-start = ((bf16[16,48,432]{2,1,0:T(8,128)(2,1)}), bf16[16,48,432]{2,1,0:T(8,128)(2,1)S(1)}, u32[]{:S(2)}, u32[]{:S(2)}) async-start(bf16[16,48,432]{2,1,0:T(8,128)(2,1)} %broadcast_in_dim.10), calls=%async_computation | async-start | bytes 1572864 | tf_op jit(solution)/shard_map/all_to_all | solution.py:25
  12.2 17.4 %copy-start.3 = (bf16[320,160]{0,1:T(8,128)(2,1)S(1)}, bf16[320,160]{0,1:T(8,128)(2,1)}, u32[]{:S(2)}) copy-start(bf16[320,160]{0,1:T(8,128)(2,1)} %param.9) | copy-start | bytes 307204
  12.2 8.7 %collective-permute-start.2 = (bf16[1,24,320]{2,1,0:T(8,128)(2,1)S(1)}, bf16[1,24,320]{2,1,0:T(8,128)(2,1)S(1)}, u32[]{:S(2)}, u32[]{:S(2)}) collective-permute-start(bf16[1,24,320]{2,1,0:T(8,128)(2,1)S(1)} %bitcast.35), channel_id=1, source_target_pairs={{0,256},{64,320},{128,384},{192,448},{256,0},{320,64},{384,128},{4... | collective-permute-start | bytes 46088 | tf_op jit(solution)/shard_map/ppermute | solution.py:55
  21.0 10.7 %collective-permute-start.3 = (bf16[2,24,320]{2,1,0:T(8,128)(2,1)S(1)}, bf16[2,24,320]{2,1,0:T(8,128)(2,1)S(1)}, u32[]{:S(2)}, u32[]{:S(2)}) collective-permute-start(bf16[2,24,320]{2,1,0:T(8,128)(2,1)S(1)} %pad_maximum_fusion.3), channel_id=1, source_target_pairs={{0,128},{64,192},{128,0},{192,64},{256,384},{320,448},{384,256},{4... | collective-permute-start | bytes 92168 | tf_op jit(solution)/shard_map/ppermute | solution.py:55
  25.5 11.4 %collective-permute-start = (bf16[432,448]{1,0:T(8,128)(2,1)S(1)}, bf16[432,448]{1,0:T(8,128)(2,1)S(1)}, u32[]{:S(2)}, u32[]{:S(2)}) collective-permute-start(bf16[432,448]{1,0:T(8,128)(2,1)S(1)} %pad.11), channel_id=1, source_target_pairs={{0,16},{16,0},{1,17},{17,1},{2,18},{18,2},{3,19},{19,3},{4,20},{20... | collective-permute-start | bytes 1161224 | tf_op jit(solution)/shard_map/ppermute | solution.py:31
  29.7 5.2 %collective-permute-start.1 = (bf16[320,160]{1,0:T(8,128)(2,1)S(1)}, bf16[320,160]{1,0:T(8,128)(2,1)S(1)}, u32[]{:S(2)}, u32[]{:S(2)}) collective-permute-start(bf16[320,160]{1,0:T(8,128)(2,1)S(1)} %copy.27), channel_id=1, source_target_pairs={{0,16},{16,0},{1,17},{17,1},{2,18},{18,2},{3,19},{19,3},{4,20},{20... | collective-permute-start | bytes 307208 | tf_op jit(solution)/shard_map/ppermute | solution.py:31
  31.7 5.1 %collective-permute-start.4 = (bf16[4,24,320]{2,1,0:T(8,128)(2,1)S(1)}, bf16[4,24,320]{2,1,0:T(8,128)(2,1)S(1)}, u32[]{:S(2)}, u32[]{:S(2)}) collective-permute-start(bf16[4,24,320]{2,1,0:T(8,128)(2,1)S(1)} %pad_maximum_fusion.2), channel_id=1, source_target_pairs={{0,64},{64,0},{128,192},{192,128},{256,320},{320,256},{384,448},{4... | collective-permute-start | bytes 184328 | tf_op jit(solution)/shard_map/ppermute | solution.py:55
  36.9 12.1 %collective-permute-start.5 = (bf16[16,48,432]{2,1,0:T(8,128)(2,1)S(1)}, bf16[16,48,432]{2,1,0:T(8,128)(2,1)S(1)}, u32[]{:S(2)}, u32[]{:S(2)}) collective-permute-start(bf16[16,48,432]{2,1,0:T(8,128)(2,1)S(1)} %all-to-all-done), channel_id=1, source_target_pairs={{0,16},{16,0},{1,17},{17,1},{2,18},{18,2},{3,19},{19,3},{4,20},{20... | collective-permute-start | bytes 1990664 | tf_op jit(solution)/shard_map/ppermute | solution.py:31
  40.4 15.6 %collective-permute-start.6 = (bf16[8,24,320]{2,1,0:T(8,128)(2,1)S(1)}, bf16[8,24,320]{2,1,0:T(8,128)(2,1)S(1)}, u32[]{:S(2)}, u32[]{:S(2)}) collective-permute-start(bf16[8,24,320]{2,1,0:T(8,128)(2,1)S(1)} %pad_maximum_fusion.1), channel_id=1, source_target_pairs={{0,32},{32,0},{1,33},{33,1},{2,34},{34,2},{3,35},{35,3},{4,36},{36... | collective-permute-start | bytes 368648 | tf_op jit(solution)/shard_map/ppermute | solution.py:55
  50.7 5.1 %copy-start = (f32[864,160]{0,1:T(8,128)S(1)}, f32[864,160]{0,1:T(8,128)}, u32[]{:S(2)}) copy-start(f32[864,160]{0,1:T(8,128)} %param.10) | copy-start | bytes 1658884
  50.7 26.6 %all-to-all-start.1 = ((bf16[8,56,768]{2,1,0:T(8,128)(2,1)}), bf16[8,56,768]{2,1,0:T(8,128)(2,1)S(1)}, u32[]{:S(2)}, u32[]{:S(2)}) async-start(bf16[8,56,768]{2,1,0:T(8,128)(2,1)} %bitcast.3), calls=%async_computation.1 | async-start | bytes 1376256 | tf_op jit(solution)/shard_map/all_to_all | solution.py:208
  56.0 12.8 %copy-start.4 = (s32[48]{0:T(128)S(1)}, s32[48]{0:T(128)}, u32[]{:S(2)}) copy-start(s32[48]{0:T(128)} %param.11) | copy-start | bytes 580
  56.4 12.6 %collective-permute-start.9 = (f32[4,24,320]{2,1,0:T(8,128)S(1)}, f32[4,24,320]{2,1,0:T(8,128)S(1)}, u32[]{:S(2)}, u32[]{:S(2)}) collective-permute-start(f32[4,24,320]{2,1,0:T(8,128)S(1)} %get-tuple-element.40), channel_id=1, source_target_pairs={{0,3},{1,2},{2,1},{3,0},{4,7},{5,6},{6,5},{7,4},{8,11},{9,10},{10,... | collective-permute-start | bytes 368648 | tf_op jit(solution)/shard_map/ppermute | solution.py:88
  61.4 7.9 %collective-permute-start.8 = (f32[4,24,320]{2,1,0:T(8,128)S(1)}, f32[4,24,320]{2,1,0:T(8,128)S(1)}, u32[]{:S(2)}, u32[]{:S(2)}) collective-permute-start(f32[4,24,320]{2,1,0:T(8,128)S(1)} %get-tuple-element.41), channel_id=1, source_target_pairs={{0,2},{1,3},{2,0},{3,1},{4,6},{5,7},{6,4},{7,5},{8,10},{9,11},{10,... | collective-permute-start | bytes 368648 | tf_op jit(solution)/shard_map/ppermute | solution.py:88
  63.9 6.2 %collective-permute-start.7 = (f32[4,24,320]{2,1,0:T(8,128)S(1)}, f32[4,24,320]{2,1,0:T(8,128)S(1)}, u32[]{:S(2)}, u32[]{:S(2)}) collective-permute-start(f32[4,24,320]{2,1,0:T(8,128)S(1)} %get-tuple-element.39), channel_id=1, source_target_pairs={{0,1},{1,0},{2,3},{3,2},{4,5},{5,4},{6,7},{7,6},{8,9},{9,8},{10,11... | collective-permute-start | bytes 368648 | tf_op jit(solution)/shard_map/ppermute | solution.py:88
  65.8 4.3 %collective-permute-start.10 = (f32[160,432]{1,0:T(8,128)S(1)}, f32[160,432]{1,0:T(8,128)S(1)}, u32[]{:S(2)}, u32[]{:S(2)}) collective-permute-start(f32[160,432]{1,0:T(8,128)S(1)} %slice_select_fusion.1), channel_id=1, source_target_pairs={{0,16},{16,0},{1,17},{17,1},{2,18},{18,2},{3,19},{19,3},{4,20},{20... | collective-permute-start | bytes 829448 | tf_op jit(solution)/shard_map/ppermute | solution.py:31
  77.4 11.7 %collective-permute-start.11 = (f32[56,768]{1,0:T(8,128)S(1)}, f32[56,768]{1,0:T(8,128)S(1)}, u32[]{:S(2)}, u32[]{:S(2)}) collective-permute-start(f32[56,768]{1,0:T(8,128)S(1)} %convert_reduce_fusion), channel_id=1, source_target_pairs={{0,32},{32,0},{1,33},{33,1},{2,34},{34,2},{3,35},{35,3},{4,36},{36... | collective-permute-start | bytes 516104 | tf_op jit(solution)/shard_map/ppermute | solution.py:31
  79.3 21.7 %collective-permute-start.13 = (f32[4,24,320]{2,1,0:T(8,128)S(1)}, f32[4,24,320]{2,1,0:T(8,128)S(1)}, u32[]{:S(2)}, u32[]{:S(2)}) collective-permute-start(f32[4,24,320]{2,1,0:T(8,128)S(1)} %fusion.3), channel_id=1, source_target_pairs={{0,8},{4,12},{8,0},{12,4},{1,9},{5,13},{9,1},{13,5},{2,10},{6,14},... | collective-permute-start | bytes 368648 | tf_op jit(solution)/shard_map/ppermute | solution.py:94
  84.0 17.0 %collective-permute-start.14 = (f32[4,24,320]{2,1,0:T(8,128)S(1)}, f32[4,24,320]{2,1,0:T(8,128)S(1)}, u32[]{:S(2)}, u32[]{:S(2)}) collective-permute-start(f32[4,24,320]{2,1,0:T(8,128)S(1)} %fusion.3), channel_id=1, source_target_pairs={{0,12},{4,8},{8,4},{12,0},{1,13},{5,9},{9,5},{13,1},{2,14},{6,10},... | collective-permute-start | bytes 368648 | tf_op jit(solution)/shard_map/ppermute | solution.py:94
  87.1 13.9 %collective-permute-start.12 = (f32[4,24,320]{2,1,0:T(8,128)S(1)}, f32[4,24,320]{2,1,0:T(8,128)S(1)}, u32[]{:S(2)}, u32[]{:S(2)}) collective-permute-start(f32[4,24,320]{2,1,0:T(8,128)S(1)} %fusion.3), channel_id=1, source_target_pairs={{0,4},{4,0},{8,12},{12,8},{1,5},{5,1},{9,13},{13,9},{2,6},{6,2},{1... | collective-permute-start | bytes 368648 | tf_op jit(solution)/shard_map/ppermute | solution.py:94
  90.0 28.3 %all-to-all-start.2 = ((bf16[8,56,768]{2,1,0:T(8,128)(2,1)}), bf16[8,56,768]{2,1,0:T(8,128)(2,1)S(1)}, u32[]{:S(2)}, u32[]{:S(2)}) async-start(bf16[8,56,768]{2,1,0:T(8,128)(2,1)} %broadcast_in_dim.12), calls=%async_computation.2 | async-start | bytes 1376256 | tf_op jit(solution)/shard_map/all_to_all | solution.py:25
  111.6 5.7 %collective-permute-start.15 = (bf16[16,24,320]{2,1,0:T(8,128)(2,1)S(1)}, bf16[16,24,320]{2,1,0:T(8,128)(2,1)S(1)}, u32[]{:S(2)}, u32[]{:S(2)}) collective-permute-start(bf16[16,24,320]{2,1,0:T(8,128)(2,1)S(1)} %all-gather.half_ref), channel_id=1, source_target_pairs={{0,16},{16,0},{1,17},{17,1},{2,18},{18,2},{3,19},{19,3},{4,20},{20... | collective-permute-start | bytes 737288 | tf_op jit(solution)/shard_map/ppermute | solution.py:31

commit v7 on v6

--- a/solution.py
+++ b/solution.py
@@ -146,7 +146,7 @@
         rows[pl.ds(q, 1), :] = jnp.sum(projected * train_ref[...], axis=0, keepdims=True)
         return carry
 
-    lax.fori_loop(0, NQ, one_query, 0, unroll=2)
+    lax.fori_loop(0, NQ, one_query, 0, unroll=16)
 
     slot = lax.broadcasted_iota(jnp.int32, (NT * TOKX, 128), 0)
     lane = lax.broadcasted_iota(jnp.int32, (NT * TOKX, 128), 1)

time: 159 us -> 157 us (0.987)
  no operation moved by 1% of the time
where the time goes in v7:
time: 157 us; the launch traced here: 156 us
  starting transfers between devices  80.1 us (51%)
  blocking collectives  42.3 us (27%)
  waiting for transfers between devices  19.3 us (12%)
  Pallas kernels  6.72 us (4%)
  local copies, waits for them, and re-layouts  3.83 us (2%)
  other arithmetic  2.25 us (1%)
    all_to_all x2, blocking collectives, spread(): lax.all_to_all(jnp.broadcast_to(x[None], (n,) + x.shape), axes, 0, 0, til...  31.7 us
    ppermute x4, starting transfers between devices, partner(): return lax.ppermute(x, axis, [(i, i ^ bit) for i in range(n)])  22.9 us
    ppermute x6, starting transfers between devices, swap(): return lax.ppermute(x, axis, SWAP)  19.1 us
    all_to_all x2, starting transfers between devices, spread(): lax.all_to_all(jnp.broadcast_to(x[None], (n,) + x.shape), axes, 0, 0, til...  13.9 us
    all_gather x1, blocking collectives, body(): act_half = lax.all_gather(act_piece, 'x', axis=0)  10.6 us
    ppermute x3, starting transfers between devices, summed(): lax.ppermute(x, axis, [(i, i ^ bit) for i in range(4)])  9.64 us
    ppermute x3, starting transfers between devices, scattered(): total = total + lax.ppermute(block, axis, [(i, i ^ bit) for i in range(4)])  9.37 us
    ppermute x3, waiting for transfers between devices, summed(): lax.ppermute(x, axis, [(i, i ^ bit) for i in range(4)])  7.37 us
  transfers between devices with their start and end apart: 19, of which 7 were waited for; matrix products, arithmetic and copies ran while one was open for 3% of the time, Pallas kernels for 1%

profile of v7, /device:TPU:1, one launch (start us, length us, event | category | flops | bytes accessed | tf_op | source)
XLA Modules:
  0.0 156.3 jit_solution(18147963595177974235)
XLA Ops:
  1.8 10.4 %all-to-all-start = ((bf16[16,48,432]{2,1,0:T(8,128)(2,1)}), bf16[16,48,432]{2,1,0:T(8,128)(2,1)S(1)}, u32[]{:S(2)}, u32[]{:S(2)}) async-start(bf16[16,48,432]{2,1,0:T(8,128)(2,1)} %broadcast_in_dim.10), calls=%async_computation | async-start | bytes 1572864 | tf_op jit(solution)/shard_map/all_to_all | solution.py:25
  12.2 7.6 %collective-permute-start.2 = (bf16[1,24,320]{2,1,0:T(8,128)(2,1)S(1)}, bf16[1,24,320]{2,1,0:T(8,128)(2,1)S(1)}, u32[]{:S(2)}, u32[]{:S(2)}) collective-permute-start(bf16[1,24,320]{2,1,0:T(8,128)(2,1)S(1)} %bitcast.35), channel_id=1, source_target_pairs={{0,256},{64,320},{128,384},{192,448},{256,0},{320,64},{384,128},{4... | collective-permute-start | bytes 46088 | tf_op jit(solution)/shard_map/ppermute | solution.py:55
  21.0 4.2 %collective-permute-start.3 = (bf16[2,24,320]{2,1,0:T(8,128)(2,1)S(1)}, bf16[2,24,320]{2,1,0:T(8,128)(2,1)S(1)}, u32[]{:S(2)}, u32[]{:S(2)}) collective-permute-start(bf16[2,24,320]{2,1,0:T(8,128)(2,1)S(1)} %pad_maximum_fusion.3), channel_id=1, source_target_pairs={{0,128},{64,192},{128,0},{192,64},{256,384},{320,448},{384,256},{4... | collective-permute-start | bytes 92168 | tf_op jit(solution)/shard_map/ppermute | solution.py:55
  25.5 4.1 %collective-permute-start = (bf16[432,448]{1,0:T(8,128)(2,1)S(1)}, bf16[432,448]{1,0:T(8,128)(2,1)S(1)}, u32[]{:S(2)}, u32[]{:S(2)}) collective-permute-start(bf16[432,448]{1,0:T(8,128)(2,1)S(1)} %pad.11), channel_id=1, source_target_pairs={{0,16},{16,0},{1,17},{17,1},{2,18},{18,2},{3,19},{19,3},{4,20},{20... | collective-permute-start | bytes 1161224 | tf_op jit(solution)/shard_map/ppermute | solution.py:31
  31.7 3.2 %collective-permute-start.4 = (bf16[4,24,320]{2,1,0:T(8,128)(2,1)S(1)}, bf16[4,24,320]{2,1,0:T(8,128)(2,1)S(1)}, u32[]{:S(2)}, u32[]{:S(2)}) collective-permute-start(bf16[4,24,320]{2,1,0:T(8,128)(2,1)S(1)} %pad_maximum_fusion.2), channel_id=1, source_target_pairs={{0,64},{64,0},{128,192},{192,128},{256,320},{320,256},{384,448},{4... | collective-permute-start | bytes 184328 | tf_op jit(solution)/shard_map/ppermute | solution.py:55
  36.9 3.6 %collective-permute-start.5 = (bf16[16,48,432]{2,1,0:T(8,128)(2,1)S(1)}, bf16[16,48,432]{2,1,0:T(8,128)(2,1)S(1)}, u32[]{:S(2)}, u32[]{:S(2)}) collective-permute-start(bf16[16,48,432]{2,1,0:T(8,128)(2,1)S(1)} %all-to-all-done), channel_id=1, source_target_pairs={{0,16},{16,0},{1,17},{17,1},{2,18},{18,2},{3,19},{19,3},{4,20},{20... | collective-permute-start | bytes 1990664 | tf_op jit(solution)/shard_map/ppermute | solution.py:31
  40.4 7.9 %collective-permute-start.6 = (bf16[8,24,320]{2,1,0:T(8,128)(2,1)S(1)}, bf16[8,24,320]{2,1,0:T(8,128)(2,1)S(1)}, u32[]{:S(2)}, u32[]{:S(2)}) collective-permute-start(bf16[8,24,320]{2,1,0:T(8,128)(2,1)S(1)} %pad_maximum_fusion.1), channel_id=1, source_target_pairs={{0,32},{32,0},{1,33},{33,1},{2,34},{34,2},{3,35},{35,3},{4,36},{36... | collective-permute-start | bytes 368648 | tf_op jit(solution)/shard_map/ppermute | solution.py:55
  50.7 5.1 %all-to-all-start.1 = ((bf16[8,56,768]{2,1,0:T(8,128)(2,1)}), bf16[8,56,768]{2,1,0:T(8,128)(2,1)S(1)}, u32[]{:S(2)}, u32[]{:S(2)}) async-start(bf16[8,56,768]{2,1,0:T(8,128)(2,1)} %bitcast.3), calls=%async_computation.1 | async-start | bytes 1376256 | tf_op jit(solution)/shard_map/all_to_all | solution.py:208
  56.4 5.0 %collective-permute-start.9 = (f32[4,24,320]{2,1,0:T(8,128)S(1)}, f32[4,24,320]{2,1,0:T(8,128)S(1)}, u32[]{:S(2)}, u32[]{:S(2)}) collective-permute-start(f32[4,24,320]{2,1,0:T(8,128)S(1)} %get-tuple-element.40), channel_id=1, source_target_pairs={{0,3},{1,2},{2,1},{3,0},{4,7},{5,6},{6,5},{7,4},{8,11},{9,10},{10,... | collective-permute-start | bytes 368648 | tf_op jit(solution)/shard_map/ppermute | solution.py:88
  61.4 2.5 %collective-permute-start.8 = (f32[4,24,320]{2,1,0:T(8,128)S(1)}, f32[4,24,320]{2,1,0:T(8,128)S(1)}, u32[]{:S(2)}, u32[]{:S(2)}) collective-permute-start(f32[4,24,320]{2,1,0:T(8,128)S(1)} %get-tuple-element.41), channel_id=1, source_target_pairs={{0,2},{1,3},{2,0},{3,1},{4,6},{5,7},{6,4},{7,5},{8,10},{9,11},{10,... | collective-permute-start | bytes 368648 | tf_op jit(solution)/shard_map/ppermute | solution.py:88
  63.9 1.9 %collective-permute-start.7 = (f32[4,24,320]{2,1,0:T(8,128)S(1)}, f32[4,24,320]{2,1,0:T(8,128)S(1)}, u32[]{:S(2)}, u32[]{:S(2)}) collective-permute-start(f32[4,24,320]{2,1,0:T(8,128)S(1)} %get-tuple-element.39), channel_id=1, source_target_pairs={{0,1},{1,0},{2,3},{3,2},{4,5},{5,4},{6,7},{7,6},{8,9},{9,8},{10,11... | collective-permute-start | bytes 368648 | tf_op jit(solution)/shard_map/ppermute | solution.py:88
  65.8 3.0 %collective-permute-start.10 = (f32[160,432]{1,0:T(8,128)S(1)}, f32[160,432]{1,0:T(8,128)S(1)}, u32[]{:S(2)}, u32[]{:S(2)}) collective-permute-start(f32[160,432]{1,0:T(8,128)S(1)} %slice_select_fusion.1), channel_id=1, source_target_pairs={{0,16},{16,0},{1,17},{17,1},{2,18},{18,2},{3,19},{19,3},{4,20},{20... | collective-permute-start | bytes 829448 | tf_op jit(solution)/shard_map/ppermute | solution.py:31
  70.1 7.2 %all-to-all-done.1 = bf16[8,56,768]{2,1,0:T(8,128)(2,1)S(1)} async-done(((bf16[8,56,768]{2,1,0:T(8,128)(2,1)}), bf16[8,56,768]{2,1,0:T(8,128)(2,1)S(1)}, u32[]{:S(2)}, u32[]{:S(2)}) %all-to-all-start.1) | async-done | bytes 688160 | tf_op jit(solution)/shard_map/all_to_all | solution.py:208
  77.4 2.0 %collective-permute-start.11 = (f32[56,768]{1,0:T(8,128)S(1)}, f32[56,768]{1,0:T(8,128)S(1)}, u32[]{:S(2)}, u32[]{:S(2)}) collective-permute-start(f32[56,768]{1,0:T(8,128)S(1)} %convert_reduce_fusion), channel_id=1, source_target_pairs={{0,32},{32,0},{1,33},{33,1},{2,34},{34,2},{3,35},{35,3},{4,36},{36... | collective-permute-start | bytes 516104 | tf_op jit(solution)/shard_map/ppermute | solution.py:31
  79.3 4.6 %collective-permute-start.13 = (f32[4,24,320]{2,1,0:T(8,128)S(1)}, f32[4,24,320]{2,1,0:T(8,128)S(1)}, u32[]{:S(2)}, u32[]{:S(2)}) collective-permute-start(f32[4,24,320]{2,1,0:T(8,128)S(1)} %fusion.3), channel_id=1, source_target_pairs={{0,8},{4,12},{8,0},{12,4},{1,9},{5,13},{9,1},{13,5},{2,10},{6,14},... | collective-permute-start | bytes 368648 | tf_op jit(solution)/shard_map/ppermute | solution.py:94
  84.0 3.1 %collective-permute-start.14 = (f32[4,24,320]{2,1,0:T(8,128)S(1)}, f32[4,24,320]{2,1,0:T(8,128)S(1)}, u32[]{:S(2)}, u32[]{:S(2)}) collective-permute-start(f32[4,24,320]{2,1,0:T(8,128)S(1)} %fusion.3), channel_id=1, source_target_pairs={{0,12},{4,8},{8,4},{12,0},{1,13},{5,9},{9,5},{13,1},{2,14},{6,10},... | collective-permute-start | bytes 368648 | tf_op jit(solution)/shard_map/ppermute | solution.py:94
  87.1 1.9 %collective-permute-start.12 = (f32[4,24,320]{2,1,0:T(8,128)S(1)}, f32[4,24,320]{2,1,0:T(8,128)S(1)}, u32[]{:S(2)}, u32[]{:S(2)}) collective-permute-start(f32[4,24,320]{2,1,0:T(8,128)S(1)} %fusion.3), channel_id=1, source_target_pairs={{0,4},{4,0},{8,12},{12,8},{1,5},{5,1},{9,13},{13,9},{2,6},{6,2},{1... | collective-permute-start | bytes 368648 | tf_op jit(solution)/shard_map/ppermute | solution.py:94
  90.0 3.5 %all-to-all-start.2 = ((bf16[8,56,768]{2,1,0:T(8,128)(2,1)}), bf16[8,56,768]{2,1,0:T(8,128)(2,1)S(1)}, u32[]{:S(2)}, u32[]{:S(2)}) async-start(bf16[8,56,768]{2,1,0:T(8,128)(2,1)} %broadcast_in_dim.12), calls=%async_computation.2 | async-start | bytes 1376256 | tf_op jit(solution)/shard_map/all_to_all | solution.py:25
  93.6 7.4 %collective-permute-done.13 = f32[4,24,320]{2,1,0:T(8,128)S(1)} collective-permute-done((f32[4,24,320]{2,1,0:T(8,128)S(1)}, f32[4,24,320]{2,1,0:T(8,128)S(1)}, u32[]{:S(2)}, u32[]{:S(2)}) %collective-permute-start.13) | collective-permute-done | bytes 122912 | tf_op jit(solution)/shard_map/ppermute | solution.py:94
  101.0 10.6 %all-gather.half_ref = bf16[16,24,320]{2,1,0:T(8,128)(2,1)S(1)} all-gather(bf16[4,24,320]{2,1,0:T(8,128)(2,1)S(1)} %add_convert_fusion.1), channel_id=2, replica_groups=mesh['y'=8,'zh'=2,'core'=2,'zl'=4,'x'=4] {'x'}, dimensions={0}, use_global_device_ids=true | all-gather | bytes 307200 | tf_op jit(solution)/shard_map/all_gather | solution.py:229
  111.6 4.5 %collective-permute-start.15 = (bf16[16,24,320]{2,1,0:T(8,128)(2,1)S(1)}, bf16[16,24,320]{2,1,0:T(8,128)(2,1)S(1)}, u32[]{:S(2)}, u32[]{:S(2)}) collective-permute-start(bf16[16,24,320]{2,1,0:T(8,128)(2,1)S(1)} %all-gather.half_ref), channel_id=1, source_target_pairs={{0,16},{16,0},{1,17},{17,1},{2,18},{18,2},{3,19},{19,3},{4,20},{20... | collective-permute-start | bytes 737288 | tf_op jit(solution)/shard_map/ppermute | solution.py:31
  118.3 5.5 %shard_map.66 = f32[4,128]{1,0:T(4,128)S(1)} custom-call(bf16[448,768]{1,0:T(8,128)(2,1)S(1)} %bitcast.26, bf16[256,320]{1,0:T(8,128)(2,1)S(1)} %get-tuple-element.32.query_ref, f32[320,512]{1,0:T(8,128)S(1)} %get-tuple-element.33.train_ref, f32[320,448]{1,0:T(8,128)S(1)} %pad.13.recip_ref), custom_call_target="tpu_custom_call" | custom-call | flops 2422210560 | bytes 1753088 | tf_op jit(solution)/shard_map/pallas_call | solution.py:167
  123.7 15.5 %all_to_all.25 = f32[32,4,128]{2,1,0:T(4,128)S(1)} all-to-all(f32[32,4,128]{2,1,0:T(4,128)S(1)} %broadcast_in_dim.13), channel_id=1, replica_groups=mesh['y'=8,'zh'=2,'core'=2,'zl'=4,'x'=4] {'core','zl','x'}, dimensions={0} | all-to-all | bytes 131072 | tf_op jit(solution)/shard_map/all_to_all | solution.py:25
  139.3 16.3 %all_to_all.26 = f32[16,4,128]{2,1,0:T(4,128)S(1)} all-to-all(f32[16,4,128]{2,1,0:T(4,128)S(1)} %broadcast_in_dim.14), channel_id=1, replica_groups=mesh['y'=8,'zh'=2,'core'=2,'zl'=4,'x'=4] {'y','zh'}, dimensions={0} | all-to-all | bytes 65536 | tf_op jit(solution)/shard_map/all_to_all | solution.py:25
  (61 shorter events, 15.3 us)
Async XLA Ops:
  0.0 12.2 %copy-start.2 = (bf16[24,320]{1,0:T(8,128)(2,1)S(1)}, bf16[24,320]{1,0:T(8,128)(2,1)}, u32[]{:S(2)}) copy-start(bf16[24,320]{1,0:T(8,128)(2,1)} %param.7) | copy-start | bytes 46084
  0.0 25.2 %copy-start.1 = (bf16[432,864]{1,0:T(8,128)(2,1)S(1)}, bf16[432,864]{1,0:T(8,128)(2,1)}, u32[]{:S(2)}) copy-start(bf16[432,864]{1,0:T(8,128)(2,1)} %param.8) | copy-start | bytes 2239492
  1.8 35.0 %all-to-all-start = ((bf16[16,48,432]{2,1,0:T(8,128)(2,1)}), bf16[16,48,432]{2,1,0:T(8,128)(2,1)S(1)}, u32[]{:S(2)}, u32[]{:S(2)}) async-start(bf16[16,48,432]{2,1,0:T(8,128)(2,1)} %broadcast_in_dim.10), calls=%async_computation | async-start | bytes 1572864 | tf_op jit(solution)/shard_map/all_to_all | solution.py:25
  12.2 17.4 %copy-start.3 = (bf16[320,160]{0,1:T(8,128)(2,1)S(1)}, bf16[320,160]{0,1:T(8,128)(2,1)}, u32[]{:S(2)}) copy-start(bf16[320,160]{0,1:T(8,128)(2,1)} %param.9) | copy-start | bytes 307204
  12.2 8.7 %collective-permute-start.2 = (bf16[1,24,320]{2,1,0:T(8,128)(2,1)S(1)}, bf16[1,24,320]{2,1,0:T(8,128)(2,1)S(1)}, u32[]{:S(2)}, u32[]{:S(2)}) collective-permute-start(bf16[1,24,320]{2,1,0:T(8,128)(2,1)S(1)} %bitcast.35), channel_id=1, source_target_pairs={{0,256},{64,320},{128,384},{192,448},{256,0},{320,64},{384,128},{4... | collective-permute-start | bytes 46088 | tf_op jit(solution)/shard_map/ppermute | solution.py:55
  21.0 10.7 %collective-permute-start.3 = (bf16[2,24,320]{2,1,0:T(8,128)(2,1)S(1)}, bf16[2,24,320]{2,1,0:T(8,128)(2,1)S(1)}, u32[]{:S(2)}, u32[]{:S(2)}) collective-permute-start(bf16[2,24,320]{2,1,0:T(8,128)(2,1)S(1)} %pad_maximum_fusion.3), channel_id=1, source_target_pairs={{0,128},{64,192},{128,0},{192,64},{256,384},{320,448},{384,256},{4... | collective-permute-start | bytes 92168 | tf_op jit(solution)/shard_map/ppermute | solution.py:55
  25.5 11.4 %collective-permute-start = (bf16[432,448]{1,0:T(8,128)(2,1)S(1)}, bf16[432,448]{1,0:T(8,128)(2,1)S(1)}, u32[]{:S(2)}, u32[]{:S(2)}) collective-permute-start(bf16[432,448]{1,0:T(8,128)(2,1)S(1)} %pad.11), channel_id=1, source_target_pairs={{0,16},{16,0},{1,17},{17,1},{2,18},{18,2},{3,19},{19,3},{4,20},{20... | collective-permute-start | bytes 1161224 | tf_op jit(solution)/shard_map/ppermute | solution.py:31
  29.7 5.2 %collective-permute-start.1 = (bf16[320,160]{1,0:T(8,128)(2,1)S(1)}, bf16[320,160]{1,0:T(8,128)(2,1)S(1)}, u32[]{:S(2)}, u32[]{:S(2)}) collective-permute-start(bf16[320,160]{1,0:T(8,128)(2,1)S(1)} %copy.27), channel_id=1, source_target_pairs={{0,16},{16,0},{1,17},{17,1},{2,18},{18,2},{3,19},{19,3},{4,20},{20... | collective-permute-start | bytes 307208 | tf_op jit(solution)/shard_map/ppermute | solution.py:31
  31.7 5.1 %collective-permute-start.4 = (bf16[4,24,320]{2,1,0:T(8,128)(2,1)S(1)}, bf16[4,24,320]{2,1,0:T(8,128)(2,1)S(1)}, u32[]{:S(2)}, u32[]{:S(2)}) collective-permute-start(bf16[4,24,320]{2,1,0:T(8,128)(2,1)S(1)} %pad_maximum_fusion.2), channel_id=1, source_target_pairs={{0,64},{64,0},{128,192},{192,128},{256,320},{320,256},{384,448},{4... | collective-permute-start | bytes 184328 | tf_op jit(solution)/shard_map/ppermute | solution.py:55
  36.9 12.1 %collective-permute-start.5 = (bf16[16,48,432]{2,1,0:T(8,128)(2,1)S(1)}, bf16[16,48,432]{2,1,0:T(8,128)(2,1)S(1)}, u32[]{:S(2)}, u32[]{:S(2)}) collective-permute-start(bf16[16,48,432]{2,1,0:T(8,128)(2,1)S(1)} %all-to-all-done), channel_id=1, source_target_pairs={{0,16},{16,0},{1,17},{17,1},{2,18},{18,2},{3,19},{19,3},{4,20},{20... | collective-permute-start | bytes 1990664 | tf_op jit(solution)/shard_map/ppermute | solution.py:31
  40.4 15.6 %collective-permute-start.6 = (bf16[8,24,320]{2,1,0:T(8,128)(2,1)S(1)}, bf16[8,24,320]{2,1,0:T(8,128)(2,1)S(1)}, u32[]{:S(2)}, u32[]{:S(2)}) collective-permute-start(bf16[8,24,320]{2,1,0:T(8,128)(2,1)S(1)} %pad_maximum_fusion.1), channel_id=1, source_target_pairs={{0,32},{32,0},{1,33},{33,1},{2,34},{34,2},{3,35},{35,3},{4,36},{36... | collective-permute-start | bytes 368648 | tf_op jit(solution)/shard_map/ppermute | solution.py:55
  50.7 5.1 %copy-start = (f32[864,160]{0,1:T(8,128)S(1)}, f32[864,160]{0,1:T(8,128)}, u32[]{:S(2)}) copy-start(f32[864,160]{0,1:T(8,128)} %param.10) | copy-start | bytes 1658884
  50.7 26.6 %all-to-all-start.1 = ((bf16[8,56,768]{2,1,0:T(8,128)(2,1)}), bf16[8,56,768]{2,1,0:T(8,128)(2,1)S(1)}, u32[]{:S(2)}, u32[]{:S(2)}) async-start(bf16[8,56,768]{2,1,0:T(8,128)(2,1)} %bitcast.3), calls=%async_computation.1 | async-start | bytes 1376256 | tf_op jit(solution)/shard_map/all_to_all | solution.py:208
  56.0 12.8 %copy-start.4 = (s32[48]{0:T(128)S(1)}, s32[48]{0:T(128)}, u32[]{:S(2)}) copy-start(s32[48]{0:T(128)} %param.11) | copy-start | bytes 580
  56.4 12.6 %collective-permute-start.9 = (f32[4,24,320]{2,1,0:T(8,128)S(1)}, f32[4,24,320]{2,1,0:T(8,128)S(1)}, u32[]{:S(2)}, u32[]{:S(2)}) collective-permute-start(f32[4,24,320]{2,1,0:T(8,128)S(1)} %get-tuple-element.40), channel_id=1, source_target_pairs={{0,3},{1,2},{2,1},{3,0},{4,7},{5,6},{6,5},{7,4},{8,11},{9,10},{10,... | collective-permute-start | bytes 368648 | tf_op jit(solution)/shard_map/ppermute | solution.py:88
  61.4 7.9 %collective-permute-start.8 = (f32[4,24,320]{2,1,0:T(8,128)S(1)}, f32[4,24,320]{2,1,0:T(8,128)S(1)}, u32[]{:S(2)}, u32[]{:S(2)}) collective-permute-start(f32[4,24,320]{2,1,0:T(8,128)S(1)} %get-tuple-element.41), channel_id=1, source_target_pairs={{0,2},{1,3},{2,0},{3,1},{4,6},{5,7},{6,4},{7,5},{8,10},{9,11},{10,... | collective-permute-start | bytes 368648 | tf_op jit(solution)/shard_map/ppermute | solution.py:88
  63.9 6.2 %collective-permute-start.7 = (f32[4,24,320]{2,1,0:T(8,128)S(1)}, f32[4,24,320]{2,1,0:T(8,128)S(1)}, u32[]{:S(2)}, u32[]{:S(2)}) collective-permute-start(f32[4,24,320]{2,1,0:T(8,128)S(1)} %get-tuple-element.39), channel_id=1, source_target_pairs={{0,1},{1,0},{2,3},{3,2},{4,5},{5,4},{6,7},{7,6},{8,9},{9,8},{10,11... | collective-permute-start | bytes 368648 | tf_op jit(solution)/shard_map/ppermute | solution.py:88
  65.8 4.3 %collective-permute-start.10 = (f32[160,432]{1,0:T(8,128)S(1)}, f32[160,432]{1,0:T(8,128)S(1)}, u32[]{:S(2)}, u32[]{:S(2)}) collective-permute-start(f32[160,432]{1,0:T(8,128)S(1)} %slice_select_fusion.1), channel_id=1, source_target_pairs={{0,16},{16,0},{1,17},{17,1},{2,18},{18,2},{3,19},{19,3},{4,20},{20... | collective-permute-start | bytes 829448 | tf_op jit(solution)/shard_map/ppermute | solution.py:31
  77.4 11.7 %collective-permute-start.11 = (f32[56,768]{1,0:T(8,128)S(1)}, f32[56,768]{1,0:T(8,128)S(1)}, u32[]{:S(2)}, u32[]{:S(2)}) collective-permute-start(f32[56,768]{1,0:T(8,128)S(1)} %convert_reduce_fusion), channel_id=1, source_target_pairs={{0,32},{32,0},{1,33},{33,1},{2,34},{34,2},{3,35},{35,3},{4,36},{36... | collective-permute-start | bytes 516104 | tf_op jit(solution)/shard_map/ppermute | solution.py:31
  79.3 21.7 %collective-permute-start.13 = (f32[4,24,320]{2,1,0:T(8,128)S(1)}, f32[4,24,320]{2,1,0:T(8,128)S(1)}, u32[]{:S(2)}, u32[]{:S(2)}) collective-permute-start(f32[4,24,320]{2,1,0:T(8,128)S(1)} %fusion.3), channel_id=1, source_target_pairs={{0,8},{4,12},{8,0},{12,4},{1,9},{5,13},{9,1},{13,5},{2,10},{6,14},... | collective-permute-start | bytes 368648 | tf_op jit(solution)/shard_map/ppermute | solution.py:94
  84.0 17.0 %collective-permute-start.14 = (f32[4,24,320]{2,1,0:T(8,128)S(1)}, f32[4,24,320]{2,1,0:T(8,128)S(1)}, u32[]{:S(2)}, u32[]{:S(2)}) collective-permute-start(f32[4,24,320]{2,1,0:T(8,128)S(1)} %fusion.3), channel_id=1, source_target_pairs={{0,12},{4,8},{8,4},{12,0},{1,13},{5,9},{9,5},{13,1},{2,14},{6,10},... | collective-permute-start | bytes 368648 | tf_op jit(solution)/shard_map/ppermute | solution.py:94
  87.1 13.9 %collective-permute-start.12 = (f32[4,24,320]{2,1,0:T(8,128)S(1)}, f32[4,24,320]{2,1,0:T(8,128)S(1)}, u32[]{:S(2)}, u32[]{:S(2)}) collective-permute-start(f32[4,24,320]{2,1,0:T(8,128)S(1)} %fusion.3), channel_id=1, source_target_pairs={{0,4},{4,0},{8,12},{12,8},{1,5},{5,1},{9,13},{13,9},{2,6},{6,2},{1... | collective-permute-start | bytes 368648 | tf_op jit(solution)/shard_map/ppermute | solution.py:94
  90.0 28.3 %all-to-all-start.2 = ((bf16[8,56,768]{2,1,0:T(8,128)(2,1)}), bf16[8,56,768]{2,1,0:T(8,128)(2,1)S(1)}, u32[]{:S(2)}, u32[]{:S(2)}) async-start(bf16[8,56,768]{2,1,0:T(8,128)(2,1)} %broadcast_in_dim.12), calls=%async_computation.2 | async-start | bytes 1376256 | tf_op jit(solution)/shard_map/all_to_all | solution.py:25
  111.6 5.7 %collective-permute-start.15 = (bf16[16,24,320]{2,1,0:T(8,128)(2,1)S(1)}, bf16[16,24,320]{2,1,0:T(8,128)(2,1)S(1)}, u32[]{:S(2)}, u32[]{:S(2)}) collective-permute-start(bf16[16,24,320]{2,1,0:T(8,128)(2,1)S(1)} %all-gather.half_ref), channel_id=1, source_target_pairs={{0,16},{16,0},{1,17},{17,1},{2,18},{18,2},{3,19},{19,3},{4,20},{20... | collective-permute-start | bytes 737288 | tf_op jit(solution)/shard_map/ppermute | solution.py:31

commit v8 on v7

--- a/solution.py
+++ b/solution.py
@@ -221,7 +221,7 @@
     pieces, part_act, used, e_other = tie(pieces, part_act, used, e_other)
 
     piece = jnp.sum(pieces.astype(f32), axis=0)
-    piece_other = swap(piece, "zh")
+    piece_other = swap(piece.astype(bf16), "zh").astype(f32)
     act_piece = summed(part_act, "zl").astype(bf16)
     piece = ((piece + piece_other) * used).astype(bf16)
 

time: 157 us -> 156 us (level)
  transfers between devices with their start and end apart: 19 -> 19, of which waited for: 7 -> 8; matrix products, arithmetic and copies ran while one was open for 3% -> 3% of each run, Pallas kernels for 1% -> 1%
where the time goes in v8:
time: 156 us; the launch traced here: 155 us
  starting transfers between devices  80 us (51%)
  blocking collectives  42.6 us (27%)
  waiting for transfers between devices  18 us (12%)
  Pallas kernels  6.7 us (4%)
  local copies, waits for them, and re-layouts  3.83 us (2%)
  other arithmetic  2.26 us (1%)
    all_to_all x2, blocking collectives, spread(): lax.all_to_all(jnp.broadcast_to(x[None], (n,) + x.shape), axes, 0, 0, til...  31.6 us
    ppermute x4, starting transfers between devices, partner(): return lax.ppermute(x, axis, [(i, i ^ bit) for i in range(n)])  22.9 us
    ppermute x6, starting transfers between devices, swap(): return lax.ppermute(x, axis, SWAP)  19 us
    all_to_all x2, starting transfers between devices, spread(): lax.all_to_all(jnp.broadcast_to(x[None], (n,) + x.shape), axes, 0, 0, til...  13.9 us
    all_gather x1, blocking collectives, body(): act_half = lax.all_gather(act_piece, 'x', axis=0)  11 us
    ppermute x3, starting transfers between devices, summed(): lax.ppermute(x, axis, [(i, i ^ bit) for i in range(4)])  9.64 us
    ppermute x3, starting transfers between devices, scattered(): total = total + lax.ppermute(block, axis, [(i, i ^ bit) for i in range(4)])  9.37 us
    all_to_all x1, waiting for transfers between devices, body(): pieces = lax.all_to_all(partial.reshape(8, -1, NTOK), 'y', 0, 0, tiled=True)  7.19 us
  transfers between devices with their start and end apart: 19, of which 8 were waited for; matrix products, arithmetic and copies ran while one was open for 3% of the time, Pallas kernels for 1%

profile of v8, /device:TPU:1, one launch (start us, length us, event | category | flops | bytes accessed | tf_op | source)
XLA Modules:
  0.0 155.1 jit_solution(4928129772127665353)
XLA Ops:
  1.8 10.4 %all-to-all-start = ((bf16[16,48,432]{2,1,0:T(8,128)(2,1)}), bf16[16,48,432]{2,1,0:T(8,128)(2,1)S(1)}, u32[]{:S(2)}, u32[]{:S(2)}) async-start(bf16[16,48,432]{2,1,0:T(8,128)(2,1)} %broadcast_in_dim.10), calls=%async_computation | async-start | bytes 1572864 | tf_op jit(solution)/shard_map/all_to_all | solution.py:25
  12.2 7.6 %collective-permute-start.2 = (bf16[1,24,320]{2,1,0:T(8,128)(2,1)S(1)}, bf16[1,24,320]{2,1,0:T(8,128)(2,1)S(1)}, u32[]{:S(2)}, u32[]{:S(2)}) collective-permute-start(bf16[1,24,320]{2,1,0:T(8,128)(2,1)S(1)} %bitcast.35), channel_id=1, source_target_pairs={{0,256},{64,320},{128,384},{192,448},{256,0},{320,64},{384,128},{4... | collective-permute-start | bytes 46088 | tf_op jit(solution)/shard_map/ppermute | solution.py:55
  21.0 4.2 %collective-permute-start.3 = (bf16[2,24,320]{2,1,0:T(8,128)(2,1)S(1)}, bf16[2,24,320]{2,1,0:T(8,128)(2,1)S(1)}, u32[]{:S(2)}, u32[]{:S(2)}) collective-permute-start(bf16[2,24,320]{2,1,0:T(8,128)(2,1)S(1)} %pad_maximum_fusion.3), channel_id=1, source_target_pairs={{0,128},{64,192},{128,0},{192,64},{256,384},{320,448},{384,256},{4... | collective-permute-start | bytes 92168 | tf_op jit(solution)/shard_map/ppermute | solution.py:55
  25.5 4.1 %collective-permute-start = (bf16[432,448]{1,0:T(8,128)(2,1)S(1)}, bf16[432,448]{1,0:T(8,128)(2,1)S(1)}, u32[]{:S(2)}, u32[]{:S(2)}) collective-permute-start(bf16[432,448]{1,0:T(8,128)(2,1)S(1)} %pad.11), channel_id=1, source_target_pairs={{0,16},{16,0},{1,17},{17,1},{2,18},{18,2},{3,19},{19,3},{4,20},{20... | collective-permute-start | bytes 1161224 | tf_op jit(solution)/shard_map/ppermute | solution.py:31
  31.7 3.2 %collective-permute-start.4 = (bf16[4,24,320]{2,1,0:T(8,128)(2,1)S(1)}, bf16[4,24,320]{2,1,0:T(8,128)(2,1)S(1)}, u32[]{:S(2)}, u32[]{:S(2)}) collective-permute-start(bf16[4,24,320]{2,1,0:T(8,128)(2,1)S(1)} %pad_maximum_fusion.2), channel_id=1, source_target_pairs={{0,64},{64,0},{128,192},{192,128},{256,320},{320,256},{384,448},{4... | collective-permute-start | bytes 184328 | tf_op jit(solution)/shard_map/ppermute | solution.py:55
  36.9 3.6 %collective-permute-start.5 = (bf16[16,48,432]{2,1,0:T(8,128)(2,1)S(1)}, bf16[16,48,432]{2,1,0:T(8,128)(2,1)S(1)}, u32[]{:S(2)}, u32[]{:S(2)}) collective-permute-start(bf16[16,48,432]{2,1,0:T(8,128)(2,1)S(1)} %all-to-all-done), channel_id=1, source_target_pairs={{0,16},{16,0},{1,17},{17,1},{2,18},{18,2},{3,19},{19,3},{4,20},{20... | collective-permute-start | bytes 1990664 | tf_op jit(solution)/shard_map/ppermute | solution.py:31
  40.4 7.9 %collective-permute-start.6 = (bf16[8,24,320]{2,1,0:T(8,128)(2,1)S(1)}, bf16[8,24,320]{2,1,0:T(8,128)(2,1)S(1)}, u32[]{:S(2)}, u32[]{:S(2)}) collective-permute-start(bf16[8,24,320]{2,1,0:T(8,128)(2,1)S(1)} %pad_maximum_fusion.1), channel_id=1, source_target_pairs={{0,32},{32,0},{1,33},{33,1},{2,34},{34,2},{3,35},{35,3},{4,36},{36... | collective-permute-start | bytes 368648 | tf_op jit(solution)/shard_map/ppermute | solution.py:55
  50.7 5.1 %all-to-all-start.1 = ((bf16[8,56,768]{2,1,0:T(8,128)(2,1)}), bf16[8,56,768]{2,1,0:T(8,128)(2,1)S(1)}, u32[]{:S(2)}, u32[]{:S(2)}) async-start(bf16[8,56,768]{2,1,0:T(8,128)(2,1)} %bitcast.3), calls=%async_computation.1 | async-start | bytes 1376256 | tf_op jit(solution)/shard_map/all_to_all | solution.py:208
  56.4 5.0 %collective-permute-start.9 = (f32[4,24,320]{2,1,0:T(8,128)S(1)}, f32[4,24,320]{2,1,0:T(8,128)S(1)}, u32[]{:S(2)}, u32[]{:S(2)}) collective-permute-start(f32[4,24,320]{2,1,0:T(8,128)S(1)} %get-tuple-element.40), channel_id=1, source_target_pairs={{0,3},{1,2},{2,1},{3,0},{4,7},{5,6},{6,5},{7,4},{8,11},{9,10},{10,... | collective-permute-start | bytes 368648 | tf_op jit(solution)/shard_map/ppermute | solution.py:88
  61.4 2.5 %collective-permute-start.8 = (f32[4,24,320]{2,1,0:T(8,128)S(1)}, f32[4,24,320]{2,1,0:T(8,128)S(1)}, u32[]{:S(2)}, u32[]{:S(2)}) collective-permute-start(f32[4,24,320]{2,1,0:T(8,128)S(1)} %get-tuple-element.41), channel_id=1, source_target_pairs={{0,2},{1,3},{2,0},{3,1},{4,6},{5,7},{6,4},{7,5},{8,10},{9,11},{10,... | collective-permute-start | bytes 368648 | tf_op jit(solution)/shard_map/ppermute | solution.py:88
  65.8 3.0 %collective-permute-start.10 = (f32[160,432]{1,0:T(8,128)S(1)}, f32[160,432]{1,0:T(8,128)S(1)}, u32[]{:S(2)}, u32[]{:S(2)}) collective-permute-start(f32[160,432]{1,0:T(8,128)S(1)} %slice_select_fusion.1), channel_id=1, source_target_pairs={{0,16},{16,0},{1,17},{17,1},{2,18},{18,2},{3,19},{19,3},{4,20},{20... | collective-permute-start | bytes 829448 | tf_op jit(solution)/shard_map/ppermute | solution.py:31
  70.1 7.2 %all-to-all-done.1 = bf16[8,56,768]{2,1,0:T(8,128)(2,1)S(1)} async-done(((bf16[8,56,768]{2,1,0:T(8,128)(2,1)}), bf16[8,56,768]{2,1,0:T(8,128)(2,1)S(1)}, u32[]{:S(2)}, u32[]{:S(2)}) %all-to-all-start.1) | async-done | bytes 688160 | tf_op jit(solution)/shard_map/all_to_all | solution.py:208
  77.4 2.0 %collective-permute-start.11 = (bf16[56,768]{1,0:T(8,128)(2,1)S(1)}, bf16[56,768]{1,0:T(8,128)(2,1)S(1)}, u32[]{:S(2)}, u32[]{:S(2)}) collective-permute-start(bf16[56,768]{1,0:T(8,128)(2,1)S(1)} %convert_element_type.40), channel_id=1, source_target_pairs={{0,32},{32,0},{1,33},{33,1},{2,34},{34,2},{3,35},{35,3},{4,36},{36... | collective-permute-start | bytes 258056 | tf_op jit(solution)/shard_map/ppermute | solution.py:31
  79.4 4.6 %collective-permute-start.13 = (f32[4,24,320]{2,1,0:T(8,128)S(1)}, f32[4,24,320]{2,1,0:T(8,128)S(1)}, u32[]{:S(2)}, u32[]{:S(2)}) collective-permute-start(f32[4,24,320]{2,1,0:T(8,128)S(1)} %fusion.3), channel_id=1, source_target_pairs={{0,8},{4,12},{8,0},{12,4},{1,9},{5,13},{9,1},{13,5},{2,10},{6,14},... | collective-permute-start | bytes 368648 | tf_op jit(solution)/shard_map/ppermute | solution.py:94
  84.0 3.1 %collective-permute-start.14 = (f32[4,24,320]{2,1,0:T(8,128)S(1)}, f32[4,24,320]{2,1,0:T(8,128)S(1)}, u32[]{:S(2)}, u32[]{:S(2)}) collective-permute-start(f32[4,24,320]{2,1,0:T(8,128)S(1)} %fusion.3), channel_id=1, source_target_pairs={{0,12},{4,8},{8,4},{12,0},{1,13},{5,9},{9,5},{13,1},{2,14},{6,10},... | collective-permute-start | bytes 368648 | tf_op jit(solution)/shard_map/ppermute | solution.py:94
  87.1 1.9 %collective-permute-start.12 = (f32[4,24,320]{2,1,0:T(8,128)S(1)}, f32[4,24,320]{2,1,0:T(8,128)S(1)}, u32[]{:S(2)}, u32[]{:S(2)}) collective-permute-start(f32[4,24,320]{2,1,0:T(8,128)S(1)} %fusion.3), channel_id=1, source_target_pairs={{0,4},{4,0},{8,12},{12,8},{1,5},{5,1},{9,13},{13,9},{2,6},{6,2},{1... | collective-permute-start | bytes 368648 | tf_op jit(solution)/shard_map/ppermute | solution.py:94
  90.0 3.5 %all-to-all-start.2 = ((bf16[8,56,768]{2,1,0:T(8,128)(2,1)}), bf16[8,56,768]{2,1,0:T(8,128)(2,1)S(1)}, u32[]{:S(2)}, u32[]{:S(2)}) async-start(bf16[8,56,768]{2,1,0:T(8,128)(2,1)} %broadcast_in_dim.12), calls=%async_computation.2 | async-start | bytes 1376256 | tf_op jit(solution)/shard_map/all_to_all | solution.py:25
  93.6 3.6 %collective-permute-done.13 = f32[4,24,320]{2,1,0:T(8,128)S(1)} collective-permute-done((f32[4,24,320]{2,1,0:T(8,128)S(1)}, f32[4,24,320]{2,1,0:T(8,128)S(1)}, u32[]{:S(2)}, u32[]{:S(2)}) %collective-permute-start.13) | collective-permute-done | bytes 122912 | tf_op jit(solution)/shard_map/ppermute | solution.py:94
  97.3 2.4 %collective-permute-done.12 = f32[4,24,320]{2,1,0:T(8,128)S(1)} collective-permute-done((f32[4,24,320]{2,1,0:T(8,128)S(1)}, f32[4,24,320]{2,1,0:T(8,128)S(1)}, u32[]{:S(2)}, u32[]{:S(2)}) %collective-permute-start.12) | collective-permute-done | bytes 122912 | tf_op jit(solution)/shard_map/ppermute | solution.py:94
  99.8 11.0 %all-gather.half_ref = bf16[16,24,320]{2,1,0:T(8,128)(2,1)S(1)} all-gather(bf16[4,24,320]{2,1,0:T(8,128)(2,1)S(1)} %add_convert_fusion.1), channel_id=2, replica_groups=mesh['y'=8,'zh'=2,'core'=2,'zl'=4,'x'=4] {'x'}, dimensions={0}, use_global_device_ids=true | all-gather | bytes 307200 | tf_op jit(solution)/shard_map/all_gather | solution.py:229
  110.7 4.4 %collective-permute-start.15 = (bf16[16,24,320]{2,1,0:T(8,128)(2,1)S(1)}, bf16[16,24,320]{2,1,0:T(8,128)(2,1)S(1)}, u32[]{:S(2)}, u32[]{:S(2)}) collective-permute-start(bf16[16,24,320]{2,1,0:T(8,128)(2,1)S(1)} %all-gather.half_ref), channel_id=1, source_target_pairs={{0,16},{16,0},{1,17},{17,1},{2,18},{18,2},{3,19},{19,3},{4,20},{20... | collective-permute-start | bytes 737288 | tf_op jit(solution)/shard_map/ppermute | solution.py:31
  117.3 5.5 %shard_map.66 = f32[4,128]{1,0:T(4,128)S(1)} custom-call(bf16[448,768]{1,0:T(8,128)(2,1)S(1)} %bitcast.26, bf16[256,320]{1,0:T(8,128)(2,1)S(1)} %get-tuple-element.32.query_ref, f32[320,512]{1,0:T(8,128)S(1)} %get-tuple-element.33.train_ref, f32[320,448]{1,0:T(8,128)S(1)} %pad.13.recip_ref), custom_call_target="tpu_custom_call" | custom-call | flops 2422210560 | bytes 1753088 | tf_op jit(solution)/shard_map/pallas_call | solution.py:167
  122.7 14.0 %all_to_all.25 = f32[32,4,128]{2,1,0:T(4,128)S(1)} all-to-all(f32[32,4,128]{2,1,0:T(4,128)S(1)} %broadcast_in_dim.13), channel_id=1, replica_groups=mesh['y'=8,'zh'=2,'core'=2,'zl'=4,'x'=4] {'core','zl','x'}, dimensions={0} | all-to-all | bytes 131072 | tf_op jit(solution)/shard_map/all_to_all | solution.py:25
  136.8 17.6 %all_to_all.26 = f32[16,4,128]{2,1,0:T(4,128)S(1)} all-to-all(f32[16,4,128]{2,1,0:T(4,128)S(1)} %broadcast_in_dim.14), channel_id=1, replica_groups=mesh['y'=8,'zh'=2,'core'=2,'zl'=4,'x'=4] {'y','zh'}, dimensions={0} | all-to-all | bytes 65536 | tf_op jit(solution)/shard_map/all_to_all | solution.py:25
  (62 shorter events, 17.2 us)
Async XLA Ops:
  0.0 12.2 %copy-start.2 = (bf16[24,320]{1,0:T(8,128)(2,1)S(1)}, bf16[24,320]{1,0:T(8,128)(2,1)}, u32[]{:S(2)}) copy-start(bf16[24,320]{1,0:T(8,128)(2,1)} %param.7) | copy-start | bytes 46084
  0.0 25.2 %copy-start.1 = (bf16[432,864]{1,0:T(8,128)(2,1)S(1)}, bf16[432,864]{1,0:T(8,128)(2,1)}, u32[]{:S(2)}) copy-start(bf16[432,864]{1,0:T(8,128)(2,1)} %param.8) | copy-start | bytes 2239492
  1.8 35.0 %all-to-all-start = ((bf16[16,48,432]{2,1,0:T(8,128)(2,1)}), bf16[16,48,432]{2,1,0:T(8,128)(2,1)S(1)}, u32[]{:S(2)}, u32[]{:S(2)}) async-start(bf16[16,48,432]{2,1,0:T(8,128)(2,1)} %broadcast_in_dim.10), calls=%async_computation | async-start | bytes 1572864 | tf_op jit(solution)/shard_map/all_to_all | solution.py:25
  12.2 17.4 %copy-start.3 = (bf16[320,160]{0,1:T(8,128)(2,1)S(1)}, bf16[320,160]{0,1:T(8,128)(2,1)}, u32[]{:S(2)}) copy-start(bf16[320,160]{0,1:T(8,128)(2,1)} %param.9) | copy-start | bytes 307204
  12.2 8.7 %collective-permute-start.2 = (bf16[1,24,320]{2,1,0:T(8,128)(2,1)S(1)}, bf16[1,24,320]{2,1,0:T(8,128)(2,1)S(1)}, u32[]{:S(2)}, u32[]{:S(2)}) collective-permute-start(bf16[1,24,320]{2,1,0:T(8,128)(2,1)S(1)} %bitcast.35), channel_id=1, source_target_pairs={{0,256},{64,320},{128,384},{192,448},{256,0},{320,64},{384,128},{4... | collective-permute-start | bytes 46088 | tf_op jit(solution)/shard_map/ppermute | solution.py:55
  21.0 10.7 %collective-permute-start.3 = (bf16[2,24,320]{2,1,0:T(8,128)(2,1)S(1)}, bf16[2,24,320]{2,1,0:T(8,128)(2,1)S(1)}, u32[]{:S(2)}, u32[]{:S(2)}) collective-permute-start(bf16[2,24,320]{2,1,0:T(8,128)(2,1)S(1)} %pad_maximum_fusion.3), channel_id=1, source_target_pairs={{0,128},{64,192},{128,0},{192,64},{256,384},{320,448},{384,256},{4... | collective-permute-start | bytes 92168 | tf_op jit(solution)/shard_map/ppermute | solution.py:55
  25.5 11.4 %collective-permute-start = (bf16[432,448]{1,0:T(8,128)(2,1)S(1)}, bf16[432,448]{1,0:T(8,128)(2,1)S(1)}, u32[]{:S(2)}, u32[]{:S(2)}) collective-permute-start(bf16[432,448]{1,0:T(8,128)(2,1)S(1)} %pad.11), channel_id=1, source_target_pairs={{0,16},{16,0},{1,17},{17,1},{2,18},{18,2},{3,19},{19,3},{4,20},{20... | collective-permute-start | bytes 1161224 | tf_op jit(solution)/shard_map/ppermute | solution.py:31
  29.7 5.2 %collective-permute-start.1 = (bf16[320,160]{1,0:T(8,128)(2,1)S(1)}, bf16[320,160]{1,0:T(8,128)(2,1)S(1)}, u32[]{:S(2)}, u32[]{:S(2)}) collective-permute-start(bf16[320,160]{1,0:T(8,128)(2,1)S(1)} %copy.27), channel_id=1, source_target_pairs={{0,16},{16,0},{1,17},{17,1},{2,18},{18,2},{3,19},{19,3},{4,20},{20... | collective-permute-start | bytes 307208 | tf_op jit(solution)/shard_map/ppermute | solution.py:31
  31.7 5.1 %collective-permute-start.4 = (bf16[4,24,320]{2,1,0:T(8,128)(2,1)S(1)}, bf16[4,24,320]{2,1,0:T(8,128)(2,1)S(1)}, u32[]{:S(2)}, u32[]{:S(2)}) collective-permute-start(bf16[4,24,320]{2,1,0:T(8,128)(2,1)S(1)} %pad_maximum_fusion.2), channel_id=1, source_target_pairs={{0,64},{64,0},{128,192},{192,128},{256,320},{320,256},{384,448},{4... | collective-permute-start | bytes 184328 | tf_op jit(solution)/shard_map/ppermute | solution.py:55
  36.9 12.1 %collective-permute-start.5 = (bf16[16,48,432]{2,1,0:T(8,128)(2,1)S(1)}, bf16[16,48,432]{2,1,0:T(8,128)(2,1)S(1)}, u32[]{:S(2)}, u32[]{:S(2)}) collective-permute-start(bf16[16,48,432]{2,1,0:T(8,128)(2,1)S(1)} %all-to-all-done), channel_id=1, source_target_pairs={{0,16},{16,0},{1,17},{17,1},{2,18},{18,2},{3,19},{19,3},{4,20},{20... | collective-permute-start | bytes 1990664 | tf_op jit(solution)/shard_map/ppermute | solution.py:31
  40.4 15.6 %collective-permute-start.6 = (bf16[8,24,320]{2,1,0:T(8,128)(2,1)S(1)}, bf16[8,24,320]{2,1,0:T(8,128)(2,1)S(1)}, u32[]{:S(2)}, u32[]{:S(2)}) collective-permute-start(bf16[8,24,320]{2,1,0:T(8,128)(2,1)S(1)} %pad_maximum_fusion.1), channel_id=1, source_target_pairs={{0,32},{32,0},{1,33},{33,1},{2,34},{34,2},{3,35},{35,3},{4,36},{36... | collective-permute-start | bytes 368648 | tf_op jit(solution)/shard_map/ppermute | solution.py:55
  50.7 5.1 %copy-start = (f32[864,160]{0,1:T(8,128)S(1)}, f32[864,160]{0,1:T(8,128)}, u32[]{:S(2)}) copy-start(f32[864,160]{0,1:T(8,128)} %param.10) | copy-start | bytes 1658884
  50.7 26.6 %all-to-all-start.1 = ((bf16[8,56,768]{2,1,0:T(8,128)(2,1)}), bf16[8,56,768]{2,1,0:T(8,128)(2,1)S(1)}, u32[]{:S(2)}, u32[]{:S(2)}) async-start(bf16[8,56,768]{2,1,0:T(8,128)(2,1)} %bitcast.3), calls=%async_computation.1 | async-start | bytes 1376256 | tf_op jit(solution)/shard_map/all_to_all | solution.py:208
  56.0 12.8 %copy-start.4 = (s32[48]{0:T(128)S(1)}, s32[48]{0:T(128)}, u32[]{:S(2)}) copy-start(s32[48]{0:T(128)} %param.11) | copy-start | bytes 580
  56.4 12.6 %collective-permute-start.9 = (f32[4,24,320]{2,1,0:T(8,128)S(1)}, f32[4,24,320]{2,1,0:T(8,128)S(1)}, u32[]{:S(2)}, u32[]{:S(2)}) collective-permute-start(f32[4,24,320]{2,1,0:T(8,128)S(1)} %get-tuple-element.40), channel_id=1, source_target_pairs={{0,3},{1,2},{2,1},{3,0},{4,7},{5,6},{6,5},{7,4},{8,11},{9,10},{10,... | collective-permute-start | bytes 368648 | tf_op jit(solution)/shard_map/ppermute | solution.py:88
  61.4 7.9 %collective-permute-start.8 = (f32[4,24,320]{2,1,0:T(8,128)S(1)}, f32[4,24,320]{2,1,0:T(8,128)S(1)}, u32[]{:S(2)}, u32[]{:S(2)}) collective-permute-start(f32[4,24,320]{2,1,0:T(8,128)S(1)} %get-tuple-element.41), channel_id=1, source_target_pairs={{0,2},{1,3},{2,0},{3,1},{4,6},{5,7},{6,4},{7,5},{8,10},{9,11},{10,... | collective-permute-start | bytes 368648 | tf_op jit(solution)/shard_map/ppermute | solution.py:88
  63.9 6.2 %collective-permute-start.7 = (f32[4,24,320]{2,1,0:T(8,128)S(1)}, f32[4,24,320]{2,1,0:T(8,128)S(1)}, u32[]{:S(2)}, u32[]{:S(2)}) collective-permute-start(f32[4,24,320]{2,1,0:T(8,128)S(1)} %get-tuple-element.39), channel_id=1, source_target_pairs={{0,1},{1,0},{2,3},{3,2},{4,5},{5,4},{6,7},{7,6},{8,9},{9,8},{10,11... | collective-permute-start | bytes 368648 | tf_op jit(solution)/shard_map/ppermute | solution.py:88
  65.8 4.3 %collective-permute-start.10 = (f32[160,432]{1,0:T(8,128)S(1)}, f32[160,432]{1,0:T(8,128)S(1)}, u32[]{:S(2)}, u32[]{:S(2)}) collective-permute-start(f32[160,432]{1,0:T(8,128)S(1)} %slice_select_fusion.1), channel_id=1, source_target_pairs={{0,16},{16,0},{1,17},{17,1},{2,18},{18,2},{3,19},{19,3},{4,20},{20... | collective-permute-start | bytes 829448 | tf_op jit(solution)/shard_map/ppermute | solution.py:31
  77.4 11.7 %collective-permute-start.11 = (bf16[56,768]{1,0:T(8,128)(2,1)S(1)}, bf16[56,768]{1,0:T(8,128)(2,1)S(1)}, u32[]{:S(2)}, u32[]{:S(2)}) collective-permute-start(bf16[56,768]{1,0:T(8,128)(2,1)S(1)} %convert_element_type.40), channel_id=1, source_target_pairs={{0,32},{32,0},{1,33},{33,1},{2,34},{34,2},{3,35},{35,3},{4,36},{36... | collective-permute-start | bytes 258056 | tf_op jit(solution)/shard_map/ppermute | solution.py:31
  79.4 17.9 %collective-permute-start.13 = (f32[4,24,320]{2,1,0:T(8,128)S(1)}, f32[4,24,320]{2,1,0:T(8,128)S(1)}, u32[]{:S(2)}, u32[]{:S(2)}) collective-permute-start(f32[4,24,320]{2,1,0:T(8,128)S(1)} %fusion.3), channel_id=1, source_target_pairs={{0,8},{4,12},{8,0},{12,4},{1,9},{5,13},{9,1},{13,5},{2,10},{6,14},... | collective-permute-start | bytes 368648 | tf_op jit(solution)/shard_map/ppermute | solution.py:94
  84.0 13.3 %collective-permute-start.14 = (f32[4,24,320]{2,1,0:T(8,128)S(1)}, f32[4,24,320]{2,1,0:T(8,128)S(1)}, u32[]{:S(2)}, u32[]{:S(2)}) collective-permute-start(f32[4,24,320]{2,1,0:T(8,128)S(1)} %fusion.3), channel_id=1, source_target_pairs={{0,12},{4,8},{8,4},{12,0},{1,13},{5,9},{9,5},{13,1},{2,14},{6,10},... | collective-permute-start | bytes 368648 | tf_op jit(solution)/shard_map/ppermute | solution.py:94
  87.1 12.6 %collective-permute-start.12 = (f32[4,24,320]{2,1,0:T(8,128)S(1)}, f32[4,24,320]{2,1,0:T(8,128)S(1)}, u32[]{:S(2)}, u32[]{:S(2)}) collective-permute-start(f32[4,24,320]{2,1,0:T(8,128)S(1)} %fusion.3), channel_id=1, source_target_pairs={{0,4},{4,0},{8,12},{12,8},{1,5},{5,1},{9,13},{13,9},{2,6},{6,2},{1... | collective-permute-start | bytes 368648 | tf_op jit(solution)/shard_map/ppermute | solution.py:94
  90.0 27.2 %all-to-all-start.2 = ((bf16[8,56,768]{2,1,0:T(8,128)(2,1)}), bf16[8,56,768]{2,1,0:T(8,128)(2,1)S(1)}, u32[]{:S(2)}, u32[]{:S(2)}) async-start(bf16[8,56,768]{2,1,0:T(8,128)(2,1)} %broadcast_in_dim.12), calls=%async_computation.2 | async-start | bytes 1376256 | tf_op jit(solution)/shard_map/all_to_all | solution.py:25
  110.7 5.6 %collective-permute-start.15 = (bf16[16,24,320]{2,1,0:T(8,128)(2,1)S(1)}, bf16[16,24,320]{2,1,0:T(8,128)(2,1)S(1)}, u32[]{:S(2)}, u32[]{:S(2)}) collective-permute-start(bf16[16,24,320]{2,1,0:T(8,128)(2,1)S(1)} %all-gather.half_ref), channel_id=1, source_target_pairs={{0,16},{16,0},{1,17},{17,1},{2,18},{18,2},{3,19},{19,3},{4,20},{20... | collective-permute-start | bytes 737288 | tf_op jit(solution)/shard_map/ppermute | solution.py:31
